TPU v7x, 512 devices: a whole 4x4x16 slice. The times are simulated.
512 devices in a mesh: row: 128 (over y, z, core), col: 4 (over x).
Axes of the slice: x: 4, y: 4, z: 16, core: 2. Of those that a mesh axis runs over, the one named last changes fastest.
Arguments:
- row_tables: bfloat16 [2, 1048576, 128], P(None, ('row', 'col')), may hold values from -1.5 to 1.5
- row_accum: float32 [2, 1048576], P(None, ('row', 'col')), may hold values from 1e-06 to 0.0001
- col_table: bfloat16 [524288, 256], P('row', 'col'), may hold values from -1.5 to 1.5
- row_owner: int32 [65536, 16, 1], P(('row', 'col')), may hold values from 0 to 511; in each aligned block of 2048 rows (0 to 2047, 2048 to 4095, ..., all dimensions but the last counted through in order) at most 6 rows name the same one
- row_local: int32 [65536, 16], P(('row', 'col')), may hold values from 0 to 2047
- row_lengths: int32 [65536, 2], P(('row', 'col')), may hold values from 1 to 8
- col_owner: int32 [65536, 8, 1], P(('row', 'col')), may hold values from 0 to 127; in each aligned block of 1024 rows (0 to 1023, 1024 to 2047, ..., all dimensions but the last counted through in order) at most 12 rows name the same one
- col_local: int32 [65536, 8], P(('row', 'col')), may hold values from 0 to 4095
- col_lengths: int32 [65536], P(('row', 'col')), may hold values from 1 to 8
- dense_in: bfloat16 [65536, 512], P(('row', 'col')), may hold values from -24 to 24
- cross_weight: bfloat16 [1024, 1024], P('col'), may hold values from -0.1875 to 0.1875
- cross_bias: float32 [1024], replicated, may hold values from -3 to 3
- head_weight: float32 [1024], replicated, may hold values from -0.1875 to 0.1875
- labels: int32 [65536], P(('row', 'col')), may hold values 0 or 1
Outputs:
- new_tables: bfloat16 [2, 1048576, 128], P(None, ('row', 'col'))
- new_accum: float32 [2, 1048576], P(None, ('row', 'col'))
- weight_grad: float32 [1024, 1024], P('col')
Inputs may be any that keep to these rules, and one draw needn't show every extreme that they name: `row_owner`: within the lookups of one device (2048 aligned rows) no owner is named more than 6 times; some owner is named exactly 6 times. `col_owner`: within the lookups of one device (1024 aligned rows) no owner is named more than 12 times; some owner is named exactly 12 times.
All inputs are finite; a program needn't handle non-finite values. No bound on the sum of `labels` on one device may be relied on, other than what follows from the above.
Results may differ from a plain program's by a relative error of at most 0.0047.
Values may be sent and summed in bfloat16 or wider, within the bound.
No kernel may reach another device: no remote copies, remote signals or barrier semaphores. Data moves between devices by JAX's collectives and lax.ppermute only.
A program may use at most 64 MiB of HBM per device.

v0:
```python
import jax
import jax.numpy as jnp
from jax import lax
from jax.sharding import PartitionSpec as P

D_EMB = 128
F_ROW = 2
L = 8


LEARN_RATE = 0.05


def bucket_ranks(owners, buckets):
    sorted_order = jnp.argsort(owners, stable=True)
    sorted_owners = owners[sorted_order]
    counts = jax.ops.segment_sum(jnp.ones_like(owners), owners, num_segments=buckets)
    starts = jnp.cumsum(counts) - counts
    ranked = jnp.arange(owners.shape[0], dtype=jnp.int32) - starts[sorted_owners]
    return jnp.zeros_like(owners).at[sorted_order].set(ranked)


def per_device(
    row_tables,
    row_accum,
    col_table,
    row_owner,
    row_local,
    row_lengths,
    col_owner,
    col_local,
    col_lengths,
    dense_in,
    cross_weight,
    cross_bias,
    head_weight,
    labels,
):
    row_count = lax.axis_size("row")
    col_count = lax.axis_size("col")
    devices_all = row_count * col_count
    batch_rows, slot_count = row_local.shape
    rows_here = row_tables.shape[1]
    bucket_size = max(2, 3 * batch_rows * slot_count // (2 * devices_all))
    zero_half = jnp.zeros((), jnp.bfloat16)
    slot_index = jnp.arange(slot_count, dtype=jnp.int32)
    feature = slot_index // L
    slot_live = ((slot_index % L)[None, :] < row_lengths[:, feature]).reshape(-1)
    lookup_code = (feature[None, :] * rows_here + row_local).reshape(-1)
    owners = row_owner[:, :, 0].reshape(-1)
    position = owners * bucket_size + bucket_ranks(owners, devices_all)
    requests = (
        jnp.full((devices_all * bucket_size,), -1, jnp.int32)
        .at[position]
        .set(jnp.where(slot_live, lookup_code, -1))
    )
    incoming = lax.all_to_all(
        lax.all_to_all(
            requests.reshape(row_count, col_count, bucket_size),
            "row",
            split_axis=0,
            concat_axis=0,
            tiled=True,
        ),
        "col",
        split_axis=1,
        concat_axis=1,
        tiled=True,
    )
    is_valid = incoming >= 0
    safe_code = jnp.maximum(incoming, 0)
    flat_table = row_tables.reshape(-1, D_EMB)
    found_rows = jnp.where(is_valid[..., None], flat_table[safe_code], zero_half)
    replies = lax.all_to_all(
        lax.all_to_all(found_rows, "row", split_axis=0, concat_axis=0, tiled=True),
        "col",
        split_axis=1,
        concat_axis=1,
        tiled=True,
    )
    slot_rows = replies.reshape(-1, D_EMB)[position].reshape(batch_rows, F_ROW, L, D_EMB)
    row_pooled = (
        jnp.sum(slot_rows.astype(jnp.float32), axis=2)
        .reshape(batch_rows, F_ROW * D_EMB)
        .astype(jnp.bfloat16)
    )
    col_bucket = max(2, 3 * batch_rows * L // (2 * row_count))
    col_live = (jnp.arange(L, dtype=jnp.int32)[None, :] < col_lengths[:, None]).reshape(-1)
    col_owners = col_owner[:, :, 0].reshape(-1)
    col_position = col_owners * col_bucket + bucket_ranks(col_owners, row_count)
    col_requests = (
        jnp.full((row_count * col_bucket,), -1, jnp.int32)
        .at[col_position]
        .set(jnp.where(col_live, col_local.reshape(-1), -1))
    )
    col_requests = col_requests.reshape(1, row_count, col_bucket)
    gathered = lax.all_gather(col_requests, "col", axis=0, tiled=True)
    arrived = lax.all_to_all(gathered, "row", split_axis=1, concat_axis=1, tiled=True)
    col_found = jnp.where((arrived >= 0)[..., None], col_table[jnp.maximum(arrived, 0)], zero_half)
    returned = lax.all_to_all(col_found, "row", split_axis=1, concat_axis=1, tiled=True)
    slice_width = col_table.shape[1]
    returned = returned.reshape(col_count, row_count * col_bucket, slice_width)
    own_slices = lax.all_to_all(returned, "col", split_axis=0, concat_axis=2, tiled=True)[0]
    picked = jnp.where(col_live[:, None], own_slices[col_position].astype(jnp.float32), 0.0)
    col_pooled = jnp.sum(picked.reshape(batch_rows, L, -1), axis=1).astype(jnp.bfloat16)
    cross_in = jnp.concatenate([row_pooled, col_pooled, dense_in], axis=1)
    cross_float = cross_in.astype(jnp.float32)
    whole_weight = lax.all_gather(cross_weight, "col", axis=0, tiled=True)
    product = jnp.dot(cross_in, whole_weight, preferred_element_type=jnp.float32)
    pre_act = product + cross_bias[None, :]
    crossed = cross_float * (pre_act + 1.0)
    logit = jnp.dot(crossed, head_weight, precision=lax.Precision.HIGHEST)
    grad_logit = (jax.nn.sigmoid(logit) - labels.astype(jnp.float32)) / batch_rows
    grad_crossed = grad_logit[:, None] * head_weight[None, :]
    grad_pre = (grad_crossed * cross_float).astype(jnp.bfloat16)
    peer_grad = lax.psum_scatter(
        lax.dot_general(
            cross_in, grad_pre, (((0,), (0,)), ((), ())), preferred_element_type=jnp.float32
        ),
        "col",
        scatter_dimension=0,
        tiled=True,
    )
    weight_grad = lax.psum(peer_grad, "row")
    back_term = lax.dot_general(
        grad_pre, whole_weight, (((1,), (1,)), ((), ())), preferred_element_type=jnp.float32
    )
    grad_in = grad_crossed * (pre_act + 1.0) + back_term
    bag_grad = grad_in[:, : F_ROW * D_EMB].astype(jnp.bfloat16).reshape(batch_rows, F_ROW, 1, D_EMB)
    slot_grad = jnp.where(slot_live.reshape(batch_rows, F_ROW, L, 1), bag_grad, zero_half).reshape(
        -1, D_EMB
    )
    grad_buffer = (
        jnp.zeros((devices_all * bucket_size, D_EMB), jnp.bfloat16).at[position].set(slot_grad)
    )
    arrived_grads = lax.all_to_all(
        lax.all_to_all(
            grad_buffer.reshape(row_count, col_count, bucket_size, D_EMB),
            "row",
            split_axis=0,
            concat_axis=0,
            tiled=True,
        ),
        "col",
        split_axis=1,
        concat_axis=1,
        tiled=True,
    )
    row_grad = jax.ops.segment_sum(
        arrived_grads.reshape(-1, D_EMB).astype(jnp.float32),
        safe_code.reshape(-1),
        num_segments=F_ROW * rows_here,
    )
    row_grad = row_grad.reshape(F_ROW, rows_here, D_EMB)
    new_accum = row_accum + jnp.mean(row_grad * row_grad, axis=2)
    new_tables = (
        row_tables.astype(jnp.float32) - LEARN_RATE * row_grad / jnp.sqrt(new_accum)[:, :, None]
    ).astype(jnp.bfloat16)
    return (new_tables, new_accum, weight_grad)


def solution(mesh):
    return jax.shard_map(
        per_device,
        mesh=mesh,
        in_specs=(
            P(None, ("row", "col"), None),
            P(None, ("row", "col")),
            P("row", "col"),
            P(("row", "col"), None, None),
            P(("row", "col"), None),
            P(("row", "col"), None),
            P(("row", "col"), None, None),
            P(("row", "col"), None),
            P(("row", "col")),
            P(("row", "col"), None),
            P("col", None),
            P(),
            P(),
            P(("row", "col")),
        ),
        out_specs=(P(None, ("row", "col"), None), P(None, ("row", "col")), P("col", None)),
        check_vma=False,
    )
```

profile of v0, /device:TPU:1, one launch (start us, length us, event | category | flops | bytes accessed | tf_op | source)
XLA Modules:
  0.0 767.9 jit_solution(5897282564844058027)
XLA Ops:
  9.9 14.7 %scatter_custom_fusion = s32[512]{0:T(512)S(1)} fusion(s32[2048]{0:T(1024)S(1)} %reshape_squeeze.6, s32[2048]{0:T(1024)S(1)} %broadcast.248, s32[]{:T(128)} %constant.33.clone.1), kind=kCustom, calls=%fused_computation.94 | custom fusion | flops 2048 | bytes 2052 | tf_op jit(solution)/shard_map/scatter-add | solution.py:17
  25.2 5.0 sort.34
  30.3 11.8 %gather_fusion = s32[2048]{0:T(1024)S(1)} fusion(s32[2048]{0:T(1024)S(1)} %reshape_squeeze.6, s32[2048]{0:T(1024)S(1)} %get-tuple-element.15), kind=kCustom, calls=%fused_computation | custom fusion | bytes 24576 | tf_op jit(solution)/shard_map/gather | solution.py:16
  42.1 13.2 %gather_fusion.1 = s32[2048]{0:T(1024)S(1)} fusion(s32[512]{0:T(512)S(1)} %bitcast_subtract_fusion, s32[2048]{0:T(1024)S(1)} %broadcast_clamp_fusion.3), kind=kCustom, calls=%fused_computation.1 | custom fusion | bytes 24576 | tf_op jit(solution)/shard_map/gather | solution.py:19
  55.3 8.0 %scatter_custom_fusion.1 = s32[2048]{0:T(1024)S(1)} fusion(s32[2048]{0:T(1024)S(1)} %get-tuple-element.16, s32[2048]{0:T(1024)S(1)} %iota_subtract_fusion, s32[]{:T(128)} %constant.33.clone.1), kind=kCustom, calls=%fused_computation.76 | custom fusion | bytes 8196 | tf_op jit(solution)/shard_map/scatter | solution.py:20
  63.4 8.1 %scatter_custom_fusion.2 = s32[3072]{0:T(1024)S(1)} fusion(s32[2048]{0:T(1024)S(1)} %get-tuple-element.10, s32[2048]{0:T(1024)S(1)} %get-tuple-element.19, s32[]{:T(128)} %constant.31.clone.1), kind=kCustom, calls=%fused_computation.65 | custom fusion | bytes 12292 | tf_op jit(solution)/shard_map/scatter | solution.py:55
  72.5 20.6 %all-to-all-start = ((s32[128,4,6]{2,1,0:T(4,128)}), s32[128,4,6]{2,1,0:T(4,128)S(1)}, u32[]{:S(2)}, u32[]{:S(2)}) async-start(s32[128,4,6]{2,1,0:T(4,128)} %reshape.235), calls=%async_computation | async-start | bytes 524288 | tf_op jit(solution)/shard_map/all_to_all | solution.py:58
  93.2 7.6 scatter_custom_fusion.3
  100.9 4.4 sort.35
  105.2 4.5 gather_fusion.5
  110.2 6.6 gather_fusion.6
  116.8 4.8 scatter_custom_fusion.4
  121.9 4.3 scatter_custom_fusion.5
  127.1 4.0 all-to-all-start.1
  131.1 9.6 %all_gather.6 = s32[4,128,12]{1,2,0:T(8,128)S(1)} all-gather(s32[1,128,12]{1,2,0:T(8,128)S(1)} %copy.69), channel_id=1, replica_groups=mesh['row'=128,'col'=4] {'col'}, dimensions={0}, use_global_device_ids=true | all-gather | bytes 30720 | tf_op jit(solution)/shard_map/all_gather | solution.py:97
  141.6 19.6 %all-to-all-start.4 = ((s32[4,128,12]{2,0,1:T(4,128)}), s32[4,128,12]{2,0,1:T(4,128)S(1)}, u32[]{:S(2)}, u32[]{:S(2)}) async-start(s32[4,128,12]{2,0,1:T(4,128)} %copy.70), calls=%async_computation.4 | async-start | bytes 524288 | tf_op jit(solution)/shard_map/all_to_all | solution.py:98
  161.9 9.2 %gather_fusion.3 = bf16[3072,128]{1,0:T(8,128)(2,1)S(1)} fusion(bf16[4096,128]{1,0:T(8,128)(2,1)S(1)} %bitcast.61, s32[3072]{0:T(1024)S(1)} %broadcast_clamp_fusion.1), kind=kCustom, calls=%fused_computation.3 | custom fusion | bytes 1585152 | tf_op jit(solution)/shard_map/gather | solution.py:73
  173.4 10.4 %all-to-all-done.4 = s32[4,128,12]{2,0,1:T(4,128)S(1)} async-done(((s32[4,128,12]{2,0,1:T(4,128)}), s32[4,128,12]{2,0,1:T(4,128)S(1)}, u32[]{:S(2)}, u32[]{:S(2)}) %all-to-all-start.4) | async-done | bytes 24608 | tf_op jit(solution)/shard_map/all_to_all | solution.py:98
  183.7 8.3 %all-to-all-start.2 = ((bf16[128,4,6,128]{3,1,2,0:T(4,128)(2,1)}), bf16[128,4,6,128]{3,1,2,0:T(4,128)(2,1)}, u32[]{:S(2)}, u32[]{:S(2)}) async-start(bf16[128,4,6,128]{3,1,2,0:T(4,128)(2,1)} %copy.62), calls=%async_computation.2 | async-start | bytes 1572864 | tf_op jit(solution)/shard_map/all_to_all | solution.py:75
  193.2 22.1 %gather_fusion.7 = bf16[6144,64]{1,0:T(8,128)(2,1)} fusion(bf16[4096,64]{1,0:T(8,128)(2,1)S(1)} %copy.75, s32[6144]{0:T(1024)S(1)} %broadcast_clamp_fusion), kind=kCustom, calls=%fused_computation.7 | custom fusion | bytes 1597440 | tf_op jit(solution)/shard_map/gather | solution.py:99
  223.6 11.7 %all-to-all-done.2 = bf16[128,4,6,128]{3,1,2,0:T(4,128)(2,1)} async-done(((bf16[128,4,6,128]{3,1,2,0:T(4,128)(2,1)}), bf16[128,4,6,128]{3,1,2,0:T(4,128)(2,1)}, u32[]{:S(2)}, u32[]{:S(2)}) %all-to-all-start.2) | async-done | bytes 786464 | tf_op jit(solution)/shard_map/all_to_all | solution.py:75
  235.3 8.1 %all-to-all-start.5 = ((bf16[128,2,1536]{2,1,0:T(2,128)(2,1)}), bf16[128,2,1536]{2,1,0:T(2,128)(2,1)S(1)}, u32[]{:S(2)}, u32[]{:S(2)}) async-start(bf16[128,2,1536]{2,1,0:T(2,128)(2,1)} %reshape.417), calls=%async_computation.5 | async-start | bytes 1572864 | tf_op jit(solution)/shard_map/all_to_all | solution.py:100
  246.3 40.6 %all-to-all-done.5 = bf16[128,2,1536]{2,1,0:T(2,128)(2,1)S(1)} async-done(((bf16[128,2,1536]{2,1,0:T(2,128)(2,1)}), bf16[128,2,1536]{2,1,0:T(2,128)(2,1)S(1)}, u32[]{:S(2)}, u32[]{:S(2)}) %all-to-all-start.5) | async-done | bytes 786464 | tf_op jit(solution)/shard_map/all_to_all | solution.py:100
  296.8 4.5 all-to-all-done.3
  301.3 4.2 all-to-all-start.6
  307.7 6.2 gather_fusion.4
  315.8 3.9 gather_fusion.8
  331.6 6.1 scatter_custom_fusion.6
  338.3 56.3 %all_to_all.55 = bf16[128,4,6,128]{3,1,2,0:T(4,128)(2,1)S(1)} all-to-all(bf16[128,4,6,128]{3,1,2,0:T(4,128)(2,1)S(1)} %copy.79), channel_id=1, replica_groups=mesh['row'=128,'col'=4] {'row'}, dimensions={0} | all-to-all | bytes 1572864 | tf_op jit(solution)/shard_map/all_to_all | solution.py:137
  394.8 13.0 %all_to_all.56 = bf16[128,4,6,128]{3,0,2,1:T(8,128)(2,1)S(1)} all-to-all(bf16[128,4,6,128]{3,0,2,1:T(8,128)(2,1)S(1)} %copy.80), channel_id=1, replica_groups=mesh['row'=128,'col'=4] {'col'}, dimensions={1} | all-to-all | bytes 1572864 | tf_op jit(solution)/shard_map/all_to_all | solution.py:136
  409.5 18.8 %scatter_custom_fusion.7 = f32[4096,128]{1,0:T(8,128)} fusion(s32[3072]{0:T(1024)} %copy-done.9, f32[3072,128]{1,0:T(8,128)} %reshape.377, f32[]{:T(128)} %constant.30.clone.1), kind=kCustom, calls=%fused_computation.32 | custom fusion | flops 393216 | bytes 2097664 | tf_op jit(solution)/shard_map/scatter-add | solution.py:149
  432.7 326.1 %all-reduce.2.cloned.1.call-done = f32[256,1024]{1,0:T(8,128)} async-done(((f32[256,1024]{1,0:T(8,128)}), f32[256,1024]{1,0:T(8,128)}) %all-reduce.2.cloned.1.call-update) | async-done | bytes 1048592 | tf_op jit(solution)/shard_map/psum | solution.py:124
  (150 shorter events, 57.1 us)
Async XLA Ops:
  7.2 1.0 copy-start
  42.1 51.0 %copy-start.14 = (s32[128,8,1]{0,2,1:T(1,128)S(1)}, s32[128,8,1]{0,2,1:T(1,128)}, u32[]{:S(2)}) copy-start(s32[128,8,1]{0,2,1:T(1,128)} %param.20) | copy-start | bytes 12292
  63.4 46.4 %copy-start.12 = (s32[2048]{0:T(1024)}, s32[2048]{0:T(1024)S(1)}, u32[]{:S(2)}) copy-start(s32[2048]{0:T(1024)S(1)} %get-tuple-element.10) | copy-start | bytes 24580
  72.5 53.9 %all-to-all-start = ((s32[128,4,6]{2,1,0:T(4,128)}), s32[128,4,6]{2,1,0:T(4,128)S(1)}, u32[]{:S(2)}, u32[]{:S(2)}) async-start(s32[128,4,6]{2,1,0:T(4,128)} %reshape.235), calls=%async_computation | async-start | bytes 524288 | tf_op jit(solution)/shard_map/all_to_all | solution.py:58
  110.2 11.4 %copy-start.15 = (s32[128,8]{0,1:T(8,128)S(1)}, s32[128,8]{0,1:T(8,128)}, u32[]{:S(2)}) copy-start(s32[128,8]{0,1:T(8,128)} %param.21) | copy-start | bytes 12292
  110.2 11.4 %copy-start.17 = (s32[128]{0:T(128)S(1)}, s32[128]{0:T(128)}, u32[]{:S(2)}) copy-start(s32[128]{0:T(128)} %param.22) | copy-start | bytes 1540
  116.8 45.1 %copy-start.1 = (bf16[2,2048,128]{2,1,0:T(8,128)(2,1)S(1)}, bf16[2,2048,128]{2,1,0:T(8,128)(2,1)}, u32[]{:S(2)}) copy-start(bf16[2,2048,128]{2,1,0:T(8,128)(2,1)} %param.14) | copy-start | bytes 3145732
  127.1 14.4 %all-to-all-start.1 = ((s32[128,4,6]{0,2,1:T(8,128)}), s32[128,4,6]{0,2,1:T(8,128)S(1)}, u32[]{:S(2)}, u32[]{:S(2)}) async-start(s32[128,4,6]{0,2,1:T(8,128)} %copy.59), calls=%async_computation.1 | async-start | bytes 32768 | tf_op jit(solution)/shard_map/all_to_all | solution.py:57
  141.6 42.1 %all-to-all-start.4 = ((s32[4,128,12]{2,0,1:T(4,128)}), s32[4,128,12]{2,0,1:T(4,128)S(1)}, u32[]{:S(2)}, u32[]{:S(2)}) async-start(s32[4,128,12]{2,0,1:T(4,128)} %copy.70), calls=%async_computation.4 | async-start | bytes 524288 | tf_op jit(solution)/shard_map/all_to_all | solution.py:98
  161.9 9.2 %copy-start.9 = (s32[3072]{0:T(1024)}, s32[3072]{0:T(1024)S(1)}, u32[]{:S(2)}) copy-start(s32[3072]{0:T(1024)S(1)} %reshape.375) | copy-start | bytes 36868
  172.2 19.9 %copy-start.7 = (bf16[4096,64]{0,1:T(8,128)(2,1)S(1)}, bf16[4096,64]{0,1:T(8,128)(2,1)}, u32[]{:S(2)}) copy-start(bf16[4096,64]{0,1:T(8,128)(2,1)} %param.16) | copy-start | bytes 1572868
  183.7 51.6 %all-to-all-start.2 = ((bf16[128,4,6,128]{3,1,2,0:T(4,128)(2,1)}), bf16[128,4,6,128]{3,1,2,0:T(4,128)(2,1)}, u32[]{:S(2)}, u32[]{:S(2)}) async-start(bf16[128,4,6,128]{3,1,2,0:T(4,128)(2,1)} %copy.62), calls=%async_computation.2 | async-start | bytes 1572864 | tf_op jit(solution)/shard_map/all_to_all | solution.py:75
  235.3 51.6 %all-to-all-start.5 = ((bf16[128,2,1536]{2,1,0:T(2,128)(2,1)}), bf16[128,2,1536]{2,1,0:T(2,128)(2,1)S(1)}, u32[]{:S(2)}, u32[]{:S(2)}) async-start(bf16[128,2,1536]{2,1,0:T(2,128)(2,1)} %reshape.417), calls=%async_computation.5 | async-start | bytes 1572864 | tf_op jit(solution)/shard_map/all_to_all | solution.py:100
  243.4 76.9 %all-gather.2.cloned.1.call-start = ((), (), s32[]{:S(2)}) async-start(), calls=%async_computation.10 | async-start | bytes 2621440 | tf_op jit(solution)/shard_map/all_gather | solution.py:108
  286.9 0.9 copy-start.5
  287.8 13.5 %all-to-all-start.3 = ((bf16[128,4,6,128]{3,0,2,1:T(8,128)(2,1)}), bf16[128,4,6,128]{3,0,2,1:T(8,128)(2,1)S(1)}, u32[]{:S(2)}, u32[]{:S(2)}) async-start(bf16[128,4,6,128]{3,0,2,1:T(8,128)(2,1)} %copy.63), calls=%async_computation.3 | async-start | bytes 1572864 | tf_op jit(solution)/shard_map/all_to_all | solution.py:74
  301.3 4.3 copy-start.4
  301.3 13.1 %all-to-all-start.6 = ((bf16[4,1536,64]{1,2,0:T(8,128)(2,1)}), bf16[4,1536,64]{1,2,0:T(8,128)(2,1)}, u32[]{:S(2)}, u32[]{:S(2)}) async-start(bf16[4,1536,64]{1,2,0:T(8,128)(2,1)} %copy.77), calls=%async_computation.6 | async-start | bytes 1572864 | tf_op jit(solution)/shard_map/all_to_all | solution.py:103
  305.5 125.7 %reduce-scatter.2.cloned.1.call-start = ((), (), s32[]{:S(2)}) async-start(), calls=%async_computation.11 | async-start | bytes 5242880 | tf_op jit(solution)/shard_map/reduce_scatter | solution.py:116
  315.8 4.5 copy-start.3
  315.8 4.5 copy-start.13
  319.8 3.4 copy-start.8
  319.8 3.4 copy-start.16
  322.4 0.8 copy-start.6
  323.7 2.8 copy-start.11
  326.4 2.4 copy-start.2
  326.5 432.4 %all-reduce.2.cloned.1.call-start = ((), (), s32[]{:S(2)}) async-start(), calls=%async_computation.12 | async-start | bytes 2097152 | tf_op jit(solution)/shard_map/psum | solution.py:124
  428.3 2.3 copy-start.10
Sparse Core Ops, SparseCore 0:
  246.3 38.7 all-gather.1
  326.6 50.4 reduce-scatter.1
  431.4 327.4 all-reduce.1
where the time goes:
time: 777 us; the launch traced here: 768 us
  waiting for transfers between devices  394 us (51%)
  local copies, waits for them, and re-layouts  142 us (18%)
  blocking collectives  78.9 us (10%)
  starting transfers between devices  68.4 us (9%)
  other arithmetic  62.7 us (8%)
  between operations  14.8 us (2%)
    psum x1, waiting for transfers between devices, per_device(): weight_grad = lax.psum(peer_grad, 'row')  326 us
    all_to_all x1, blocking collectives, per_device(): lax.all_to_all(grad_buffer.reshape(row_count, col_count, bucket_size, D_E...  56.3 us
    all_to_all x1, waiting for transfers between devices, per_device(): lax.all_to_all(col_found, 'row', split_axis=1, concat_axis=1, tiled=True)  40.6 us
    gather x2, local copies, waits for them, and re-layouts, per_device(): col_table[jnp.maximum(arrived, 0)]  24.7 us
    scatter-add x2, other arithmetic, bucket_ranks(): jax.ops.segment_sum(jnp.ones_like(owners), owners, num_segments=buckets)  22.3 us
    all_to_all x1, starting transfers between devices, per_device(): lax.all_to_all(requests.reshape(row_count, col_count, bucket_size), 'row'...  20.6 us
    gather x2, local copies, waits for them, and re-layouts, bucket_ranks(): starts[sorted_owners]  19.8 us
    all_to_all x1, starting transfers between devices, per_device(): lax.all_to_all(gathered, 'row', split_axis=1, concat_axis=1, tiled=True)  19.6 us
  transfers between devices with their start and end apart: 10, of which 6 were waited for; matrix products, arithmetic and copies ran while one was open for 18% of the time, Pallas kernels for 0%

commit v1 on v0

v1 whole, which is shorter than its diff:
```python
import jax
import jax.numpy as jnp
from jax import lax
from jax.experimental import pallas as pl
from jax.experimental.pallas import tpu as pltpu
from jax.sharding import Mesh, PartitionSpec as P

ROW = ("y", "z", "core")
COL = "x"
ALL = ROW + (COL,)
Y, Z, CORES, PEERS = 4, 16, 2, 4
N_ROW = Y * Z * CORES
OWNERS = N_ROW * PEERS
B = 128
L = 8
D = 128
CAP = 6
CAPC = 12
SLICE = 64
X = 1024
POOL = 256
LEARN_RATE = 0.05
LANES = 128
SHARE = 2 * POOL + LANES
BLOCK = LANES // PEERS
KEEP = 24
FOLD = 8
GROUP = 16
PART_ROWS, PART_COLS = 8, X // 4
VMEM = 40 * 1024 * 1024
MOST_VMEM = 60 * 1024 * 1024

F32 = jnp.float32
BF16 = jnp.bfloat16
I32 = jnp.int32


def iota(shape, axis):
    return lax.broadcasted_iota(I32, shape, axis)


def dot(a, b, dims=((1,), (0,))):
    return lax.dot_general(a, b, (dims, ((), ())), preferred_element_type=F32)


NT = ((1,), (1,))


def half_iota(shape, axis, offset=0):
    return (iota(shape, axis) - offset).astype(F32).astype(BF16)


def to_half(numbers):
    return numbers.astype(F32).astype(BF16)


def ones_where(mask):
    return jnp.where(mask, jnp.ones((), BF16), jnp.zeros((), BF16))


def call(kernel, out_shape, scratch=(), flops=0, bytes_accessed=0):
    return pl.pallas_call(
        kernel,
        out_shape=out_shape,
        scratch_shapes=list(scratch),
        compiler_params=pltpu.CompilerParams(vmem_limit_bytes=VMEM),
        cost_estimate=pl.CostEstimate(
            flops=flops, bytes_accessed=bytes_accessed, transcendentals=0
        ),
    )


def ranks(onehot, mask, carry, ahead):
    counted = dot(onehot, ahead)
    before = jnp.where(mask, counted[:, :LANES] + carry, 0.0)
    return jnp.sum(before, axis=0, keepdims=True).astype(I32), carry + counted[:, LANES:]


def index_kernel(
    owner_in, local_in, length_in, cowner_in, clocal_in, clength_in,
    request_ref, bag_ref,
    owner_ref, local_ref, length_ref, cowner_ref, clocal_ref, clength_ref,
    own_s, high_s, low_s, bag_s, sems,
):
    moves = (
        (owner_in, owner_ref), (local_in, local_ref), (length_in, length_ref),
        (cowner_in, cowner_ref), (clocal_in, clocal_ref), (clength_in, clength_ref),
    )
    copies = [pltpu.make_async_copy(a, b, sems.at[i]) for i, (a, b) in enumerate(moves)]
    for copy in copies:
        copy.start()
    for copy in copies:
        copy.wait()
    ahead = jnp.concatenate(
        [
            (iota((LANES, LANES), 0) < iota((LANES, LANES), 1)).astype(F32),
            jnp.ones((LANES, LANES), F32),
        ],
        axis=1,
    ).astype(BF16)
    sample = iota((1, B), 1)
    rows128 = iota((LANES, LANES), 0)

    def put(step, row, spot, code, bag):
        at = slice(step * LANES, (step + 1) * LANES)
        own_s[:, at] = (rows128 == row).astype(F32).astype(BF16)
        high_s[:, at] = jnp.where(spot, code >> 6, 0).astype(F32).astype(BF16)
        low_s[:, at] = jnp.where(spot, code & 63, 0).astype(F32).astype(BF16)
        bag_s[:, at] = jnp.where(spot, bag, 0).astype(F32).astype(BF16)

    carry = jnp.zeros((OWNERS, LANES), F32)
    rows512 = iota((OWNERS, LANES), 0)
    for slot in range(2 * L):
        table = slot // L
        live = slot % L < length_ref[table : table + 1, :]
        owner = jnp.where(live, owner_ref[slot : slot + 1, :], -1)
        mask = rows512 == owner
        rank, carry = ranks(mask.astype(F32).astype(BF16), mask, carry, ahead)
        place = jnp.where(live, (owner & (PEERS - 1)) * BLOCK + rank, -1)
        code = local_ref[slot : slot + 1, :] + (table * 2048 + 1)
        put(slot, owner >> 2, rows128 == place, code, sample + (table * B + 1))
    carry = jnp.zeros((N_ROW, LANES), F32)
    for slot in range(L):
        live = slot < clength_ref[...]
        owner = jnp.where(live, cowner_ref[slot : slot + 1, :], -1)
        mask = rows128 == owner
        rank, carry = ranks(mask.astype(F32).astype(BF16), mask, carry, ahead)
        place = jnp.where(live, rank + CAP, -1)
        spot = (rows128 & (BLOCK - 1)) == place
        put(2 * L + slot, owner, spot, clocal_ref[slot : slot + 1, :] + 1, sample + 1)
    own = own_s[...]
    high = dot(own, high_s[...], NT)
    low = dot(own, low_s[...], NT)
    request_ref[...] = (high * 64.0 + low).astype(I32)
    bag_ref[...] = dot(bag_s[...], own, NT).astype(I32)


def columns(codes, first):
    return jnp.concatenate([codes[:, r : r + 1] for r in range(first, first + GROUP)], axis=0)


def fold_cols_kernel(after_ref, col_ref, out_ref):
    groups = out_ref.shape[0]
    for pair in range(FOLD // 2):
        both = jnp.concatenate(
            [col_ref[:, (2 * pair + i) * groups : (2 * pair + i + 1) * groups] for i in range(2)],
            axis=0,
        )
        out_ref[:, pair * D : (pair + 1) * D] = both.T


def fold_rows_kernel(after_ref, row_ref, out_ref):
    groups = out_ref.shape[0]
    for h in range(FOLD):
        out_ref[:, h * D : (h + 1) * D] = row_ref[h * groups : (h + 1) * groups, :]


def lookup_kernel(code_ref, fold_ref, cfold_ref, out_ref):
    groups = fold_ref.shape[0]
    picks = [
        jnp.concatenate([code_ref[c, i * CAP : (i + 1) * CAP, :] for c in range(PEERS)], axis=0) - 1
        for i in range(3)
    ]
    inner = [(pick & (groups - 1)) - groups // 2 for pick in picks]
    outer = [pick // groups for pick in picks]
    wide = PEERS * CAP
    size = GROUP * wide
    lane = half_iota((size, groups), 1, groups // 2)
    left = iota((size, D), 1) < SLICE
    for first in range(0, N_ROW, GROUP):

        def found(i, table_ref):
            return dot(ones_where(to_half(columns(inner[i], first)) == lane), table_ref[...])

        full = found(0, fold_ref)
        part = jnp.broadcast_to(columns(outer[0], first), (size, D))
        rows = jnp.zeros((size, D), F32)
        for h in range(FOLD):
            rows = jnp.where(part == h, full[:, h * D : (h + 1) * D], rows)
        halves = []
        for i in range(2):
            full = found(1 + i, cfold_ref)
            part = jnp.broadcast_to(columns(outer[1 + i], first), (size, D))
            pair_of = part >> 1
            got = jnp.zeros((size, D), F32)
            for pair in range(FOLD // 2):
                got = jnp.where(pair_of == pair, full[:, pair * D : (pair + 1) * D], got)
            turned = pltpu.roll(got, SLICE, 1)
            halves.append(jnp.where((part & 1) == i, got, turned))
        cols = jnp.where(left, halves[0], halves[1])
        parts = []
        for r in range(GROUP * PEERS):
            parts.append(rows[r * CAP : (r + 1) * CAP])
            parts.append(cols[r * CAP : (r + 1) * CAP])
        out_ref[first * 2 * wide : (first + GROUP) * 2 * wide, :] = jnp.concatenate(
            parts, axis=0
        ).astype(BF16)


def dense_kernel(
    bag_ref, reply_ref, dense_ref, weight_in, bias_ref, head_ref, label_ref,
    grads_ref, share_ref, weight_ref, sem,
):
    fetch = pltpu.make_async_copy(weight_in, weight_ref, sem)
    fetch.start()
    span = CAP * N_ROW

    def lanes_of(first):
        return jnp.concatenate([bag_ref[first + k : first + k + 1, :] for k in range(CAP)], axis=1)

    pooled = jnp.zeros((2 * B, D), F32)
    for c in range(PEERS):
        picks = iota((2 * B, span), 0) + 1 == lanes_of(c * BLOCK)
        pooled += dot(picks.astype(F32).astype(BF16), reply_ref[c, 0])
    halves = [
        (iota((B, span), 0) + 1 == lanes_of((i + 1) * CAP)).astype(F32).astype(BF16)
        for i in range(2)
    ]
    wide_cols = []
    for c in range(PEERS):
        first = dot(halves[0], reply_ref[c, 1])
        second = dot(halves[1], reply_ref[c, 1])
        wide_cols.append(first[:, :SLICE] + second[:, SLICE:])
    cross_in = jnp.concatenate(
        [pooled[:B].astype(BF16), pooled[B:].astype(BF16)]
        + [
            jnp.concatenate(wide_cols[2 * i : 2 * i + 2], axis=1).astype(BF16)
            for i in range(PEERS // 2)
        ]
        + [dense_ref[...]],
        axis=1,
    )
    cross_float = cross_in.astype(F32)
    head = head_ref[...]
    fetch.wait()
    scale = (dot(cross_in, weight_ref[...]) + bias_ref[...]) + 1.0
    logit = jnp.sum(cross_float * scale * head, axis=1, keepdims=True)
    diagonal = iota((B, B), 0) == iota((B, B), 1)
    label = jnp.sum(
        jnp.where(diagonal, label_ref[...].astype(F32), 0.0), axis=1, keepdims=True
    )
    grad_logit = (1.0 / (1.0 + jnp.exp(-logit)) - label) / B
    grad_crossed = grad_logit * head
    grad_pre = (grad_crossed * cross_float).astype(BF16)
    back = dot(grad_pre, weight_ref[:POOL, :], NT)
    bag_grad = (grad_crossed[:, :POOL] * scale[:, :POOL] + back).astype(BF16)
    bags = jnp.concatenate([bag_grad[:, :D], bag_grad[:, D:]], axis=0)
    places = jnp.concatenate(
        [bag_ref[c * BLOCK : c * BLOCK + CAP, :] for c in range(PEERS)], axis=0
    )
    size = GROUP * PEERS * CAP
    for first in range(0, N_ROW, GROUP):
        picks = columns(places, first) == iota((size, 2 * B), 1) + 1
        at = slice(first * PEERS * CAP, (first + GROUP) * PEERS * CAP)
        grads_ref[at, :] = dot(picks.astype(F32).astype(BF16), bags).astype(BF16)
    share_ref[:, : 2 * POOL] = cross_in[:, : 2 * POOL]
    high = grad_logit.astype(BF16)
    rest = grad_logit - high.astype(F32)
    middle = rest.astype(BF16)
    low = (rest - middle.astype(F32)).astype(BF16)
    lane = iota((B, LANES), 1)
    pieces = jnp.where(
        lane == 0,
        high.astype(F32),
        jnp.where(lane == 1, middle.astype(F32), jnp.where(lane == 2, low.astype(F32), 0.0)),
    )
    share_ref[:, 2 * POOL :] = pieces.astype(BF16)


def aligned(index, size):
    return pl.ds(pl.multiple_of(index * size, size), size)


def block_at(place_ref, far_core, far_y, z):
    chunk = (place_ref[1] ^ far_core) * Y + (place_ref[2] ^ far_y)
    across = X // PART_COLS
    row, col = chunk * (Z // across) + z // across, z & (across - 1)
    return aligned(row, PART_ROWS), aligned(col, PART_COLS)


def weight_kernel(
    place_ref, s0, s1, s2, s3, dense_ref, head_ref, near_ref, far_ref, cross_s, logit_s, sum_s
):
    for step, share in enumerate((s0, s1, s2, s3)):
        rows = aligned((place_ref[0] + PEERS - step) & (PEERS - 1), B)
        cross_s[rows, : 2 * POOL] = share[:, : 2 * POOL]
        logit_s[rows, :] = share[:, 2 * POOL :]
    cross_s[:, 2 * POOL :] = dense_ref[...]
    grad_logit = jnp.sum(logit_s[...].astype(F32), axis=1, keepdims=True)
    grad_pre = ((grad_logit * head_ref[...]) * cross_s[...].astype(F32)).astype(BF16)
    mine = cross_s[:, aligned(place_ref[0], X // PEERS)]
    sum_s[...] = dot(mine, grad_pre, ((0,), (0,)))
    for far_core in range(CORES):
        for far_y in range(Y):
            for far_z in range(Z):
                at = block_at(place_ref, far_core, far_y, place_ref[3] ^ far_z)
                (near_ref, far_ref)[far_core][far_y, far_z] = sum_s[at]


def place_kernel(place_ref, y0, y1, y23, far_ref, out_ref):
    near = (y0, y1, y23.at[0], y23.at[1])
    for far_y in range(Y):
        for z in range(Z):
            out_ref[block_at(place_ref, 0, far_y, z)] = near[far_y][z].astype(F32)
            out_ref[block_at(place_ref, 1, far_y, z)] = far_ref[far_y, z].astype(F32)


def update_kernel(code_ref, grad_ref, table_ref, accum_ref, table_out, accum_out, sum_s):
    groups = table_ref.shape[0] // FOLD
    span = CAP * N_ROW
    total = None
    for c in range(PEERS):
        codes = code_ref[c, :8, :] - 1
        line = jnp.concatenate([codes[k : k + 1, :] for k in range(CAP)], axis=1)
        line = to_half((line & (groups - 1)) - groups // 2)
        picks = ones_where(line == half_iota((groups, span), 0, groups // 2))
        upright = codes.T // groups
        part = jnp.concatenate([upright[:, k : k + 1] for k in range(CAP)], axis=0)
        part = to_half(jnp.broadcast_to(part, (span, D)))
        grads = grad_ref[c]
        split = jnp.concatenate(
            [jnp.where(part == h, grads, jnp.zeros((), BF16)) for h in range(FOLD)], axis=1
        )
        if c == 0:
            sum_s[...] = dot(picks, split)
        else:
            sum_s[...] += dot(picks, split)
    diagonal = iota((LANES, LANES), 0) == iota((LANES, LANES), 1)
    per_table = accum_ref.shape[1]
    for block in range(table_ref.shape[0] // LANES):
        first = block * LANES
        h, inner = first // groups, first % groups
        grad = sum_s[inner : inner + LANES, h * D : (h + 1) * D]
        table, lane = first // per_table, first % per_table
        accum = accum_ref[table : table + 1, lane : lane + LANES]
        accum = jnp.sum(jnp.where(diagonal, accum, 0.0), axis=1, keepdims=True)
        accum = accum + jnp.sum(grad * grad, axis=1, keepdims=True) / D
        accum_out[table : table + 1, lane : lane + LANES] = jnp.sum(
            jnp.where(diagonal, accum, 0.0), axis=0, keepdims=True
        )
        rows = table_ref[first : first + LANES, :].astype(F32)
        table_out[first : first + LANES, :] = (
            rows - LEARN_RATE * grad / jnp.sqrt(accum)
        ).astype(BF16)


def build_index(owner, local, length, cowner, clocal, clength):
    pairs = 3 * L * LANES
    arrays = (owner, local, length, cowner, clocal, clength)
    return pl.pallas_call(
        index_kernel,
        out_shape=(
            jax.ShapeDtypeStruct((N_ROW, LANES), I32),
            jax.ShapeDtypeStruct((LANES, N_ROW), I32),
        ),
        in_specs=[pl.BlockSpec(memory_space=pltpu.HBM)] * len(arrays),
        scratch_shapes=[pltpu.VMEM(array.shape, I32) for array in arrays]
        + [pltpu.VMEM((LANES, pairs), BF16) for _ in range(4)]
        + [pltpu.SemaphoreType.DMA((len(arrays),))],
        compiler_params=pltpu.CompilerParams(vmem_limit_bytes=MOST_VMEM),
        cost_estimate=pl.CostEstimate(
            flops=2 * 10**9, bytes_accessed=200_000, transcendentals=0
        ),
    )(*arrays)


def fold_after(kernel, after, table, out_cols):
    return pl.pallas_call(
        kernel,
        out_shape=jax.ShapeDtypeStruct((2 * 2048 // FOLD, out_cols), BF16),
        in_specs=[
            pl.BlockSpec(memory_space=pl.ANY),
            pl.BlockSpec(memory_space=pltpu.VMEM),
        ],
        compiler_params=pltpu.CompilerParams(vmem_limit_bytes=VMEM),
        cost_estimate=pl.CostEstimate(flops=0, bytes_accessed=2_000_000, transcendentals=0),
    )(after, table)


def look_up(codes, fold, cfold):
    return call(
        lookup_kernel,
        jax.ShapeDtypeStruct((N_ROW * 2 * PEERS * CAP, D), BF16),
        flops=7 * 10**9,
        bytes_accessed=3_200_000,
    )(codes, fold, cfold)


def dense_step(bags, replies, dense_in, weight, bias, head, labels):
    vmem = pl.BlockSpec(memory_space=pltpu.VMEM)
    return pl.pallas_call(
        dense_kernel,
        out_shape=(
            jax.ShapeDtypeStruct((N_ROW * PEERS * CAP, D), BF16),
            jax.ShapeDtypeStruct((B, SHARE), BF16),
        ),
        in_specs=[vmem] * 3 + [pl.BlockSpec(memory_space=pltpu.HBM)] + [vmem] * 3,
        scratch_shapes=[pltpu.VMEM((X, X), BF16), pltpu.SemaphoreType.DMA],
        compiler_params=pltpu.CompilerParams(vmem_limit_bytes=MOST_VMEM),
        cost_estimate=pl.CostEstimate(
            flops=2 * 10**9, bytes_accessed=5_000_000, transcendentals=0
        ),
    )(bags, replies, dense_in, weight, bias, head, labels)


def with_place(kernel, out_shape, scratch, arrays, flops, bytes_accessed):
    return pl.pallas_call(
        kernel,
        out_shape=out_shape,
        in_specs=[pl.BlockSpec(memory_space=pltpu.SMEM)]
        + [pl.BlockSpec(memory_space=pltpu.VMEM)] * (len(arrays) - 1),
        scratch_shapes=scratch,
        compiler_params=pltpu.CompilerParams(vmem_limit_bytes=VMEM),
        cost_estimate=pl.CostEstimate(
            flops=flops, bytes_accessed=bytes_accessed, transcendentals=0
        ),
    )(*arrays)


def weight_part(place, shares, dense, head):
    half = jax.ShapeDtypeStruct((Y, Z, PART_ROWS, PART_COLS), F32)
    return with_place(
        weight_kernel,
        (half, half),
        [
            pltpu.VMEM((PEERS * B, X), BF16),
            pltpu.VMEM((PEERS * B, LANES), BF16),
            pltpu.VMEM((X // PEERS, X), F32),
        ],
        (place, *shares, dense, head),
        0,
        0,
    )


def put_in_place(place, near, far):
    return with_place(
        place_kernel,
        jax.ShapeDtypeStruct((X // PEERS, X), F32),
        [],
        (place, *near, far),
        0,
        0,
    )


def update(codes, grads, table, accum):
    groups = table.shape[0] // FOLD
    return call(
        update_kernel,
        (
            jax.ShapeDtypeStruct(table.shape, BF16),
            jax.ShapeDtypeStruct(accum.shape, F32),
        ),
        [pltpu.VMEM((groups, FOLD * D), F32)],
        flops=7 * 10**9,
        bytes_accessed=3_000_000,
    )(codes, grads, table, accum)


def to_rows(array):
    return lax.all_to_all(array, ROW, split_axis=0, concat_axis=0, tiled=True)


def to_peers(array):
    return lax.all_to_all(array, COL, split_axis=0, concat_axis=0, tiled=True)


def to_all(array):
    return lax.all_to_all(array, ALL, split_axis=0, concat_axis=0, tiled=True)


def shifted(array, axis, step):
    size = lax.axis_size(axis)
    return lax.ppermute(array, axis, [(i, (i + step) % size) for i in range(size)])


def swapped(array, axis, bit):
    return lax.ppermute(array, axis, [(i, i ^ bit) for i in range(lax.axis_size(axis))])


def along_z(array):
    return lax.all_to_all(array, "z", split_axis=0, concat_axis=0, tiled=True)


def halved(total, axis):
    bit = total.shape[0] // 2
    while bit:
        total = total[:bit] + swapped(total[bit:], axis, bit)
        bit //= 2
    return total[0]


def sum_over_rows(place, near, far, after):
    total = halved(near + swapped(far, "core", 1), "y")
    total, after = lax.optimization_barrier((total, after))
    total = halved(total, "z")
    own = along_z(jnp.broadcast_to(total.astype(BF16)[None], (Z, *total.shape)))
    side = swapped(own, "y", 1)
    rest = swapped(jnp.stack([own, side]), "y", 2)
    far = swapped(jnp.concatenate([own[None], side[None], rest]), "core", 1)
    return put_in_place(place, (own, side, rest), far), after


def per_device(
    row_tables,
    row_accum,
    col_table,
    row_owner,
    row_local,
    row_lengths,
    col_owner,
    col_local,
    col_lengths,
    dense_in,
    cross_weight,
    cross_bias,
    head_weight,
    labels,
):
    whole_weight = lax.all_gather(cross_weight, COL, axis=0, tiled=True)
    whole_dense = lax.all_gather(dense_in, COL, axis=0, tiled=True)
    head = head_weight[None, :]
    requests, bags = build_index(
        row_owner[:, :, 0].T,
        row_local.T,
        row_lengths.T,
        col_owner[:, :, 0].T,
        col_local.T,
        col_lengths[None, :],
    )
    arrived = to_rows(requests)
    cfold = fold_after(fold_cols_kernel, requests, col_table.T, FOLD * SLICE)
    codes = to_peers(arrived.T.reshape(PEERS, BLOCK, N_ROW)[:, :KEEP])
    flat_table = row_tables.reshape(-1, D)
    fold = fold_after(fold_rows_kernel, arrived, flat_table, FOLD * D)
    replies = look_up(codes, fold, cfold)
    replies = to_all(replies.reshape(OWNERS, 3, 4, D))
    replies = replies.reshape(N_ROW, PEERS, 2 * CAP, D).transpose(1, 2, 0, 3)
    grads, share = dense_step(
        bags,
        replies.reshape(PEERS, 2, CAP * N_ROW, D),
        dense_in,
        whole_weight,
        cross_bias[None, :],
        head,
        labels[None, :],
    )
    shares = [share] + [shifted(share, COL, step) for step in range(1, PEERS)]
    place = jnp.stack([lax.axis_index(axis) for axis in (COL, "core", "y", "z")]).astype(I32)
    grads = to_all(grads.reshape(OWNERS, 3, 2, D))
    near, far = weight_part(place, shares, whole_dense, head)
    weight_grad, grads = sum_over_rows(place, near, far, grads)
    grads = grads.reshape(N_ROW, PEERS, CAP, D).transpose(1, 2, 0, 3)
    grads = grads.reshape(PEERS, CAP * N_ROW, D)
    new_tables, new_accum = update(codes, grads, flat_table, row_accum)
    return (new_tables.reshape(row_tables.shape), new_accum, weight_grad)


def solution(mesh):
    split = Mesh(mesh.devices.reshape(Y, Z, CORES, PEERS), ALL)
    return jax.shard_map(
        per_device,
        mesh=split,
        in_specs=(
            P(None, ALL, None),
            P(None, ALL),
            P(ROW, COL),
            P(ALL, None, None),
            P(ALL, None),
            P(ALL, None),
            P(ALL, None, None),
            P(ALL, None),
            P(ALL),
            P(ALL, None),
            P(COL, None),
            P(),
            P(),
            P(ALL),
        ),
        out_specs=(P(None, ALL, None), P(None, ALL), P(COL, None)),
        check_vma=False,
    )
```

time: 777 us -> 320 us (0.41); the launches traced: 768 us -> 319 us
  waiting for transfers between devices: 394 us -> 112 us
  local copies, waits for them, and re-layouts: 142 us -> 3.7 us
  other arithmetic: 62.7 us -> 0.26 us
  Pallas kernels: 0 us -> 27.8 us
  starting transfers between devices: 68.4 us -> 87.9 us
    psum x1 -> x0, waiting for transfers between devices: 326 us -> none  [per_device(): weight_grad = lax.psum(peer_grad, 'row')]
    gather x13 -> x0, local copies, waits for them, and re-layouts: 81 us -> none  [the longest x2 24.7 us: per_device(): col_table[jnp.maximum(arrived, 0)]]
    ppermute x0 -> x13, starting transfers between devices: none -> 64 us  [the longest x10 54.3 us: swapped(): lax.ppermute(array, axis, [(i, i ^ bit) for i in range(lax.axis_size(axis...]
    all_to_all x7 -> x3, starting transfers between devices: 68.3 us -> 23.6 us  [the longest x2 19.6 us: to_all(): return lax.all_to_all(array, ALL, split_axis=0, concat_axis=0, tiled=True)]
    scatter-add x3 -> x0, other arithmetic: 41.1 us -> none  [the longest x2 22.3 us: bucket_ranks(): jax.ops.segment_sum(jnp.ones_like(owners), owners, num_segments=buckets)]
    scatter x5 -> x0, local copies, waits for them, and re-layouts: 31.3 us -> none  [the longest x2 12.8 us: bucket_ranks(): return jnp.zeros_like(owners).at[sorted_order].set(ranked)]
    ppermute x0 -> x13, waiting for transfers between devices: none -> 28.3 us  [the longest x10 28.3 us: swapped(): lax.ppermute(array, axis, [(i, i ^ bit) for i in range(lax.axis_size(axis...]
    pallas_call x0 -> x8, Pallas kernels: none -> 27.8 us  [the longest x1 8.37 us: look_up(): call(lookup_kernel, jax.ShapeDtypeStruct((N_ROW * 2 * PEERS * CAP, D), BF...]
  transfers between devices with their start and end apart: 10 -> 17, of which waited for: 6 -> 11; matrix products, arithmetic and copies ran while one was open for 18% -> 1% of each run, Pallas kernels for 0% -> 2%
where the time goes in v1:
time: 320 us; the launch traced here: 319 us
  waiting for transfers between devices  112 us (35%)
  starting transfers between devices  87.9 us (27%)
  blocking collectives  73.1 us (23%)
  Pallas kernels  27.8 us (9%)
  between operations  14.4 us (4%)
  local copies, waits for them, and re-layouts  3.7 us (1%)
    all_to_all x2, waiting for transfers between devices, to_all(): return lax.all_to_all(array, ALL, split_axis=0, concat_axis=0, tiled=True)  80.2 us
    ppermute x10, starting transfers between devices, swapped(): lax.ppermute(array, axis, [(i, i ^ bit) for i in range(lax.axis_size(axis...  54.3 us
    all_to_all x1, blocking collectives, to_rows(): return lax.all_to_all(array, ROW, split_axis=0, concat_axis=0, tiled=True)  35.7 us
    ppermute x10, waiting for transfers between devices, swapped(): lax.ppermute(array, axis, [(i, i ^ bit) for i in range(lax.axis_size(axis...  28.3 us
    all_to_all x1, blocking collectives, along_z(): return lax.all_to_all(array, 'z', split_axis=0, concat_axis=0, tiled=True)  23.8 us
    all_to_all x2, starting transfers between devices, to_all(): return lax.all_to_all(array, ALL, split_axis=0, concat_axis=0, tiled=True)  19.6 us
    all_gather x1, blocking collectives, per_device(): whole_dense = lax.all_gather(dense_in, COL, axis=0, tiled=True)  13.7 us
    ppermute x3, starting transfers between devices, shifted(): lax.ppermute(array, axis, [(i, (i + step) % size) for i in range(size)])  9.78 us
  transfers between devices with their start and end apart: 17, of which 11 were waited for; matrix products, arithmetic and copies ran while one was open for 1% of the time, Pallas kernels for 2%

profile of v1, /device:TPU:1, one launch (start us, length us, event | category | flops | bytes accessed | tf_op | source)
XLA Modules:
  0.0 319.1 jit_solution(3405365997866466698)
XLA Ops:
  7.2 4.3 %shard_map.157 = (s32[128,128]{1,0:T(8,128)}, s32[128,128]{1,0:T(8,128)}) custom-call(s32[16,128]{1,0:T(8,128)} %bitcast.61, s32[16,128]{1,0:T(8,128)} %bitcast.62, s32[2,128]{1,0:T(2,128)} %bitcast.66, s32[8,128]{1,0:T(8,128)} %bitcast.63, s32[8,128]{1,0:T(8,128)} %bitcast.64, s32[1,128]{1,0:T(1,128)} %bitcast.67), custom_call_target="tpu_custom_call" | custom-call | flops 2000000000 | bytes 200000 | tf_op jit(solution)/shard_map/pallas_call | solution.py:350
  11.5 35.7 %all_to_all.31 = s32[128,1,128]{2,1,0:T(1,128)S(1)} all-to-all(s32[128,1,128]{2,1,0:T(1,128)} %bitcast.53), channel_id=1, replica_groups=mesh['y'=4,'z'=16,'core'=2,'x'=4] {'y','z','core'}, dimensions={0} | all-to-all | bytes 131072 | tf_op jit(solution)/shard_map/all_to_all | solution.py:462
  47.9 4.0 %all-to-all-start.1 = ((s32[4,24,128]{2,1,0:T(8,128)}), s32[4,24,128]{2,1,0:T(8,128)S(1)}, u32[]{:S(2)}, u32[]{:S(2)}) async-start(s32[4,24,128]{2,1,0:T(8,128)} %slice.52), calls=%async_computation.1 | async-start | bytes 98304 | tf_op jit(solution)/shard_map/all_to_all | solution.py:466
  53.3 3.0 all-to-all-done.1.code_ref
  56.3 8.4 %shard_map.160 = bf16[6144,128]{1,0:T(8,128)(2,1)} custom-call(s32[4,24,128]{2,1,0:T(8,128)S(1)} %all-to-all-done.1.code_ref, bf16[512,1024]{1,0:T(8,128)(2,1)S(1)} %shard_map.158.fold_ref, bf16[512,512]{1,0:T(8,128)(2,1)S(1)} %shard_map.159.cfold_ref), custom_call_target="tpu_custom_call" | custom-call | flops 7000000000 | bytes 3200000 | tf_op jit(solution)/shard_map/pallas_call | solution.py:381
  64.7 11.0 %all-to-all-start.2 = ((bf16[512,3,4,128]{3,2,1,0:T(4,128)(2,1)}), bf16[512,3,4,128]{3,2,1,0:T(4,128)(2,1)S(1)}, u32[]{:S(2)}, u32[]{:S(2)}) async-start(bf16[512,3,4,128]{3,2,1,0:T(4,128)(2,1)} %bitcast.19), calls=%async_computation.2 | async-start | bytes 3145728 | tf_op jit(solution)/shard_map/all_to_all | solution.py:470
  76.5 80.2 %all-to-all-done.2 = bf16[512,3,4,128]{3,2,1,0:T(4,128)(2,1)S(1)} async-done(((bf16[512,3,4,128]{3,2,1,0:T(4,128)(2,1)}), bf16[512,3,4,128]{3,2,1,0:T(4,128)(2,1)S(1)}, u32[]{:S(2)}, u32[]{:S(2)}) %all-to-all-start.2) | async-done | bytes 1572896 | tf_op jit(solution)/shard_map/all_to_all | solution.py:470
  158.5 5.5 %shard_map.161 = (bf16[3072,128]{1,0:T(8,128)(2,1)}, bf16[128,640]{1,0:T(8,128)(2,1)}) custom-call(s32[128,128]{1,0:T(8,128)} %get-tuple-element.14.bag_ref, bf16[4,2,768,128]{3,2,1,0:T(8,128)(2,1)} %bitcast.58, bf16[128,512]{1,0:T(8,128)(2,1)} %dense_ref.1, bf16[1024,1024]{1,0:T(8,128)(2,1)} %all-gather.2.cloned.1.call-done.weight_in, f32[1,1024]{1,0:T(1,128)} %bitcast.65, ...), custom_call_target="tpu_custom_call" | custom-call | flops 2000000000 | bytes 5000000 | tf_op jit(solution)/shard_map/pallas_call | solution.py:391
  164.1 8.5 %all-to-all-start.3 = ((bf16[512,3,2,128]{3,2,1,0:T(2,128)(2,1)}), bf16[512,3,2,128]{3,2,1,0:T(2,128)(2,1)S(1)}, u32[]{:S(2)}, u32[]{:S(2)}) async-start(bf16[512,3,2,128]{3,2,1,0:T(2,128)(2,1)} %bitcast.59), calls=%async_computation.3 | async-start | bytes 1572864 | tf_op jit(solution)/shard_map/all_to_all | solution.py:470
  172.7 2.4 collective-permute-start
  175.1 4.3 %collective-permute-start.1 = (bf16[128,640]{1,0:T(8,128)(2,1)S(1)}, bf16[128,640]{1,0:T(8,128)(2,1)S(1)}, u32[]{:S(2)}, u32[]{:S(2)}) collective-permute-start(bf16[128,640]{1,0:T(8,128)(2,1)S(1)} %copy-done.3), channel_id=1, source_target_pairs={{0,2},{1,3},{2,0},{3,1},{4,6},{5,7},{6,4},{7,5},{8,10},{9,11},{10,... | collective-permute-start | bytes 491528 | tf_op jit(solution)/shard_map/ppermute | solution.py:475
  179.4 3.1 collective-permute-start.2
  182.5 13.7 %all_gather.7.dense_ref = bf16[512,512]{1,0:T(8,128)(2,1)S(1)} all-gather(bf16[128,512]{1,0:T(8,128)(2,1)S(1)} %copy-done.6), channel_id=1, replica_groups=mesh['y'=4,'z'=16,'core'=2,'x'=4] {'x'}, dimensions={0}, use_global_device_ids=true | all-gather | bytes 655360 | tf_op jit(solution)/shard_map/all_gather | solution.py:522
  196.2 2.0 shard_map.162
  198.2 7.2 %collective-permute-start.3 = (f32[4,16,8,256]{3,2,1,0:T(8,128)S(1)}, f32[4,16,8,256]{3,2,1,0:T(8,128)S(1)}, u32[]{:S(2)}, u32[]{:S(2)}) collective-permute-start(f32[4,16,8,256]{3,2,1,0:T(8,128)S(1)} %get-tuple-element.17), channel_id=1, source_target_pairs={{0,4},{4,0},{1,5},{5,1},{2,6},{6,2},{3,7},{7,3},{8,12},{12,8},{9,1... | collective-permute-start | bytes 1572872 | tf_op jit(solution)/shard_map/ppermute | solution.py:479
  207.1 2.0 collective-permute-start.4
  209.2 9.1 %collective-permute-done.4 = f32[2,16,8,256]{3,2,1,0:T(8,128)S(1)} collective-permute-done((f32[2,16,8,256]{3,2,1,0:T(8,128)S(1)}, f32[2,16,8,256]{3,2,1,0:T(8,128)S(1)}, u32[]{:S(2)}, u32[]{:S(2)}) %collective-permute-start.4) | collective-permute-done | bytes 262176 | tf_op jit(solution)/shard_map/ppermute | solution.py:479
  220.3 3.8 %collective-permute-done.5 = f32[1,16,8,256]{3,2,1,0:T(8,128)S(1)} collective-permute-done((f32[1,16,8,256]{3,2,1,0:T(8,128)S(1)}, f32[1,16,8,256]{3,2,1,0:T(8,128)S(1)}, u32[]{:S(2)}, u32[]{:S(2)}) %collective-permute-start.5) | collective-permute-done | bytes 131104 | tf_op jit(solution)/shard_map/ppermute | solution.py:479
  224.1 11.0 %collective-permute-start.6 = (f32[8,8,256]{2,1,0:T(8,128)S(1)}, f32[8,8,256]{2,1,0:T(8,128)S(1)}, u32[]{:S(2)}, u32[]{:S(2)}) collective-permute-start(f32[8,8,256]{2,1,0:T(8,128)S(1)} %slice.45), channel_id=1, source_target_pairs={{0,64},{8,72},{16,80},{24,88},{32,96},{40,104},{48,112},{56,120},{... | collective-permute-start | bytes 196616 | tf_op jit(solution)/shard_map/ppermute | solution.py:479
  235.1 2.8 collective-permute-done.6
  237.9 5.7 %collective-permute-start.7 = (f32[4,8,256]{2,1,0:T(8,128)S(1)}, f32[4,8,256]{2,1,0:T(8,128)S(1)}, u32[]{:S(2)}, u32[]{:S(2)}) collective-permute-start(f32[4,8,256]{2,1,0:T(8,128)S(1)} %slice.58), channel_id=1, source_target_pairs={{0,32},{8,40},{16,48},{24,56},{32,0},{40,8},{48,16},{56,24},{64,96... | collective-permute-start | bytes 98312 | tf_op jit(solution)/shard_map/ppermute | solution.py:479
  243.6 2.9 collective-permute-done.7
  246.5 3.5 %collective-permute-start.8 = (f32[2,8,256]{2,1,0:T(8,128)S(1)}, f32[2,8,256]{2,1,0:T(8,128)S(1)}, u32[]{:S(2)}, u32[]{:S(2)}) collective-permute-start(f32[2,8,256]{2,1,0:T(8,128)S(1)} %slice.60), channel_id=1, source_target_pairs={{0,16},{8,24},{16,0},{24,8},{32,48},{40,56},{48,32},{56,40},{64,80... | collective-permute-start | bytes 49160 | tf_op jit(solution)/shard_map/ppermute | solution.py:479
  251.9 2.2 collective-permute-start.9
  254.1 2.1 collective-permute-done.9
  256.3 23.8 %all_to_all.32.y0 = bf16[16,8,256]{2,1,0:T(8,128)(2,1)S(1)} all-to-all(bf16[16,8,256]{2,1,0:T(8,128)(2,1)S(1)} %broadcast_in_dim.27), channel_id=1, replica_groups=mesh['y'=4,'z'=16,'core'=2,'x'=4] {'z'}, dimensions={0} | all-to-all | bytes 131072 | tf_op jit(solution)/shard_map/all_to_all | solution.py:483
  280.1 3.3 %collective-permute-start.10 = (bf16[16,8,256]{2,1,0:T(8,128)(2,1)S(1)}, bf16[16,8,256]{2,1,0:T(8,128)(2,1)S(1)}, u32[]{:S(2)}, u32[]{:S(2)}) collective-permute-start(bf16[16,8,256]{2,1,0:T(8,128)(2,1)S(1)} %all_to_all.32.y0), channel_id=1, source_target_pairs={{0,128},{128,0},{256,384},{384,256},{1,129},{129,1},{257,385},{385... | collective-permute-start | bytes 196616 | tf_op jit(solution)/shard_map/ppermute | solution.py:479
  283.4 2.0 collective-permute-done.10.y1
  285.4 4.8 %collective-permute-start.11 = (bf16[2,16,8,256]{3,2,1,0:T(8,128)(2,1)S(1)}, bf16[2,16,8,256]{3,2,1,0:T(8,128)(2,1)S(1)}, u32[]{:S(2)}, u32[]{:S(2)}) collective-permute-start(bf16[2,16,8,256]{3,2,1,0:T(8,128)(2,1)S(1)} %pad_maximum_fusion.1), channel_id=1, source_target_pairs={{0,256},{128,384},{256,0},{384,128},{1,257},{129,385},{257,1},{385... | collective-permute-start | bytes 393224 | tf_op jit(solution)/shard_map/ppermute | solution.py:479
  290.5 2.1 collective-permute-done.11.y23
  292.7 12.6 %collective-permute-start.12 = (bf16[4,16,8,256]{3,2,1,0:T(8,128)(2,1)S(1)}, bf16[4,16,8,256]{3,2,1,0:T(8,128)(2,1)S(1)}, u32[]{:S(2)}, u32[]{:S(2)}) collective-permute-start(bf16[4,16,8,256]{3,2,1,0:T(8,128)(2,1)S(1)} %pad_maximum_fusion), channel_id=1, source_target_pairs={{0,4},{4,0},{1,5},{5,1},{2,6},{6,2},{3,7},{7,3},{8,12},{12,8},{9,1... | collective-permute-start | bytes 786440 | tf_op jit(solution)/shard_map/ppermute | solution.py:479
  305.3 5.5 %shard_map.163 = (bf16[4096,128]{1,0:T(8,128)(2,1)}, f32[2,2048]{1,0:T(2,128)}) custom-call(s32[4,24,128]{2,1,0:T(8,128)S(1)} %all-to-all-done.1.code_ref, bf16[4,768,128]{2,1,0:T(8,128)(2,1)S(1)} %bitcast.47, bf16[4096,128]{1,0:T(8,128)(2,1)S(1)} %bitcast.44, f32[2,2048]{1,0:T(2,128)S(1)} %copy-done.5), custom_call_target="tpu_custom_call" | custom-call | flops 7000000000 | bytes 3000000 | tf_op jit(solution)/shard_map/pallas_call | solution.py:449
  (51 shorter events, 12.1 us)
Async XLA Ops:
  7.2 44.8 %copy-start.1 = (bf16[4096,64]{0,1:T(8,128)(2,1)S(1)}, bf16[4096,64]{0,1:T(8,128)(2,1)}, u32[]{:S(2)}) copy-start(bf16[4096,64]{0,1:T(8,128)(2,1)} %param.16) | copy-start | bytes 1572868
  11.5 41.5 %copy-start = (bf16[2,2048,128]{2,1,0:T(8,128)(2,1)S(1)}, bf16[2,2048,128]{2,1,0:T(8,128)(2,1)}, u32[]{:S(2)}) copy-start(bf16[2,2048,128]{2,1,0:T(8,128)(2,1)} %param.14) | copy-start | bytes 3145732
  47.9 8.4 %all-to-all-start.1 = ((s32[4,24,128]{2,1,0:T(8,128)}), s32[4,24,128]{2,1,0:T(8,128)S(1)}, u32[]{:S(2)}, u32[]{:S(2)}) async-start(s32[4,24,128]{2,1,0:T(8,128)} %slice.52), calls=%async_computation.1 | async-start | bytes 98304 | tf_op jit(solution)/shard_map/all_to_all | solution.py:466
  51.9 0.8 copy-start.2
  64.7 92.0 %all-to-all-start.2 = ((bf16[512,3,4,128]{3,2,1,0:T(4,128)(2,1)}), bf16[512,3,4,128]{3,2,1,0:T(4,128)(2,1)S(1)}, u32[]{:S(2)}, u32[]{:S(2)}) async-start(bf16[512,3,4,128]{3,2,1,0:T(4,128)(2,1)} %bitcast.19), calls=%async_computation.2 | async-start | bytes 3145728 | tf_op jit(solution)/shard_map/all_to_all | solution.py:470
  75.7 82.8 %all-gather.2.cloned.1.call-start = ((), (), s32[]{:S(2)}) async-start(), calls=%async_computation.5 | async-start | bytes 2621440 | tf_op jit(solution)/shard_map/all_gather | solution.py:521
  164.0 8.6 %copy-start.3 = (bf16[128,640]{1,0:T(8,128)(2,1)S(1)}, bf16[128,640]{1,0:T(8,128)(2,1)}, u32[]{:S(2)}) copy-start(bf16[128,640]{1,0:T(8,128)(2,1)} %get-tuple-element.15.s0) | copy-start | bytes 491524
  164.1 18.4 %copy-start.6 = (bf16[128,512]{1,0:T(8,128)(2,1)S(1)}, bf16[128,512]{1,0:T(8,128)(2,1)}, u32[]{:S(2)}) copy-start(bf16[128,512]{1,0:T(8,128)(2,1)} %dense_ref.1) | copy-start | bytes 393220
  164.1 32.1 %copy-start.4 = (f32[1024]{0:T(1024)S(1)}, f32[1024]{0:T(1024)}, u32[]{:S(2)}) copy-start(f32[1024]{0:T(1024)} %param.26) | copy-start | bytes 12292
  164.1 60.0 %all-to-all-start.3 = ((bf16[512,3,2,128]{3,2,1,0:T(2,128)(2,1)}), bf16[512,3,2,128]{3,2,1,0:T(2,128)(2,1)S(1)}, u32[]{:S(2)}, u32[]{:S(2)}) async-start(bf16[512,3,2,128]{3,2,1,0:T(2,128)(2,1)} %bitcast.59), calls=%async_computation.3 | async-start | bytes 1572864 | tf_op jit(solution)/shard_map/all_to_all | solution.py:470
  172.7 23.5 %collective-permute-start = (bf16[128,640]{1,0:T(8,128)(2,1)S(1)}, bf16[128,640]{1,0:T(8,128)(2,1)S(1)}, u32[]{:S(2)}, u32[]{:S(2)}) collective-permute-start(bf16[128,640]{1,0:T(8,128)(2,1)S(1)} %copy-done.3), channel_id=1, source_target_pairs={{0,1},{1,2},{2,3},{3,0},{4,5},{5,6},{6,7},{7,4},{8,9},{9,10},{10,1... | collective-permute-start | bytes 491528 | tf_op jit(solution)/shard_map/ppermute | solution.py:475
  175.1 21.1 %collective-permute-start.1 = (bf16[128,640]{1,0:T(8,128)(2,1)S(1)}, bf16[128,640]{1,0:T(8,128)(2,1)S(1)}, u32[]{:S(2)}, u32[]{:S(2)}) collective-permute-start(bf16[128,640]{1,0:T(8,128)(2,1)S(1)} %copy-done.3), channel_id=1, source_target_pairs={{0,2},{1,3},{2,0},{3,1},{4,6},{5,7},{6,4},{7,5},{8,10},{9,11},{10,... | collective-permute-start | bytes 491528 | tf_op jit(solution)/shard_map/ppermute | solution.py:475
  179.4 16.8 %collective-permute-start.2 = (bf16[128,640]{1,0:T(8,128)(2,1)S(1)}, bf16[128,640]{1,0:T(8,128)(2,1)S(1)}, u32[]{:S(2)}, u32[]{:S(2)}) collective-permute-start(bf16[128,640]{1,0:T(8,128)(2,1)S(1)} %copy-done.3), channel_id=1, source_target_pairs={{0,3},{1,0},{2,1},{3,2},{4,7},{5,4},{6,5},{7,6},{8,11},{9,8},{10,9... | collective-permute-start | bytes 491528 | tf_op jit(solution)/shard_map/ppermute | solution.py:475
  198.2 8.8 %collective-permute-start.3 = (f32[4,16,8,256]{3,2,1,0:T(8,128)S(1)}, f32[4,16,8,256]{3,2,1,0:T(8,128)S(1)}, u32[]{:S(2)}, u32[]{:S(2)}) collective-permute-start(f32[4,16,8,256]{3,2,1,0:T(8,128)S(1)} %get-tuple-element.17), channel_id=1, source_target_pairs={{0,4},{4,0},{1,5},{5,1},{2,6},{6,2},{3,7},{7,3},{8,12},{12,8},{9,1... | collective-permute-start | bytes 1572872 | tf_op jit(solution)/shard_map/ppermute | solution.py:479
  207.1 11.2 %collective-permute-start.4 = (f32[2,16,8,256]{3,2,1,0:T(8,128)S(1)}, f32[2,16,8,256]{3,2,1,0:T(8,128)S(1)}, u32[]{:S(2)}, u32[]{:S(2)}) collective-permute-start(f32[2,16,8,256]{3,2,1,0:T(8,128)S(1)} %slice.54), channel_id=1, source_target_pairs={{0,256},{128,384},{256,0},{384,128},{1,257},{129,385},{257,1},{385... | collective-permute-start | bytes 786440 | tf_op jit(solution)/shard_map/ppermute | solution.py:479
  218.3 5.7 %collective-permute-start.5 = (f32[1,16,8,256]{3,2,1,0:T(8,128)S(1)}, f32[1,16,8,256]{3,2,1,0:T(8,128)S(1)}, u32[]{:S(2)}, u32[]{:S(2)}) collective-permute-start(f32[1,16,8,256]{3,2,1,0:T(8,128)S(1)} %slice.56), channel_id=1, source_target_pairs={{0,128},{128,0},{256,384},{384,256},{1,129},{129,1},{257,385},{385... | collective-permute-start | bytes 393224 | tf_op jit(solution)/shard_map/ppermute | solution.py:479
  224.1 13.8 %collective-permute-start.6 = (f32[8,8,256]{2,1,0:T(8,128)S(1)}, f32[8,8,256]{2,1,0:T(8,128)S(1)}, u32[]{:S(2)}, u32[]{:S(2)}) collective-permute-start(f32[8,8,256]{2,1,0:T(8,128)S(1)} %slice.45), channel_id=1, source_target_pairs={{0,64},{8,72},{16,80},{24,88},{32,96},{40,104},{48,112},{56,120},{... | collective-permute-start | bytes 196616 | tf_op jit(solution)/shard_map/ppermute | solution.py:479
  237.9 8.6 %collective-permute-start.7 = (f32[4,8,256]{2,1,0:T(8,128)S(1)}, f32[4,8,256]{2,1,0:T(8,128)S(1)}, u32[]{:S(2)}, u32[]{:S(2)}) collective-permute-start(f32[4,8,256]{2,1,0:T(8,128)S(1)} %slice.58), channel_id=1, source_target_pairs={{0,32},{8,40},{16,48},{24,56},{32,0},{40,8},{48,16},{56,24},{64,96... | collective-permute-start | bytes 98312 | tf_op jit(solution)/shard_map/ppermute | solution.py:479
  246.5 5.4 %collective-permute-start.8 = (f32[2,8,256]{2,1,0:T(8,128)S(1)}, f32[2,8,256]{2,1,0:T(8,128)S(1)}, u32[]{:S(2)}, u32[]{:S(2)}) collective-permute-start(f32[2,8,256]{2,1,0:T(8,128)S(1)} %slice.60), channel_id=1, source_target_pairs={{0,16},{8,24},{16,0},{24,8},{32,48},{40,56},{48,32},{56,40},{64,80... | collective-permute-start | bytes 49160 | tf_op jit(solution)/shard_map/ppermute | solution.py:479
  251.9 4.4 %collective-permute-start.9 = (f32[1,8,256]{2,1,0:T(8,128)S(1)}, f32[1,8,256]{2,1,0:T(8,128)S(1)}, u32[]{:S(2)}, u32[]{:S(2)}) collective-permute-start(f32[1,8,256]{2,1,0:T(8,128)S(1)} %slice.62), channel_id=1, source_target_pairs={{0,8},{8,0},{16,24},{24,16},{32,40},{40,32},{48,56},{56,48},{64,72... | collective-permute-start | bytes 24584 | tf_op jit(solution)/shard_map/ppermute | solution.py:479
  280.1 5.3 %collective-permute-start.10 = (bf16[16,8,256]{2,1,0:T(8,128)(2,1)S(1)}, bf16[16,8,256]{2,1,0:T(8,128)(2,1)S(1)}, u32[]{:S(2)}, u32[]{:S(2)}) collective-permute-start(bf16[16,8,256]{2,1,0:T(8,128)(2,1)S(1)} %all_to_all.32.y0), channel_id=1, source_target_pairs={{0,128},{128,0},{256,384},{384,256},{1,129},{129,1},{257,385},{385... | collective-permute-start | bytes 196616 | tf_op jit(solution)/shard_map/ppermute | solution.py:479
  285.4 19.8 %copy-start.5 = (f32[2,2048]{1,0:T(2,128)S(1)}, f32[2,2048]{1,0:T(2,128)}, u32[]{:S(2)}) copy-start(f32[2,2048]{1,0:T(2,128)} %accum_ref.1) | copy-start | bytes 49156
  285.4 7.2 %collective-permute-start.11 = (bf16[2,16,8,256]{3,2,1,0:T(8,128)(2,1)S(1)}, bf16[2,16,8,256]{3,2,1,0:T(8,128)(2,1)S(1)}, u32[]{:S(2)}, u32[]{:S(2)}) collective-permute-start(bf16[2,16,8,256]{3,2,1,0:T(8,128)(2,1)S(1)} %pad_maximum_fusion.1), channel_id=1, source_target_pairs={{0,256},{128,384},{256,0},{384,128},{1,257},{129,385},{257,1},{385... | collective-permute-start | bytes 393224 | tf_op jit(solution)/shard_map/ppermute | solution.py:479
  292.7 18.0 %collective-permute-start.12 = (bf16[4,16,8,256]{3,2,1,0:T(8,128)(2,1)S(1)}, bf16[4,16,8,256]{3,2,1,0:T(8,128)(2,1)S(1)}, u32[]{:S(2)}, u32[]{:S(2)}) collective-permute-start(bf16[4,16,8,256]{3,2,1,0:T(8,128)(2,1)S(1)} %pad_maximum_fusion), channel_id=1, source_target_pairs={{0,4},{4,0},{1,5},{5,1},{2,6},{6,2},{3,7},{7,3},{8,12},{12,8},{9,1... | collective-permute-start | bytes 786440 | tf_op jit(solution)/shard_map/ppermute | solution.py:479
Sparse Core Ops, SparseCore 0:
  78.7 45.5 all-gather.1

commit v2 on v1

--- a/solution.py
+++ b/solution.py
@@ -7,6 +7,8 @@
 
 ROW = ("y", "z", "core")
 COL = "x"
+LINE = ("y", "core", "z")
+NEAR_Z = ("y", "core", "x", "z")
 ALL = ROW + (COL,)
 Y, Z, CORES, PEERS = 4, 16, 2, 4
 N_ROW = Y * Z * CORES
@@ -21,6 +23,7 @@
 POOL = 256
 LEARN_RATE = 0.05
 LANES = 128
+DENSE = 512
 SHARE = 2 * POOL + LANES
 BLOCK = LANES // PEERS
 KEEP = 24
@@ -29,6 +32,7 @@
 PART_ROWS, PART_COLS = 8, X // 4
 VMEM = 40 * 1024 * 1024
 MOST_VMEM = 60 * 1024 * 1024
+DENSE_VMEM = 58 * 1024 * 1024
 
 F32 = jnp.float32
 BF16 = jnp.bfloat16
@@ -102,6 +106,7 @@
     rows128 = iota((LANES, LANES), 0)
 
     def put(step, row, spot, code, bag):
+        row = jnp.where(row < 0, -1, (row & 96) | ((row & 1) << 4) | ((row >> 1) & 15))
         at = slice(step * LANES, (step + 1) * LANES)
         own_s[:, at] = (rows128 == row).astype(F32).astype(BF16)
         high_s[:, at] = jnp.where(spot, code >> 6, 0).astype(F32).astype(BF16)
@@ -139,6 +144,13 @@
     return jnp.concatenate([codes[:, r : r + 1] for r in range(first, first + GROUP)], axis=0)
 
 
+def peer_major():
+    for c in range(PEERS):
+        for r in range(GROUP):
+            first = (r * PEERS + c) * CAP
+            yield slice(first, first + CAP)
+
+
 def fold_cols_kernel(after_ref, col_ref, out_ref):
     groups = out_ref.shape[0]
     for pair in range(FOLD // 2):
@@ -189,9 +201,9 @@
             halves.append(jnp.where((part & 1) == i, got, turned))
         cols = jnp.where(left, halves[0], halves[1])
         parts = []
-        for r in range(GROUP * PEERS):
-            parts.append(rows[r * CAP : (r + 1) * CAP])
-            parts.append(cols[r * CAP : (r + 1) * CAP])
+        for at in peer_major():
+            parts.append(rows[at])
+            parts.append(cols[at])
         out_ref[first * 2 * wide : (first + GROUP) * 2 * wide, :] = jnp.concatenate(
             parts, axis=0
         ).astype(BF16)
@@ -199,10 +211,17 @@
 
 def dense_kernel(
     bag_ref, reply_ref, dense_ref, weight_in, bias_ref, head_ref, label_ref,
-    grads_ref, share_ref, weight_ref, sem,
+    grads_ref, share_ref, weight_ref, sems,
 ):
-    fetch = pltpu.make_async_copy(weight_in, weight_ref, sem)
-    fetch.start()
+    wide = X // PEERS
+    fetches = [
+        pltpu.make_async_copy(
+            weight_in.at[c, pl.ds(0, wide)], weight_ref.at[pl.ds(c * wide, wide)], sems.at[c]
+        )
+        for c in range(PEERS)
+    ]
+    for fetch in fetches:
+        fetch.start()
     span = CAP * N_ROW
 
     def lanes_of(first):
@@ -232,7 +251,8 @@
     )
     cross_float = cross_in.astype(F32)
     head = head_ref[...]
-    fetch.wait()
+    for fetch in fetches:
+        fetch.wait()
     scale = (dot(cross_in, weight_ref[...]) + bias_ref[...]) + 1.0
     logit = jnp.sum(cross_float * scale * head, axis=1, keepdims=True)
     diagonal = iota((B, B), 0) == iota((B, B), 1)
@@ -252,7 +272,10 @@
     for first in range(0, N_ROW, GROUP):
         picks = columns(places, first) == iota((size, 2 * B), 1) + 1
         at = slice(first * PEERS * CAP, (first + GROUP) * PEERS * CAP)
-        grads_ref[at, :] = dot(picks.astype(F32).astype(BF16), bags).astype(BF16)
+        spread = dot(picks.astype(F32).astype(BF16), bags)
+        grads_ref[at, :] = jnp.concatenate([spread[one] for one in peer_major()], axis=0).astype(
+            BF16
+        )
     share_ref[:, : 2 * POOL] = cross_in[:, : 2 * POOL]
     high = grad_logit.astype(BF16)
     rest = grad_logit - high.astype(F32)
@@ -268,41 +291,59 @@
 
 
 def aligned(index, size):
+    if isinstance(index, int):
+        return slice(index * size, (index + 1) * size)
     return pl.ds(pl.multiple_of(index * size, size), size)
 
 
-def block_at(place_ref, far_core, far_y, z):
-    chunk = (place_ref[1] ^ far_core) * Y + (place_ref[2] ^ far_y)
+def blocks_of(core, y):
     across = X // PART_COLS
-    row, col = chunk * (Z // across) + z // across, z & (across - 1)
-    return aligned(row, PART_ROWS), aligned(col, PART_COLS)
+    for z in range(Z):
+        row = (core * Y + y) * (Z // across) + z // across
+        col = z % across * PART_COLS
+        yield aligned(row, PART_ROWS), slice(col, col + PART_COLS)
 
 
 def weight_kernel(
-    place_ref, s0, s1, s2, s3, dense_ref, head_ref, near_ref, far_ref, cross_s, logit_s, sum_s
+    place_ref, s0, s1, s2, s3, joined_ref, head_ref, near_ref, far_ref,
+    cross_s, logit_s, dense_s, sum_s, sems,
 ):
+    wide = X // PEERS
+    fetches = [
+        pltpu.make_async_copy(
+            joined_ref.at[c, pl.ds(wide, B // 2)], dense_s.at[c], sems.at[c]
+        )
+        for c in range(PEERS)
+    ]
+    for fetch in fetches:
+        fetch.start()
     for step, share in enumerate((s0, s1, s2, s3)):
         rows = aligned((place_ref[0] + PEERS - step) & (PEERS - 1), B)
         cross_s[rows, : 2 * POOL] = share[:, : 2 * POOL]
         logit_s[rows, :] = share[:, 2 * POOL :]
-    cross_s[:, 2 * POOL :] = dense_ref[...]
     grad_logit = jnp.sum(logit_s[...].astype(F32), axis=1, keepdims=True)
+    for c in range(PEERS):
+        fetches[c].wait()
+        for half in range(2):
+            first = c * B + half * (B // 2)
+            cross_s[first : first + B // 2, 2 * POOL :] = dense_s[
+                c, :, half * DENSE : (half + 1) * DENSE
+            ]
     grad_pre = ((grad_logit * head_ref[...]) * cross_s[...].astype(F32)).astype(BF16)
-    mine = cross_s[:, aligned(place_ref[0], X // PEERS)]
+    mine = cross_s[:, aligned(place_ref[0], wide)]
     sum_s[...] = dot(mine, grad_pre, ((0,), (0,)))
     for far_core in range(CORES):
         for far_y in range(Y):
-            for far_z in range(Z):
-                at = block_at(place_ref, far_core, far_y, place_ref[3] ^ far_z)
-                (near_ref, far_ref)[far_core][far_y, far_z] = sum_s[at]
-
-
-def place_kernel(place_ref, y0, y1, y23, far_ref, out_ref):
-    near = (y0, y1, y23.at[0], y23.at[1])
-    for far_y in range(Y):
-        for z in range(Z):
-            out_ref[block_at(place_ref, 0, far_y, z)] = near[far_y][z].astype(F32)
-            out_ref[block_at(place_ref, 1, far_y, z)] = far_ref[far_y, z].astype(F32)
+            parts = blocks_of(place_ref[1] ^ far_core, (place_ref[2] + far_y) & (Y - 1))
+            for z, at in enumerate(parts):
+                (near_ref, far_ref)[far_core][far_y, z] = sum_s[at]
+
+
+def place_kernel(parts_ref, out_ref):
+    for y in range(Y):
+        for core in range(CORES):
+            for z, (rows, cols) in enumerate(blocks_of(core, y)):
+                out_ref[rows, cols] = parts_ref[y * CORES + core, z].astype(F32)
 
 
 def update_kernel(code_ref, grad_ref, table_ref, accum_ref, table_out, accum_out, sum_s):
@@ -395,53 +436,37 @@
             jax.ShapeDtypeStruct((B, SHARE), BF16),
         ),
         in_specs=[vmem] * 3 + [pl.BlockSpec(memory_space=pltpu.HBM)] + [vmem] * 3,
-        scratch_shapes=[pltpu.VMEM((X, X), BF16), pltpu.SemaphoreType.DMA],
-        compiler_params=pltpu.CompilerParams(vmem_limit_bytes=MOST_VMEM),
+        scratch_shapes=[pltpu.VMEM((X, X), BF16), pltpu.SemaphoreType.DMA((PEERS,))],
+        compiler_params=pltpu.CompilerParams(vmem_limit_bytes=DENSE_VMEM),
         cost_estimate=pl.CostEstimate(
             flops=2 * 10**9, bytes_accessed=5_000_000, transcendentals=0
         ),
     )(bags, replies, dense_in, weight, bias, head, labels)
 
 
-def with_place(kernel, out_shape, scratch, arrays, flops, bytes_accessed):
+def weight_part(place, shares, joined, head):
+    half = jax.ShapeDtypeStruct((Y, Z, PART_ROWS, PART_COLS), F32)
+    vmem = pl.BlockSpec(memory_space=pltpu.VMEM)
     return pl.pallas_call(
-        kernel,
-        out_shape=out_shape,
+        weight_kernel,
+        out_shape=(half, half),
         in_specs=[pl.BlockSpec(memory_space=pltpu.SMEM)]
-        + [pl.BlockSpec(memory_space=pltpu.VMEM)] * (len(arrays) - 1),
-        scratch_shapes=scratch,
-        compiler_params=pltpu.CompilerParams(vmem_limit_bytes=VMEM),
-        cost_estimate=pl.CostEstimate(
-            flops=flops, bytes_accessed=bytes_accessed, transcendentals=0
-        ),
-    )(*arrays)
-
-
-def weight_part(place, shares, dense, head):
-    half = jax.ShapeDtypeStruct((Y, Z, PART_ROWS, PART_COLS), F32)
-    return with_place(
-        weight_kernel,
-        (half, half),
-        [
+        + [vmem] * PEERS
+        + [pl.BlockSpec(memory_space=pltpu.HBM), vmem],
+        scratch_shapes=[
             pltpu.VMEM((PEERS * B, X), BF16),
             pltpu.VMEM((PEERS * B, LANES), BF16),
+            pltpu.VMEM((PEERS, B // 2, X), BF16),
             pltpu.VMEM((X // PEERS, X), F32),
+            pltpu.SemaphoreType.DMA((PEERS,)),
         ],
-        (place, *shares, dense, head),
-        0,
-        0,
-    )
-
-
-def put_in_place(place, near, far):
-    return with_place(
-        place_kernel,
-        jax.ShapeDtypeStruct((X // PEERS, X), F32),
-        [],
-        (place, *near, far),
-        0,
-        0,
-    )
+        compiler_params=pltpu.CompilerParams(vmem_limit_bytes=VMEM),
+        cost_estimate=pl.CostEstimate(flops=0, bytes_accessed=0, transcendentals=0),
+    )(place, *shares, joined, head)
+
+
+def put_in_place(parts):
+    return call(place_kernel, jax.ShapeDtypeStruct((X // PEERS, X), F32))(parts)
 
 
 def update(codes, grads, table, accum):
@@ -458,16 +483,8 @@
     )(codes, grads, table, accum)
 
 
-def to_rows(array):
-    return lax.all_to_all(array, ROW, split_axis=0, concat_axis=0, tiled=True)
-
-
-def to_peers(array):
-    return lax.all_to_all(array, COL, split_axis=0, concat_axis=0, tiled=True)
-
-
-def to_all(array):
-    return lax.all_to_all(array, ALL, split_axis=0, concat_axis=0, tiled=True)
+def exchange(array, axes):
+    return lax.all_to_all(array, axes, split_axis=0, concat_axis=0, tiled=True)
 
 
 def shifted(array, axis, step):
@@ -475,31 +492,21 @@
     return lax.ppermute(array, axis, [(i, (i + step) % size) for i in range(size)])
 
 
-def swapped(array, axis, bit):
-    return lax.ppermute(array, axis, [(i, i ^ bit) for i in range(lax.axis_size(axis))])
-
-
-def along_z(array):
-    return lax.all_to_all(array, "z", split_axis=0, concat_axis=0, tiled=True)
-
-
-def halved(total, axis):
-    bit = total.shape[0] // 2
-    while bit:
-        total = total[:bit] + swapped(total[bit:], axis, bit)
-        bit //= 2
-    return total[0]
-
-
-def sum_over_rows(place, near, far, after):
-    total = halved(near + swapped(far, "core", 1), "y")
-    total, after = lax.optimization_barrier((total, after))
-    total = halved(total, "z")
-    own = along_z(jnp.broadcast_to(total.astype(BF16)[None], (Z, *total.shape)))
-    side = swapped(own, "y", 1)
-    rest = swapped(jnp.stack([own, side]), "y", 2)
-    far = swapped(jnp.concatenate([own[None], side[None], rest]), "core", 1)
-    return put_in_place(place, (own, side, rest), far), after
+def sum_over_rows(near, far, after):
+    total = near + shifted(far, "core", 1)
+    own = total[0]
+    for step in range(1, Y):
+        own = own + shifted(total[step], "y", step)
+    own, after = lax.optimization_barrier((own, after))
+    own = jnp.sum(exchange(own, "z"), axis=0).astype(BF16)
+    own = exchange(jnp.broadcast_to(own[None], (Z, *own.shape)), "z")
+    parts = exchange(jnp.broadcast_to(own[None], (Y * CORES, *own.shape)), ("y", "core"))
+    return put_in_place(parts), after
+
+
+def by_peer(array, rows):
+    array = array.reshape(Y * CORES, PEERS, Z, rows, D).transpose(1, 3, 0, 2, 4)
+    return array.reshape(PEERS, rows, N_ROW, D)
 
 
 def per_device(
@@ -518,8 +525,9 @@
     head_weight,
     labels,
 ):
-    whole_weight = lax.all_gather(cross_weight, COL, axis=0, tiled=True)
-    whole_dense = lax.all_gather(dense_in, COL, axis=0, tiled=True)
+    packed = jnp.concatenate([dense_in[: B // 2], dense_in[B // 2 :]], axis=1)
+    joined = jnp.concatenate([cross_weight, packed], axis=0)
+    joined = lax.all_gather(joined, COL, axis=0)
     head = head_weight[None, :]
     requests, bags = build_index(
         row_owner[:, :, 0].T,
@@ -529,30 +537,28 @@
         col_local.T,
         col_lengths[None, :],
     )
-    arrived = to_rows(requests)
+    arrived = exchange(requests, LINE)
     cfold = fold_after(fold_cols_kernel, requests, col_table.T, FOLD * SLICE)
-    codes = to_peers(arrived.T.reshape(PEERS, BLOCK, N_ROW)[:, :KEEP])
+    codes = exchange(arrived.T.reshape(PEERS, BLOCK, N_ROW)[:, :KEEP], COL)
     flat_table = row_tables.reshape(-1, D)
     fold = fold_after(fold_rows_kernel, arrived, flat_table, FOLD * D)
     replies = look_up(codes, fold, cfold)
-    replies = to_all(replies.reshape(OWNERS, 3, 4, D))
-    replies = replies.reshape(N_ROW, PEERS, 2 * CAP, D).transpose(1, 2, 0, 3)
+    replies = by_peer(exchange(replies.reshape(OWNERS, 3, 4, D), NEAR_Z), 2 * CAP)
     grads, share = dense_step(
         bags,
         replies.reshape(PEERS, 2, CAP * N_ROW, D),
         dense_in,
-        whole_weight,
+        joined,
         cross_bias[None, :],
         head,
         labels[None, :],
     )
     shares = [share] + [shifted(share, COL, step) for step in range(1, PEERS)]
-    place = jnp.stack([lax.axis_index(axis) for axis in (COL, "core", "y", "z")]).astype(I32)
-    grads = to_all(grads.reshape(OWNERS, 3, 2, D))
-    near, far = weight_part(place, shares, whole_dense, head)
-    weight_grad, grads = sum_over_rows(place, near, far, grads)
-    grads = grads.reshape(N_ROW, PEERS, CAP, D).transpose(1, 2, 0, 3)
-    grads = grads.reshape(PEERS, CAP * N_ROW, D)
+    place = jnp.stack([lax.axis_index(axis) for axis in (COL, "core", "y")]).astype(I32)
+    grads = exchange(grads.reshape(OWNERS, 3, 2, D), NEAR_Z)
+    near, far = weight_part(place, shares, joined, head)
+    weight_grad, grads = sum_over_rows(near, far, grads)
+    grads = by_peer(grads, CAP).reshape(PEERS, CAP * N_ROW, D)
     new_tables, new_accum = update(codes, grads, flat_table, row_accum)
     return (new_tables.reshape(row_tables.shape), new_accum, weight_grad)
 

time: 320 us -> 281 us (0.88)
  starting transfers between devices: 87.9 us -> 63.8 us
  blocking collectives: 73.1 us -> 54.2 us
    ppermute x10 -> x0, starting transfers between devices: 54.3 us -> none  [swapped(): lax.ppermute(array, axis, [(i, i ^ bit) for i in range(lax.axis_size(axis...]
    ppermute x10 -> x0, waiting for transfers between devices: 28.3 us -> none  [swapped(): lax.ppermute(array, axis, [(i, i ^ bit) for i in range(lax.axis_size(axis...]
    all_to_all x3 -> x5, waiting for transfers between devices: 83.3 us -> 101 us  [exchange(): return lax.all_to_all(array, axes, split_axis=0, concat_axis=0, tiled=True)]
    ppermute x3 -> x7, starting transfers between devices: 9.78 us -> 25.5 us  [shifted(): lax.ppermute(array, axis, [(i, (i + step) % size) for i in range(size)])]
    all_to_all x3 -> x5, starting transfers between devices: 23.6 us -> 38.3 us  [exchange(): return lax.all_to_all(array, axes, split_axis=0, concat_axis=0, tiled=True)]
    all_gather x1 -> x0, blocking collectives: 13.7 us -> none  [per_device(): whole_dense = lax.all_gather(dense_in, COL, axis=0, tiled=True)]
    ppermute x3 -> x7, waiting for transfers between devices: 0.01 us -> 11.3 us  [shifted(): lax.ppermute(array, axis, [(i, (i + step) % size) for i in range(size)])]
    all_to_all x2, blocking collectives: 59.5 us -> 54.2 us  [exchange(): return lax.all_to_all(array, axes, split_axis=0, concat_axis=0, tiled=True)]
  transfers between devices with their start and end apart: 17 -> 13, of which waited for: 11 -> 11; matrix products, arithmetic and copies ran while one was open for 1% -> 2% of each run, Pallas kernels for 2% -> 3%
where the time goes in v2:
time: 281 us; the launch traced here: 280 us
  waiting for transfers between devices  112 us (40%)
  starting transfers between devices  63.8 us (23%)
  blocking collectives  54.2 us (19%)
  Pallas kernels  27.5 us (10%)
  between operations  14.3 us (5%)
  local copies, waits for them, and re-layouts  6.4 us (2%)
    all_to_all x5, waiting for transfers between devices, exchange(): return lax.all_to_all(array, axes, split_axis=0, concat_axis=0, tiled=True)  101 us
    all_to_all x2, blocking collectives, exchange(): return lax.all_to_all(array, axes, split_axis=0, concat_axis=0, tiled=True)  54.2 us
    all_to_all x5, starting transfers between devices, exchange(): return lax.all_to_all(array, axes, split_axis=0, concat_axis=0, tiled=True)  38.3 us
    ppermute x7, starting transfers between devices, shifted(): lax.ppermute(array, axis, [(i, (i + step) % size) for i in range(size)])  25.5 us
    ppermute x7, waiting for transfers between devices, shifted(): lax.ppermute(array, axis, [(i, (i + step) % size) for i in range(size)])  11.3 us
    pallas_call x1, Pallas kernels, look_up(): call(lookup_kernel, jax.ShapeDtypeStruct((N_ROW * 2 * PEERS * CAP, D), BF...  8.37 us
    pallas_call x1, Pallas kernels, dense_step(): pl.pallas_call(dense_kernel, out_shape=(jax.ShapeDtypeStruct((N_ROW * PEE...  5.64 us
  transfers between devices with their start and end apart: 13, of which 11 were waited for; matrix products, arithmetic and copies ran while one was open for 2% of the time, Pallas kernels for 3%

profile of v2, /device:TPU:1, one launch (start us, length us, event | category | flops | bytes accessed | tf_op | source)
XLA Modules:
  0.0 279.8 jit_solution(16036472726899383923)
XLA Ops:
  7.2 4.4 %shard_map.157 = (s32[128,128]{1,0:T(8,128)}, s32[128,128]{1,0:T(8,128)}) custom-call(s32[16,128]{1,0:T(8,128)} %bitcast.67, s32[16,128]{1,0:T(8,128)} %bitcast.68, s32[2,128]{1,0:T(2,128)} %bitcast.72, s32[8,128]{1,0:T(8,128)} %bitcast.69, s32[8,128]{1,0:T(8,128)} %bitcast.70, s32[1,128]{1,0:T(1,128)} %bitcast.73), custom_call_target="tpu_custom_call" | custom-call | flops 2000000000 | bytes 200000 | tf_op jit(solution)/shard_map/pallas_call | solution.py:391
  11.6 36.2 %all_to_all.41 = s32[128,1,128]{2,1,0:T(1,128)S(1)} all-to-all(s32[128,1,128]{2,1,0:T(1,128)} %bitcast.59), channel_id=1, replica_groups=mesh['y'=4,'z'=16,'core'=2,'x'=4] {'y','core','z'}, dimensions={0} | all-to-all | bytes 131072 | tf_op jit(solution)/shard_map/all_to_all | solution.py:487
  48.6 4.0 %all-to-all-start.1 = ((s32[4,24,128]{2,1,0:T(8,128)}), s32[4,24,128]{2,1,0:T(8,128)S(1)}, u32[]{:S(2)}, u32[]{:S(2)}) async-start(s32[4,24,128]{2,1,0:T(8,128)} %slice.28), calls=%async_computation.1 | async-start | bytes 98304 | tf_op jit(solution)/shard_map/all_to_all | solution.py:487
  54.0 3.0 %all-to-all-done.1.code_ref = s32[4,24,128]{2,1,0:T(8,128)S(1)} async-done(((s32[4,24,128]{2,1,0:T(8,128)}), s32[4,24,128]{2,1,0:T(8,128)S(1)}, u32[]{:S(2)}, u32[]{:S(2)}) %all-to-all-start.1) | async-done | bytes 49184 | tf_op jit(solution)/shard_map/all_to_all | solution.py:487
  57.0 8.4 %shard_map.160 = bf16[6144,128]{1,0:T(8,128)(2,1)} custom-call(s32[4,24,128]{2,1,0:T(8,128)S(1)} %all-to-all-done.1.code_ref, bf16[512,1024]{1,0:T(8,128)(2,1)S(1)} %shard_map.158.fold_ref, bf16[512,512]{1,0:T(8,128)(2,1)S(1)} %shard_map.159.cfold_ref), custom_call_target="tpu_custom_call" | custom-call | flops 7000000000 | bytes 3200000 | tf_op jit(solution)/shard_map/pallas_call | solution.py:422
  65.4 9.9 %all-to-all-start.2 = ((bf16[512,3,4,128]{3,2,1,0:T(4,128)(2,1)}), bf16[512,3,4,128]{3,2,1,0:T(4,128)(2,1)S(1)}, u32[]{:S(2)}, u32[]{:S(2)}) async-start(bf16[512,3,4,128]{3,2,1,0:T(4,128)(2,1)} %bitcast.18), calls=%async_computation.2 | async-start | bytes 3145728 | tf_op jit(solution)/shard_map/all_to_all | solution.py:487
  76.3 78.8 %all-to-all-done.2 = bf16[512,3,4,128]{3,2,1,0:T(4,128)(2,1)S(1)} async-done(((bf16[512,3,4,128]{3,2,1,0:T(4,128)(2,1)}), bf16[512,3,4,128]{3,2,1,0:T(4,128)(2,1)S(1)}, u32[]{:S(2)}, u32[]{:S(2)}) %all-to-all-start.2) | async-done | bytes 1572896 | tf_op jit(solution)/shard_map/all_to_all | solution.py:487
  155.3 1.6 copy.26
  156.9 5.6 %shard_map.161 = (bf16[3072,128]{1,0:T(8,128)(2,1)}, bf16[128,640]{1,0:T(8,128)(2,1)}) custom-call(s32[128,128]{1,0:T(8,128)} %get-tuple-element.14.bag_ref, bf16[4,2,768,128]{3,2,1,0:T(8,128)(2,1)} %bitcast.64, bf16[128,512]{1,0:T(8,128)(2,1)} %dense_ref.1, bf16[4,320,1024]{2,1,0:T(8,128)(2,1)} %bitcast.51, f32[1,1024]{1,0:T(1,128)} %bitcast.71, ...), custom_call_target="tpu_custom_call" | custom-call | flops 2000000000 | bytes 5000000 | tf_op jit(solution)/shard_map/pallas_call | solution.py:432
  162.6 11.5 %all-to-all-start.3 = ((bf16[512,3,2,128]{3,2,1,0:T(2,128)(2,1)}), bf16[512,3,2,128]{3,2,1,0:T(2,128)(2,1)}, u32[]{:S(2)}, u32[]{:S(2)}) async-start(bf16[512,3,2,128]{3,2,1,0:T(2,128)(2,1)} %bitcast.65), calls=%async_computation.3 | async-start | bytes 1572864 | tf_op jit(solution)/shard_map/all_to_all | solution.py:487
  174.1 3.3 %collective-permute-start = (bf16[128,640]{1,0:T(8,128)(2,1)S(1)}, bf16[128,640]{1,0:T(8,128)(2,1)S(1)}, u32[]{:S(2)}, u32[]{:S(2)}) collective-permute-start(bf16[128,640]{1,0:T(8,128)(2,1)S(1)} %copy-done.5), channel_id=1, source_target_pairs={{0,1},{1,2},{2,3},{3,0},{4,5},{5,6},{6,7},{7,4},{8,9},{9,10},{10,1... | collective-permute-start | bytes 491528 | tf_op jit(solution)/shard_map/ppermute | solution.py:492
  177.4 4.3 %collective-permute-start.1 = (bf16[128,640]{1,0:T(8,128)(2,1)S(1)}, bf16[128,640]{1,0:T(8,128)(2,1)S(1)}, u32[]{:S(2)}, u32[]{:S(2)}) collective-permute-start(bf16[128,640]{1,0:T(8,128)(2,1)S(1)} %copy-done.5), channel_id=1, source_target_pairs={{0,2},{1,3},{2,0},{3,1},{4,6},{5,7},{6,4},{7,5},{8,10},{9,11},{10,... | collective-permute-start | bytes 491528 | tf_op jit(solution)/shard_map/ppermute | solution.py:492
  181.7 3.1 %collective-permute-start.2 = (bf16[128,640]{1,0:T(8,128)(2,1)S(1)}, bf16[128,640]{1,0:T(8,128)(2,1)S(1)}, u32[]{:S(2)}, u32[]{:S(2)}) collective-permute-start(bf16[128,640]{1,0:T(8,128)(2,1)S(1)} %copy-done.5), channel_id=1, source_target_pairs={{0,3},{1,0},{2,1},{3,2},{4,7},{5,4},{6,5},{7,6},{8,11},{9,8},{10,9... | collective-permute-start | bytes 491528 | tf_op jit(solution)/shard_map/ppermute | solution.py:492
  184.9 3.9 %collective-permute-done.1.s2 = bf16[128,640]{1,0:T(8,128)(2,1)S(1)} collective-permute-done((bf16[128,640]{1,0:T(8,128)(2,1)S(1)}, bf16[128,640]{1,0:T(8,128)(2,1)S(1)}, u32[]{:S(2)}, u32[]{:S(2)}) %collective-permute-start.1) | collective-permute-done | bytes 163872 | tf_op jit(solution)/shard_map/ppermute | solution.py:492
  188.8 1.0 collective-permute-done.2.s3
  189.8 2.1 shard_map.162
  192.0 5.8 %collective-permute-start.3 = (f32[4,16,8,256]{3,2,1,0:T(8,128)S(1)}, f32[4,16,8,256]{3,2,1,0:T(8,128)S(1)}, u32[]{:S(2)}, u32[]{:S(2)}) collective-permute-start(f32[4,16,8,256]{3,2,1,0:T(8,128)S(1)} %get-tuple-element.17), channel_id=1, source_target_pairs={{0,4},{4,0},{1,5},{5,1},{2,6},{6,2},{3,7},{7,3},{8,12},{12,8},{9,1... | collective-permute-start | bytes 1572872 | tf_op jit(solution)/shard_map/ppermute | solution.py:492
  197.7 1.5 collective-permute-done.3
  199.3 1.9 collective-permute-start.4
  201.3 4.1 %collective-permute-start.5 = (f32[16,8,256]{2,1,0:T(8,128)S(1)}, f32[16,8,256]{2,1,0:T(8,128)S(1)}, u32[]{:S(2)}, u32[]{:S(2)}) collective-permute-start(f32[16,8,256]{2,1,0:T(8,128)S(1)} %get-tuple-element.25), channel_id=1, source_target_pairs={{0,256},{128,384},{256,0},{384,128},{1,257},{129,385},{257,1},{385... | collective-permute-start | bytes 393224 | tf_op jit(solution)/shard_map/ppermute | solution.py:492
  205.3 3.0 %collective-permute-start.6 = (f32[16,8,256]{2,1,0:T(8,128)S(1)}, f32[16,8,256]{2,1,0:T(8,128)S(1)}, u32[]{:S(2)}, u32[]{:S(2)}) collective-permute-start(f32[16,8,256]{2,1,0:T(8,128)S(1)} %get-tuple-element.24), channel_id=1, source_target_pairs={{0,384},{128,0},{256,128},{384,256},{1,385},{129,1},{257,129},{385... | collective-permute-start | bytes 393224 | tf_op jit(solution)/shard_map/ppermute | solution.py:492
  208.9 2.3 collective-permute-done.5
  211.2 2.1 collective-permute-done.6
  213.3 5.2 %all-to-all-done.3 = bf16[512,3,2,128]{3,2,1,0:T(2,128)(2,1)} async-done(((bf16[512,3,2,128]{3,2,1,0:T(2,128)(2,1)}), bf16[512,3,2,128]{3,2,1,0:T(2,128)(2,1)}, u32[]{:S(2)}, u32[]{:S(2)}) %all-to-all-start.3) | async-done | bytes 786464 | tf_op jit(solution)/shard_map/all_to_all | solution.py:487
  218.5 18.0 %all_to_all.42 = f32[16,8,256]{2,1,0:T(8,128)S(1)} all-to-all(f32[16,8,256]{2,1,0:T(8,128)S(1)} %fusion.2), channel_id=1, replica_groups=mesh['y'=4,'z'=16,'core'=2,'x'=4] {'z'}, dimensions={0} | all-to-all | bytes 262144 | tf_op jit(solution)/shard_map/all_to_all | solution.py:487
  237.1 4.0 %all-to-all-start.5 = ((bf16[16,8,256]{2,1,0:T(8,128)(2,1)}), bf16[16,8,256]{2,1,0:T(8,128)(2,1)S(1)}, u32[]{:S(2)}, u32[]{:S(2)}) async-start(bf16[16,8,256]{2,1,0:T(8,128)(2,1)} %broadcast_in_dim.28), calls=%async_computation.5 | async-start | bytes 131072 | tf_op jit(solution)/shard_map/all_to_all | solution.py:487
  241.1 1.2 copy.27
  242.6 10.1 %all-to-all-done.5 = bf16[16,8,256]{2,1,0:T(8,128)(2,1)S(1)} async-done(((bf16[16,8,256]{2,1,0:T(8,128)(2,1)}), bf16[16,8,256]{2,1,0:T(8,128)(2,1)S(1)}, u32[]{:S(2)}, u32[]{:S(2)}) %all-to-all-start.5) | async-done | bytes 65568 | tf_op jit(solution)/shard_map/all_to_all | solution.py:487
  253.5 8.9 %all-to-all-start.6 = ((bf16[8,16,8,256]{3,2,1,0:T(8,128)(2,1)}), bf16[8,16,8,256]{3,2,1,0:T(8,128)(2,1)S(1)}, u32[]{:S(2)}, u32[]{:S(2)}) async-start(bf16[8,16,8,256]{3,2,1,0:T(8,128)(2,1)} %broadcast_in_dim.29), calls=%async_computation.6 | async-start | bytes 1048576 | tf_op jit(solution)/shard_map/all_to_all | solution.py:487
  262.5 5.5 %shard_map.163 = (bf16[4096,128]{1,0:T(8,128)(2,1)}, f32[2,2048]{1,0:T(2,128)}) custom-call(s32[4,24,128]{2,1,0:T(8,128)S(1)} %all-to-all-done.1.code_ref, bf16[4,768,128]{2,1,0:T(8,128)(2,1)S(1)} %bitcast.55, bf16[4096,128]{1,0:T(8,128)(2,1)S(1)} %bitcast.54, f32[2,2048]{1,0:T(2,128)S(1)} %copy-done.7), custom_call_target="tpu_custom_call" | custom-call | flops 7000000000 | bytes 3000000 | tf_op jit(solution)/shard_map/pallas_call | solution.py:474
  267.9 4.0 %all-to-all-done.6.parts_ref = bf16[8,16,8,256]{3,2,1,0:T(8,128)(2,1)S(1)} async-done(((bf16[8,16,8,256]{3,2,1,0:T(8,128)(2,1)}), bf16[8,16,8,256]{3,2,1,0:T(8,128)(2,1)S(1)}, u32[]{:S(2)}, u32[]{:S(2)}) %all-to-all-start.6) | async-done | bytes 524320 | tf_op jit(solution)/shard_map/all_to_all | solution.py:487
  271.9 1.0 shard_map.164
  (40 shorter events, 5.7 us)
Async XLA Ops:
  7.2 45.5 %copy-start.3 = (bf16[4096,64]{0,1:T(8,128)(2,1)S(1)}, bf16[4096,64]{0,1:T(8,128)(2,1)}, u32[]{:S(2)}) copy-start(bf16[4096,64]{0,1:T(8,128)(2,1)} %param.16) | copy-start | bytes 1572868
  11.6 42.1 %copy-start.1 = (bf16[2,2048,128]{2,1,0:T(8,128)(2,1)S(1)}, bf16[2,2048,128]{2,1,0:T(8,128)(2,1)}, u32[]{:S(2)}) copy-start(bf16[2,2048,128]{2,1,0:T(8,128)(2,1)} %param.14) | copy-start | bytes 3145732
  48.6 8.4 %all-to-all-start.1 = ((s32[4,24,128]{2,1,0:T(8,128)}), s32[4,24,128]{2,1,0:T(8,128)S(1)}, u32[]{:S(2)}, u32[]{:S(2)}) async-start(s32[4,24,128]{2,1,0:T(8,128)} %slice.28), calls=%async_computation.1 | async-start | bytes 98304 | tf_op jit(solution)/shard_map/all_to_all | solution.py:487
  52.6 0.8 copy-start.4
  65.4 9.9 %copy-start.9 = (bf16[128,512]{1,0:T(8,128)(2,1)S(1)}, bf16[128,512]{1,0:T(8,128)(2,1)}, u32[]{:S(2)}) copy-start(bf16[128,512]{1,0:T(8,128)(2,1)} %dense_ref.1) | copy-start | bytes 393220
  65.4 10.0 %copy-start.8 = (bf16[256,1024]{1,0:T(8,128)(2,1)S(1)}, bf16[256,1024]{1,0:T(8,128)(2,1)}, u32[]{:S(2)}) copy-start(bf16[256,1024]{1,0:T(8,128)(2,1)} %param.24) | copy-start | bytes 1572868
  65.4 89.7 %all-to-all-start.2 = ((bf16[512,3,4,128]{3,2,1,0:T(4,128)(2,1)}), bf16[512,3,4,128]{3,2,1,0:T(4,128)(2,1)S(1)}, u32[]{:S(2)}, u32[]{:S(2)}) async-start(bf16[512,3,4,128]{3,2,1,0:T(4,128)(2,1)} %bitcast.18), calls=%async_computation.2 | async-start | bytes 3145728 | tf_op jit(solution)/shard_map/all_to_all | solution.py:487
  75.3 81.6 %all-gather.3.cloned.1.call-start = ((), (), s32[]{:S(2)}) async-start(), calls=%async_computation.7 | async-start | bytes 3276800 | tf_op jit(solution)/shard_map/all_gather | solution.py:530
  156.9 32.9 %copy-start = (bf16[1280,1024]{1,0:T(8,128)(2,1)S(1)}, bf16[1280,1024]{1,0:T(8,128)(2,1)}, u32[]{:S(2)}) copy-start(bf16[1280,1024]{1,0:T(8,128)(2,1)} %all-gather.3.cloned.1.call-done) | copy-start | bytes 7864324
  162.6 11.5 %copy-start.5 = (bf16[128,640]{1,0:T(8,128)(2,1)S(1)}, bf16[128,640]{1,0:T(8,128)(2,1)}, u32[]{:S(2)}) copy-start(bf16[128,640]{1,0:T(8,128)(2,1)} %get-tuple-element.15.s0) | copy-start | bytes 491524
  162.6 27.2 %copy-start.6 = (f32[1024]{0:T(1024)S(1)}, f32[1024]{0:T(1024)}, u32[]{:S(2)}) copy-start(f32[1024]{0:T(1024)} %param.26) | copy-start | bytes 12292
  162.6 55.9 %all-to-all-start.3 = ((bf16[512,3,2,128]{3,2,1,0:T(2,128)(2,1)}), bf16[512,3,2,128]{3,2,1,0:T(2,128)(2,1)}, u32[]{:S(2)}, u32[]{:S(2)}) async-start(bf16[512,3,2,128]{3,2,1,0:T(2,128)(2,1)} %bitcast.65), calls=%async_computation.3 | async-start | bytes 1572864 | tf_op jit(solution)/shard_map/all_to_all | solution.py:487
  174.1 10.8 %collective-permute-start = (bf16[128,640]{1,0:T(8,128)(2,1)S(1)}, bf16[128,640]{1,0:T(8,128)(2,1)S(1)}, u32[]{:S(2)}, u32[]{:S(2)}) collective-permute-start(bf16[128,640]{1,0:T(8,128)(2,1)S(1)} %copy-done.5), channel_id=1, source_target_pairs={{0,1},{1,2},{2,3},{3,0},{4,5},{5,6},{6,7},{7,4},{8,9},{9,10},{10,1... | collective-permute-start | bytes 491528 | tf_op jit(solution)/shard_map/ppermute | solution.py:492
  177.4 11.4 %collective-permute-start.1 = (bf16[128,640]{1,0:T(8,128)(2,1)S(1)}, bf16[128,640]{1,0:T(8,128)(2,1)S(1)}, u32[]{:S(2)}, u32[]{:S(2)}) collective-permute-start(bf16[128,640]{1,0:T(8,128)(2,1)S(1)} %copy-done.5), channel_id=1, source_target_pairs={{0,2},{1,3},{2,0},{3,1},{4,6},{5,7},{6,4},{7,5},{8,10},{9,11},{10,... | collective-permute-start | bytes 491528 | tf_op jit(solution)/shard_map/ppermute | solution.py:492
  181.7 8.1 %collective-permute-start.2 = (bf16[128,640]{1,0:T(8,128)(2,1)S(1)}, bf16[128,640]{1,0:T(8,128)(2,1)S(1)}, u32[]{:S(2)}, u32[]{:S(2)}) collective-permute-start(bf16[128,640]{1,0:T(8,128)(2,1)S(1)} %copy-done.5), channel_id=1, source_target_pairs={{0,3},{1,0},{2,1},{3,2},{4,7},{5,4},{6,5},{7,6},{8,11},{9,8},{10,9... | collective-permute-start | bytes 491528 | tf_op jit(solution)/shard_map/ppermute | solution.py:492
  192.0 7.3 %collective-permute-start.3 = (f32[4,16,8,256]{3,2,1,0:T(8,128)S(1)}, f32[4,16,8,256]{3,2,1,0:T(8,128)S(1)}, u32[]{:S(2)}, u32[]{:S(2)}) collective-permute-start(f32[4,16,8,256]{3,2,1,0:T(8,128)S(1)} %get-tuple-element.17), channel_id=1, source_target_pairs={{0,4},{4,0},{1,5},{5,1},{2,6},{6,2},{3,7},{7,3},{8,12},{12,8},{9,1... | collective-permute-start | bytes 1572872 | tf_op jit(solution)/shard_map/ppermute | solution.py:492
  199.3 9.6 %collective-permute-start.4 = (f32[16,8,256]{2,1,0:T(8,128)S(1)}, f32[16,8,256]{2,1,0:T(8,128)S(1)}, u32[]{:S(2)}, u32[]{:S(2)}) collective-permute-start(f32[16,8,256]{2,1,0:T(8,128)S(1)} %get-tuple-element.23), channel_id=1, source_target_pairs={{0,128},{128,256},{256,384},{384,0},{1,129},{129,257},{257,385},{3... | collective-permute-start | bytes 393224 | tf_op jit(solution)/shard_map/ppermute | solution.py:492
  201.3 9.9 %collective-permute-start.5 = (f32[16,8,256]{2,1,0:T(8,128)S(1)}, f32[16,8,256]{2,1,0:T(8,128)S(1)}, u32[]{:S(2)}, u32[]{:S(2)}) collective-permute-start(f32[16,8,256]{2,1,0:T(8,128)S(1)} %get-tuple-element.25), channel_id=1, source_target_pairs={{0,256},{128,384},{256,0},{384,128},{1,257},{129,385},{257,1},{385... | collective-permute-start | bytes 393224 | tf_op jit(solution)/shard_map/ppermute | solution.py:492
  205.3 7.9 %collective-permute-start.6 = (f32[16,8,256]{2,1,0:T(8,128)S(1)}, f32[16,8,256]{2,1,0:T(8,128)S(1)}, u32[]{:S(2)}, u32[]{:S(2)}) collective-permute-start(f32[16,8,256]{2,1,0:T(8,128)S(1)} %get-tuple-element.24), channel_id=1, source_target_pairs={{0,384},{128,0},{256,128},{384,256},{1,385},{129,1},{257,129},{385... | collective-permute-start | bytes 393224 | tf_op jit(solution)/shard_map/ppermute | solution.py:492
  237.1 15.6 %all-to-all-start.5 = ((bf16[16,8,256]{2,1,0:T(8,128)(2,1)}), bf16[16,8,256]{2,1,0:T(8,128)(2,1)S(1)}, u32[]{:S(2)}, u32[]{:S(2)}) async-start(bf16[16,8,256]{2,1,0:T(8,128)(2,1)} %broadcast_in_dim.28), calls=%async_computation.5 | async-start | bytes 131072 | tf_op jit(solution)/shard_map/all_to_all | solution.py:487
  242.4 20.1 %copy-start.2 = (bf16[2,2048,128]{2,1,0:T(8,128)(2,1)S(1)}, bf16[2,2048,128]{2,1,0:T(8,128)(2,1)}, u32[]{:S(2)}) copy-start(bf16[2,2048,128]{2,1,0:T(8,128)(2,1)} %param.14) | copy-start | bytes 3145732
  242.4 20.1 %copy-start.7 = (f32[2,2048]{1,0:T(2,128)S(1)}, f32[2,2048]{1,0:T(2,128)}, u32[]{:S(2)}) copy-start(f32[2,2048]{1,0:T(2,128)} %accum_ref.1) | copy-start | bytes 49156
  253.5 18.4 %all-to-all-start.6 = ((bf16[8,16,8,256]{3,2,1,0:T(8,128)(2,1)}), bf16[8,16,8,256]{3,2,1,0:T(8,128)(2,1)S(1)}, u32[]{:S(2)}, u32[]{:S(2)}) async-start(bf16[8,16,8,256]{3,2,1,0:T(8,128)(2,1)} %broadcast_in_dim.29), calls=%async_computation.6 | async-start | bytes 1048576 | tf_op jit(solution)/shard_map/all_to_all | solution.py:487
Sparse Core Ops, SparseCore 0:
  78.8 52.3 all-gather.2

commit v3 on v2

--- a/solution.py
+++ b/solution.py
@@ -7,8 +7,6 @@
 
 ROW = ("y", "z", "core")
 COL = "x"
-LINE = ("y", "core", "z")
-NEAR_Z = ("y", "core", "x", "z")
 ALL = ROW + (COL,)
 Y, Z, CORES, PEERS = 4, 16, 2, 4
 N_ROW = Y * Z * CORES
@@ -26,13 +24,13 @@
 DENSE = 512
 SHARE = 2 * POOL + LANES
 BLOCK = LANES // PEERS
-KEEP = 24
+STEPS = 3 * L
 FOLD = 8
 GROUP = 16
 PART_ROWS, PART_COLS = 8, X // 4
 VMEM = 40 * 1024 * 1024
 MOST_VMEM = 60 * 1024 * 1024
-DENSE_VMEM = 58 * 1024 * 1024
+DENSE_VMEM = 57 * 1024 * 1024
 
 F32 = jnp.float32
 BF16 = jnp.bfloat16
@@ -82,9 +80,9 @@
 
 def index_kernel(
     owner_in, local_in, length_in, cowner_in, clocal_in, clength_in,
-    request_ref, bag_ref,
+    request_ref, place_ref,
     owner_ref, local_ref, length_ref, cowner_ref, clocal_ref, clength_ref,
-    own_s, high_s, low_s, bag_s, sems,
+    own_s, high_s, low_s, sems,
 ):
     moves = (
         (owner_in, owner_ref), (local_in, local_ref), (length_in, length_ref),
@@ -102,16 +100,18 @@
         ],
         axis=1,
     ).astype(BF16)
-    sample = iota((1, B), 1)
     rows128 = iota((LANES, LANES), 0)
-
-    def put(step, row, spot, code, bag):
-        row = jnp.where(row < 0, -1, (row & 96) | ((row & 1) << 4) | ((row >> 1) & 15))
+    half128 = half_iota((LANES, LANES), 0)
+    half32 = (rows128 & (BLOCK - 1)).astype(F32).astype(BF16)
+
+    def put(step, row, place, spot, code):
+        place_ref[step : step + 1, :] = place
+        place_ref[STEPS + step : STEPS + step + 1, :] = row
         at = slice(step * LANES, (step + 1) * LANES)
-        own_s[:, at] = (rows128 == row).astype(F32).astype(BF16)
-        high_s[:, at] = jnp.where(spot, code >> 6, 0).astype(F32).astype(BF16)
-        low_s[:, at] = jnp.where(spot, code & 63, 0).astype(F32).astype(BF16)
-        bag_s[:, at] = jnp.where(spot, bag, 0).astype(F32).astype(BF16)
+        none = jnp.zeros((), BF16)
+        own_s[:, at] = ones_where(half128 == to_half(row))
+        high_s[:, at] = jnp.where(spot, to_half(code >> 6), none)
+        low_s[:, at] = jnp.where(spot, to_half(code & 63), none)
 
     carry = jnp.zeros((OWNERS, LANES), F32)
     rows512 = iota((OWNERS, LANES), 0)
@@ -123,7 +123,7 @@
         rank, carry = ranks(mask.astype(F32).astype(BF16), mask, carry, ahead)
         place = jnp.where(live, (owner & (PEERS - 1)) * BLOCK + rank, -1)
         code = local_ref[slot : slot + 1, :] + (table * 2048 + 1)
-        put(slot, owner >> 2, rows128 == place, code, sample + (table * B + 1))
+        put(slot, owner >> 2, place, half128 == to_half(place), code)
     carry = jnp.zeros((N_ROW, LANES), F32)
     for slot in range(L):
         live = slot < clength_ref[...]
@@ -131,24 +131,31 @@
         mask = rows128 == owner
         rank, carry = ranks(mask.astype(F32).astype(BF16), mask, carry, ahead)
         place = jnp.where(live, rank + CAP, -1)
-        spot = (rows128 & (BLOCK - 1)) == place
-        put(2 * L + slot, owner, spot, clocal_ref[slot : slot + 1, :] + 1, sample + 1)
+        code = clocal_ref[slot : slot + 1, :] + 1
+        put(2 * L + slot, owner, place, half32 == to_half(place), code)
     own = own_s[...]
     high = dot(own, high_s[...], NT)
     low = dot(own, low_s[...], NT)
     request_ref[...] = (high * 64.0 + low).astype(I32)
-    bag_ref[...] = dot(bag_s[...], own, NT).astype(I32)
+
+
+def bag_kernel(place_ref, bag_ref, own_s, bag_s):
+    sample = iota((1, B), 1) + 1
+    half128 = half_iota((LANES, LANES), 0)
+    half32 = (iota((LANES, LANES), 0) & (BLOCK - 1)).astype(F32).astype(BF16)
+    for step in range(STEPS):
+        place = to_half(place_ref[step : step + 1, :])
+        row = to_half(place_ref[STEPS + step : STEPS + step + 1, :])
+        spot = (half128 if step < 2 * L else half32) == place
+        bag = to_half(sample + B if L <= step < 2 * L else sample)
+        at = slice(step * LANES, (step + 1) * LANES)
+        own_s[:, at] = ones_where(half128 == row)
+        bag_s[:, at] = jnp.where(spot, bag, jnp.zeros((), BF16))
+    bag_ref[...] = dot(bag_s[...], own_s[...], NT).astype(I32)
 
 
 def columns(codes, first):
     return jnp.concatenate([codes[:, r : r + 1] for r in range(first, first + GROUP)], axis=0)
-
-
-def peer_major():
-    for c in range(PEERS):
-        for r in range(GROUP):
-            first = (r * PEERS + c) * CAP
-            yield slice(first, first + CAP)
 
 
 def fold_cols_kernel(after_ref, col_ref, out_ref):
@@ -201,19 +208,25 @@
             halves.append(jnp.where((part & 1) == i, got, turned))
         cols = jnp.where(left, halves[0], halves[1])
         parts = []
-        for at in peer_major():
-            parts.append(rows[at])
-            parts.append(cols[at])
+        for at in range(0, size, CAP):
+            parts.append(rows[at : at + CAP])
+            parts.append(cols[at : at + CAP])
         out_ref[first * 2 * wide : (first + GROUP) * 2 * wide, :] = jnp.concatenate(
             parts, axis=0
         ).astype(BF16)
 
 
 def dense_kernel(
-    bag_ref, reply_ref, dense_ref, weight_in, bias_ref, head_ref, label_ref,
-    grads_ref, share_ref, weight_ref, sems,
+    bag_ref, reply_in, dense_ref, weight_in, bias_ref, head_ref, label_ref,
+    grads_ref, share_ref, weight_ref, reply_ref, sems, reply_sems,
 ):
     wide = X // PEERS
+    replies = [
+        pltpu.make_async_copy(reply_in.at[c], reply_ref.at[c], reply_sems.at[c])
+        for c in range(PEERS)
+    ]
+    for reply in replies:
+        reply.start()
     fetches = [
         pltpu.make_async_copy(
             weight_in.at[c, pl.ds(0, wide)], weight_ref.at[pl.ds(c * wide, wide)], sems.at[c]
@@ -225,15 +238,17 @@
     span = CAP * N_ROW
 
     def lanes_of(first):
-        return jnp.concatenate([bag_ref[first + k : first + k + 1, :] for k in range(CAP)], axis=1)
-
+        return to_half(
+            jnp.concatenate([bag_ref[first + k : first + k + 1, :] for k in range(CAP)], axis=1)
+        )
+
+    bag_rows = half_iota((2 * B, span), 0, -1)
     pooled = jnp.zeros((2 * B, D), F32)
     for c in range(PEERS):
-        picks = iota((2 * B, span), 0) + 1 == lanes_of(c * BLOCK)
-        pooled += dot(picks.astype(F32).astype(BF16), reply_ref[c, 0])
+        replies[c].wait()
+        pooled += dot(ones_where(bag_rows == lanes_of(c * BLOCK)), reply_ref[c, 0])
     halves = [
-        (iota((B, span), 0) + 1 == lanes_of((i + 1) * CAP)).astype(F32).astype(BF16)
-        for i in range(2)
+        ones_where(bag_rows[:B] == lanes_of((i + 1) * CAP)) for i in range(2)
     ]
     wide_cols = []
     for c in range(PEERS):
@@ -270,12 +285,12 @@
     )
     size = GROUP * PEERS * CAP
     for first in range(0, N_ROW, GROUP):
-        picks = columns(places, first) == iota((size, 2 * B), 1) + 1
+        bag = to_half(jnp.broadcast_to(columns(places, first), (size, LANES)))
+        picks = jnp.concatenate(
+            [ones_where(bag == half_iota((size, LANES), 1, -1 - t * B)) for t in range(2)], axis=1
+        )
         at = slice(first * PEERS * CAP, (first + GROUP) * PEERS * CAP)
-        spread = dot(picks.astype(F32).astype(BF16), bags)
-        grads_ref[at, :] = jnp.concatenate([spread[one] for one in peer_major()], axis=0).astype(
-            BF16
-        )
+        grads_ref[at, :] = dot(picks, bags).astype(BF16)
     share_ref[:, : 2 * POOL] = cross_in[:, : 2 * POOL]
     high = grad_logit.astype(BF16)
     rest = grad_logit - high.astype(F32)
@@ -339,11 +354,12 @@
                 (near_ref, far_ref)[far_core][far_y, z] = sum_s[at]
 
 
-def place_kernel(parts_ref, out_ref):
-    for y in range(Y):
+def place_kernel(place_ref, y0, y1, y2, y3, out_ref):
+    for step, part in enumerate((y0, y1, y2, y3)):
         for core in range(CORES):
-            for z, (rows, cols) in enumerate(blocks_of(core, y)):
-                out_ref[rows, cols] = parts_ref[y * CORES + core, z].astype(F32)
+            parts = blocks_of(core, (place_ref[2] + Y - step) & (Y - 1))
+            for z, (rows, cols) in enumerate(parts):
+                out_ref[rows, cols] = part[z * CORES + core].astype(F32)
 
 
 def update_kernel(code_ref, grad_ref, table_ref, accum_ref, table_out, accum_out, sum_s):
@@ -385,18 +401,29 @@
         ).astype(BF16)
 
 
+def build_bags(places):
+    pairs = STEPS * LANES
+    return call(
+        bag_kernel,
+        jax.ShapeDtypeStruct((LANES, N_ROW), I32),
+        [pltpu.VMEM((LANES, pairs), BF16) for _ in range(2)],
+        flops=10**9,
+        bytes_accessed=1_000_000,
+    )(places)
+
+
 def build_index(owner, local, length, cowner, clocal, clength):
-    pairs = 3 * L * LANES
+    pairs = STEPS * LANES
     arrays = (owner, local, length, cowner, clocal, clength)
     return pl.pallas_call(
         index_kernel,
         out_shape=(
             jax.ShapeDtypeStruct((N_ROW, LANES), I32),
-            jax.ShapeDtypeStruct((LANES, N_ROW), I32),
+            jax.ShapeDtypeStruct((2 * STEPS, LANES), I32),
         ),
         in_specs=[pl.BlockSpec(memory_space=pltpu.HBM)] * len(arrays),
         scratch_shapes=[pltpu.VMEM(array.shape, I32) for array in arrays]
-        + [pltpu.VMEM((LANES, pairs), BF16) for _ in range(4)]
+        + [pltpu.VMEM((LANES, pairs), BF16) for _ in range(3)]
         + [pltpu.SemaphoreType.DMA((len(arrays),))],
         compiler_params=pltpu.CompilerParams(vmem_limit_bytes=MOST_VMEM),
         cost_estimate=pl.CostEstimate(
@@ -429,14 +456,20 @@
 
 def dense_step(bags, replies, dense_in, weight, bias, head, labels):
     vmem = pl.BlockSpec(memory_space=pltpu.VMEM)
+    hbm = pl.BlockSpec(memory_space=pltpu.HBM)
     return pl.pallas_call(
         dense_kernel,
         out_shape=(
             jax.ShapeDtypeStruct((N_ROW * PEERS * CAP, D), BF16),
             jax.ShapeDtypeStruct((B, SHARE), BF16),
         ),
-        in_specs=[vmem] * 3 + [pl.BlockSpec(memory_space=pltpu.HBM)] + [vmem] * 3,
-        scratch_shapes=[pltpu.VMEM((X, X), BF16), pltpu.SemaphoreType.DMA((PEERS,))],
+        in_specs=[vmem, hbm, vmem, hbm, vmem, vmem, vmem],
+        scratch_shapes=[
+            pltpu.VMEM((X, X), BF16),
+            pltpu.VMEM(replies.shape, BF16),
+            pltpu.SemaphoreType.DMA((PEERS,)),
+            pltpu.SemaphoreType.DMA((PEERS,)),
+        ],
         compiler_params=pltpu.CompilerParams(vmem_limit_bytes=DENSE_VMEM),
         cost_estimate=pl.CostEstimate(
             flops=2 * 10**9, bytes_accessed=5_000_000, transcendentals=0
@@ -465,8 +498,15 @@
     )(place, *shares, joined, head)
 
 
-def put_in_place(parts):
-    return call(place_kernel, jax.ShapeDtypeStruct((X // PEERS, X), F32))(parts)
+def put_in_place(place, parts):
+    return pl.pallas_call(
+        place_kernel,
+        out_shape=jax.ShapeDtypeStruct((X // PEERS, X), F32),
+        in_specs=[pl.BlockSpec(memory_space=pltpu.SMEM)]
+        + [pl.BlockSpec(memory_space=pltpu.VMEM)] * len(parts),
+        compiler_params=pltpu.CompilerParams(vmem_limit_bytes=VMEM),
+        cost_estimate=pl.CostEstimate(flops=0, bytes_accessed=0, transcendentals=0),
+    )(place, *parts)
 
 
 def update(codes, grads, table, accum):
@@ -492,21 +532,20 @@
     return lax.ppermute(array, axis, [(i, (i + step) % size) for i in range(size)])
 
 
-def sum_over_rows(near, far, after):
+def sum_over_rows(place, near, far, after):
     total = near + shifted(far, "core", 1)
     own = total[0]
     for step in range(1, Y):
         own = own + shifted(total[step], "y", step)
     own, after = lax.optimization_barrier((own, after))
     own = jnp.sum(exchange(own, "z"), axis=0).astype(BF16)
-    own = exchange(jnp.broadcast_to(own[None], (Z, *own.shape)), "z")
-    parts = exchange(jnp.broadcast_to(own[None], (Y * CORES, *own.shape)), ("y", "core"))
-    return put_in_place(parts), after
+    own = exchange(jnp.broadcast_to(own[None], (Z * CORES, *own.shape)), ("z", "core"))
+    parts = [own] + [shifted(own, "y", step) for step in range(1, Y)]
+    return put_in_place(place, parts), after
 
 
 def by_peer(array, rows):
-    array = array.reshape(Y * CORES, PEERS, Z, rows, D).transpose(1, 3, 0, 2, 4)
-    return array.reshape(PEERS, rows, N_ROW, D)
+    return array.reshape(N_ROW, PEERS, rows, D).transpose(1, 2, 0, 3)
 
 
 def per_device(
@@ -529,7 +568,7 @@
     joined = jnp.concatenate([cross_weight, packed], axis=0)
     joined = lax.all_gather(joined, COL, axis=0)
     head = head_weight[None, :]
-    requests, bags = build_index(
+    requests, places = build_index(
         row_owner[:, :, 0].T,
         row_local.T,
         row_lengths.T,
@@ -537,13 +576,15 @@
         col_local.T,
         col_lengths[None, :],
     )
-    arrived = exchange(requests, LINE)
+    arrived = exchange(requests, ROW)
+    bags = build_bags(places)
     cfold = fold_after(fold_cols_kernel, requests, col_table.T, FOLD * SLICE)
-    codes = exchange(arrived.T.reshape(PEERS, BLOCK, N_ROW)[:, :KEEP], COL)
+    arrived, bags, cfold = lax.optimization_barrier((arrived, bags, cfold))
+    codes = exchange(arrived.T.reshape(PEERS, BLOCK, N_ROW), COL)
     flat_table = row_tables.reshape(-1, D)
     fold = fold_after(fold_rows_kernel, arrived, flat_table, FOLD * D)
     replies = look_up(codes, fold, cfold)
-    replies = by_peer(exchange(replies.reshape(OWNERS, 3, 4, D), NEAR_Z), 2 * CAP)
+    replies = by_peer(exchange(replies.reshape(OWNERS, 3, 4, D), ALL), 2 * CAP)
     grads, share = dense_step(
         bags,
         replies.reshape(PEERS, 2, CAP * N_ROW, D),
@@ -555,9 +596,9 @@
     )
     shares = [share] + [shifted(share, COL, step) for step in range(1, PEERS)]
     place = jnp.stack([lax.axis_index(axis) for axis in (COL, "core", "y")]).astype(I32)
-    grads = exchange(grads.reshape(OWNERS, 3, 2, D), NEAR_Z)
+    grads = exchange(grads.reshape(OWNERS, 3, 2, D), ALL)
     near, far = weight_part(place, shares, joined, head)
-    weight_grad, grads = sum_over_rows(near, far, grads)
+    weight_grad, grads = sum_over_rows(place, near, far, grads)
     grads = by_peer(grads, CAP).reshape(PEERS, CAP * N_ROW, D)
     new_tables, new_accum = update(codes, grads, flat_table, row_accum)
     return (new_tables.reshape(row_tables.shape), new_accum, weight_grad)

time: 281 us -> 288 us (1.025)
  blocking collectives: 54.2 us -> 16.9 us
  starting transfers between devices: 63.8 us -> 90.3 us
  waiting for transfers between devices: 112 us -> 127 us
    all_to_all x2 -> x1, blocking collectives: 54.2 us -> 16.9 us  [exchange(): return lax.all_to_all(array, axes, split_axis=0, concat_axis=0, tiled=True)]
    all_to_all x5, starting transfers between devices: 38.3 us -> 54.3 us  [exchange(): return lax.all_to_all(array, axes, split_axis=0, concat_axis=0, tiled=True)]
    all_to_all x5, waiting for transfers between devices: 101 us -> 116 us  [exchange(): return lax.all_to_all(array, axes, split_axis=0, concat_axis=0, tiled=True)]
    ppermute x7 -> x10, starting transfers between devices: 25.5 us -> 35.8 us  [shifted(): lax.ppermute(array, axis, [(i, (i + step) % size) for i in range(size)])]
    ppermute x7 -> x10, waiting for transfers between devices: 11.3 us -> 11.2 us  [shifted(): lax.ppermute(array, axis, [(i, (i + step) % size) for i in range(size)])]
  transfers between devices with their start and end apart: 13 -> 16, of which waited for: 11 -> 10; matrix products, arithmetic and copies ran while one was open for 2% -> 2% of each run, Pallas kernels for 3% -> 3%
where the time goes in v3:
time: 288 us; the launch traced here: 286 us
  waiting for transfers between devices  127 us (44%)
  starting transfers between devices  90.3 us (31%)
  Pallas kernels  28.7 us (10%)
  blocking collectives  16.9 us (6%)
  between operations  14.4 us (5%)
  local copies, waits for them, and re-layouts  6.98 us (2%)
    all_to_all x5, waiting for transfers between devices, exchange(): return lax.all_to_all(array, axes, split_axis=0, concat_axis=0, tiled=True)  116 us
    all_to_all x5, starting transfers between devices, exchange(): return lax.all_to_all(array, axes, split_axis=0, concat_axis=0, tiled=True)  54.3 us
    ppermute x10, starting transfers between devices, shifted(): lax.ppermute(array, axis, [(i, (i + step) % size) for i in range(size)])  35.8 us
    all_to_all x1, blocking collectives, exchange(): return lax.all_to_all(array, axes, split_axis=0, concat_axis=0, tiled=True)  16.9 us
    ppermute x10, waiting for transfers between devices, shifted(): lax.ppermute(array, axis, [(i, (i + step) % size) for i in range(size)])  11.2 us
    pallas_call x1, Pallas kernels, look_up(): call(lookup_kernel, jax.ShapeDtypeStruct((N_ROW * 2 * PEERS * CAP, D), BF...  8.4 us
    pallas_call x1, Pallas kernels, dense_step(): pl.pallas_call(dense_kernel, out_shape=(jax.ShapeDtypeStruct((N_ROW * PEE...  6.41 us
  transfers between devices with their start and end apart: 16, of which 10 were waited for; matrix products, arithmetic and copies ran while one was open for 2% of the time, Pallas kernels for 3%

profile of v3, /device:TPU:1, one launch (start us, length us, event | category | flops | bytes accessed | tf_op | source)
XLA Modules:
  0.0 285.7 jit_solution(17177206903285440157)
XLA Ops:
  7.2 3.6 %shard_map.157 = (s32[128,128]{1,0:T(8,128)}, s32[48,128]{1,0:T(8,128)}) custom-call(s32[16,128]{1,0:T(8,128)} %bitcast.65, s32[16,128]{1,0:T(8,128)} %bitcast.66, s32[2,128]{1,0:T(2,128)} %bitcast.70, s32[8,128]{1,0:T(8,128)} %bitcast.67, s32[8,128]{1,0:T(8,128)} %bitcast.68, s32[1,128]{1,0:T(1,128)} %bitcast.71), custom_call_target="tpu_custom_call" | custom-call | flops 2000000000 | bytes 200000 | tf_op jit(solution)/shard_map/pallas_call | solution.py:418
  10.8 20.6 %all-to-all-start = ((s32[128,1,128]{2,1,0:T(1,128)}), s32[128,1,128]{2,1,0:T(1,128)S(1)}, u32[]{:S(2)}, u32[]{:S(2)}) async-start(s32[128,1,128]{2,1,0:T(1,128)} %bitcast.58), calls=%async_computation | async-start | bytes 131072 | tf_op jit(solution)/shard_map/all_to_all | solution.py:527
  34.4 11.9 %all-to-all-done = s32[128,1,128]{2,1,0:T(1,128)S(1)} async-done(((s32[128,1,128]{2,1,0:T(1,128)}), s32[128,1,128]{2,1,0:T(1,128)S(1)}, u32[]{:S(2)}, u32[]{:S(2)}) %all-to-all-start) | async-done | bytes 65568 | tf_op jit(solution)/shard_map/all_to_all | solution.py:527
  47.1 4.0 %all-to-all-start.1 = ((s32[4,32,128]{2,1,0:T(8,128)}), s32[4,32,128]{2,1,0:T(8,128)S(1)}, u32[]{:S(2)}, u32[]{:S(2)}) async-start(s32[4,32,128]{2,1,0:T(8,128)} %bitcast.13), calls=%async_computation.1 | async-start | bytes 131072 | tf_op jit(solution)/shard_map/all_to_all | solution.py:527
  51.4 4.2 %all-to-all-done.1.code_ref = s32[4,32,128]{2,1,0:T(8,128)S(1)} async-done(((s32[4,32,128]{2,1,0:T(8,128)}), s32[4,32,128]{2,1,0:T(8,128)S(1)}, u32[]{:S(2)}, u32[]{:S(2)}) %all-to-all-start.1) | async-done | bytes 65568 | tf_op jit(solution)/shard_map/all_to_all | solution.py:527
  55.6 8.4 %shard_map.161 = bf16[6144,128]{1,0:T(8,128)(2,1)} custom-call(s32[4,32,128]{2,1,0:T(8,128)S(1)} %all-to-all-done.1.code_ref, bf16[512,1024]{1,0:T(8,128)(2,1)S(1)} %shard_map.160.fold_ref, bf16[512,512]{1,0:T(8,128)(2,1)S(1)} %shard_map.159.cfold_ref), custom_call_target="tpu_custom_call" | custom-call | flops 7000000000 | bytes 3200000 | tf_op jit(solution)/shard_map/pallas_call | solution.py:449
  64.0 11.2 %all-to-all-start.2 = ((bf16[512,3,4,128]{3,2,1,0:T(4,128)(2,1)}), bf16[512,3,4,128]{3,2,1,0:T(4,128)(2,1)S(1)}, u32[]{:S(2)}, u32[]{:S(2)}) async-start(bf16[512,3,4,128]{3,2,1,0:T(4,128)(2,1)} %bitcast.18), calls=%async_computation.2 | async-start | bytes 3145728 | tf_op jit(solution)/shard_map/all_to_all | solution.py:527
  76.4 79.8 %all-to-all-done.2 = bf16[512,3,4,128]{3,2,1,0:T(4,128)(2,1)S(1)} async-done(((bf16[512,3,4,128]{3,2,1,0:T(4,128)(2,1)}), bf16[512,3,4,128]{3,2,1,0:T(4,128)(2,1)S(1)}, u32[]{:S(2)}, u32[]{:S(2)}) %all-to-all-start.2) | async-done | bytes 1572896 | tf_op jit(solution)/shard_map/all_to_all | solution.py:527
  156.4 1.5 copy.26
  157.9 6.4 %shard_map.162 = (bf16[3072,128]{1,0:T(8,128)(2,1)}, bf16[128,640]{1,0:T(8,128)(2,1)}) custom-call(s32[128,128]{1,0:T(8,128)} %copy-done.8, bf16[4,2,768,128]{3,2,1,0:T(8,128)(2,1)} %bitcast.63, bf16[128,512]{1,0:T(8,128)(2,1)} %dense_ref.1, bf16[4,320,1024]{2,1,0:T(8,128)(2,1)} %bitcast.50, f32[1,1024]{1,0:T(1,128)} %bitcast.69, f32[1,1024]{1,0:T(1,128)} %bitcast.59, ...), custom_call_target="tpu_custom_call" | custom-call | flops 2000000000 | bytes 5000000 | tf_op jit(solution)/shard_map/pallas_call | solution.py:460
  164.4 11.0 %all-to-all-start.3 = ((bf16[512,3,2,128]{3,2,1,0:T(2,128)(2,1)}), bf16[512,3,2,128]{3,2,1,0:T(2,128)(2,1)}, u32[]{:S(2)}, u32[]{:S(2)}) async-start(bf16[512,3,2,128]{3,2,1,0:T(2,128)(2,1)} %bitcast.64), calls=%async_computation.3 | async-start | bytes 1572864 | tf_op jit(solution)/shard_map/all_to_all | solution.py:527
  175.4 2.3 collective-permute-start
  177.7 4.3 %collective-permute-start.1 = (bf16[128,640]{1,0:T(8,128)(2,1)S(1)}, bf16[128,640]{1,0:T(8,128)(2,1)S(1)}, u32[]{:S(2)}, u32[]{:S(2)}) collective-permute-start(bf16[128,640]{1,0:T(8,128)(2,1)S(1)} %copy-done.5), channel_id=1, source_target_pairs={{0,2},{1,3},{2,0},{3,1},{4,6},{5,7},{6,4},{7,5},{8,10},{9,11},{10,... | collective-permute-start | bytes 491528 | tf_op jit(solution)/shard_map/ppermute | solution.py:532
  182.1 3.1 %collective-permute-start.2 = (bf16[128,640]{1,0:T(8,128)(2,1)S(1)}, bf16[128,640]{1,0:T(8,128)(2,1)S(1)}, u32[]{:S(2)}, u32[]{:S(2)}) collective-permute-start(bf16[128,640]{1,0:T(8,128)(2,1)S(1)} %copy-done.5), channel_id=1, source_target_pairs={{0,3},{1,0},{2,1},{3,2},{4,7},{5,4},{6,5},{7,6},{8,11},{9,8},{10,9... | collective-permute-start | bytes 491528 | tf_op jit(solution)/shard_map/ppermute | solution.py:532
  185.2 3.9 %collective-permute-done.1.s2 = bf16[128,640]{1,0:T(8,128)(2,1)S(1)} collective-permute-done((bf16[128,640]{1,0:T(8,128)(2,1)S(1)}, bf16[128,640]{1,0:T(8,128)(2,1)S(1)}, u32[]{:S(2)}, u32[]{:S(2)}) %collective-permute-start.1) | collective-permute-done | bytes 163872 | tf_op jit(solution)/shard_map/ppermute | solution.py:532
  190.0 2.1 shard_map.163
  192.1 5.9 %collective-permute-start.3 = (f32[4,16,8,256]{3,2,1,0:T(8,128)S(1)}, f32[4,16,8,256]{3,2,1,0:T(8,128)S(1)}, u32[]{:S(2)}, u32[]{:S(2)}) collective-permute-start(f32[4,16,8,256]{3,2,1,0:T(8,128)S(1)} %get-tuple-element.23), channel_id=1, source_target_pairs={{0,4},{4,0},{1,5},{5,1},{2,6},{6,2},{3,7},{7,3},{8,12},{12,8},{9,1... | collective-permute-start | bytes 1572872 | tf_op jit(solution)/shard_map/ppermute | solution.py:532
  198.0 1.5 collective-permute-done.3
  199.6 1.9 collective-permute-start.4
  201.5 4.3 %collective-permute-start.5 = (f32[16,8,256]{2,1,0:T(8,128)S(1)}, f32[16,8,256]{2,1,0:T(8,128)S(1)}, u32[]{:S(2)}, u32[]{:S(2)}) collective-permute-start(f32[16,8,256]{2,1,0:T(8,128)S(1)} %get-tuple-element.31), channel_id=1, source_target_pairs={{0,256},{128,384},{256,0},{384,128},{1,257},{129,385},{257,1},{385... | collective-permute-start | bytes 393224 | tf_op jit(solution)/shard_map/ppermute | solution.py:532
  205.9 3.0 %collective-permute-start.6 = (f32[16,8,256]{2,1,0:T(8,128)S(1)}, f32[16,8,256]{2,1,0:T(8,128)S(1)}, u32[]{:S(2)}, u32[]{:S(2)}) collective-permute-start(f32[16,8,256]{2,1,0:T(8,128)S(1)} %get-tuple-element.30), channel_id=1, source_target_pairs={{0,384},{128,0},{256,128},{384,256},{1,385},{129,1},{257,129},{385... | collective-permute-start | bytes 393224 | tf_op jit(solution)/shard_map/ppermute | solution.py:532
  208.9 2.5 collective-permute-done.5
  211.5 2.3 collective-permute-done.6
  213.8 6.1 %all-to-all-done.3 = bf16[512,3,2,128]{3,2,1,0:T(2,128)(2,1)} async-done(((bf16[512,3,2,128]{3,2,1,0:T(2,128)(2,1)}), bf16[512,3,2,128]{3,2,1,0:T(2,128)(2,1)}, u32[]{:S(2)}, u32[]{:S(2)}) %all-to-all-start.3) | async-done | bytes 786464 | tf_op jit(solution)/shard_map/all_to_all | solution.py:527
  219.9 16.9 %all_to_all.37 = f32[16,8,256]{2,1,0:T(8,128)S(1)} all-to-all(f32[16,8,256]{2,1,0:T(8,128)S(1)} %fusion.2), channel_id=1, replica_groups=mesh['y'=4,'z'=16,'core'=2,'x'=4] {'z'}, dimensions={0} | all-to-all | bytes 262144 | tf_op jit(solution)/shard_map/all_to_all | solution.py:527
  237.5 7.6 %all-to-all-start.5 = ((bf16[32,8,256]{2,1,0:T(8,128)(2,1)}), bf16[32,8,256]{2,1,0:T(8,128)(2,1)S(1)}, u32[]{:S(2)}, u32[]{:S(2)}) async-start(bf16[32,8,256]{2,1,0:T(8,128)(2,1)} %broadcast_in_dim.22), calls=%async_computation.5 | async-start | bytes 262144 | tf_op jit(solution)/shard_map/all_to_all | solution.py:527
  246.5 14.3 %all-to-all-done.5.y0 = bf16[32,8,256]{2,1,0:T(8,128)(2,1)S(1)} async-done(((bf16[32,8,256]{2,1,0:T(8,128)(2,1)}), bf16[32,8,256]{2,1,0:T(8,128)(2,1)S(1)}, u32[]{:S(2)}, u32[]{:S(2)}) %all-to-all-start.5) | async-done | bytes 131104 | tf_op jit(solution)/shard_map/all_to_all | solution.py:527
  260.9 4.4 %collective-permute-start.7 = (bf16[32,8,256]{2,1,0:T(8,128)(2,1)S(1)}, bf16[32,8,256]{2,1,0:T(8,128)(2,1)S(1)}, u32[]{:S(2)}, u32[]{:S(2)}) collective-permute-start(bf16[32,8,256]{2,1,0:T(8,128)(2,1)S(1)} %all-to-all-done.5.y0), channel_id=1, source_target_pairs={{0,128},{128,256},{256,384},{384,0},{1,129},{129,257},{257,385},{3... | collective-permute-start | bytes 393224 | tf_op jit(solution)/shard_map/ppermute | solution.py:532
  265.3 2.9 %collective-permute-start.8 = (bf16[32,8,256]{2,1,0:T(8,128)(2,1)S(1)}, bf16[32,8,256]{2,1,0:T(8,128)(2,1)S(1)}, u32[]{:S(2)}, u32[]{:S(2)}) collective-permute-start(bf16[32,8,256]{2,1,0:T(8,128)(2,1)S(1)} %all-to-all-done.5.y0), channel_id=1, source_target_pairs={{0,256},{128,384},{256,0},{384,128},{1,257},{129,385},{257,1},{385... | collective-permute-start | bytes 393224 | tf_op jit(solution)/shard_map/ppermute | solution.py:532
  268.2 3.6 %collective-permute-start.9 = (bf16[32,8,256]{2,1,0:T(8,128)(2,1)S(1)}, bf16[32,8,256]{2,1,0:T(8,128)(2,1)S(1)}, u32[]{:S(2)}, u32[]{:S(2)}) collective-permute-start(bf16[32,8,256]{2,1,0:T(8,128)(2,1)S(1)} %all-to-all-done.5.y0), channel_id=1, source_target_pairs={{0,384},{128,0},{256,128},{384,256},{1,385},{129,1},{257,129},{385... | collective-permute-start | bytes 393224 | tf_op jit(solution)/shard_map/ppermute | solution.py:532
  271.8 5.5 %shard_map.164 = (bf16[4096,128]{1,0:T(8,128)(2,1)}, f32[2,2048]{1,0:T(2,128)}) custom-call(s32[4,32,128]{2,1,0:T(8,128)S(1)} %all-to-all-done.1.code_ref, bf16[4,768,128]{2,1,0:T(8,128)(2,1)S(1)} %bitcast.54, bf16[4096,128]{1,0:T(8,128)(2,1)S(1)} %bitcast.53, f32[2,2048]{1,0:T(2,128)S(1)} %copy-done.7), custom_call_target="tpu_custom_call" | custom-call | flops 7000000000 | bytes 3000000 | tf_op jit(solution)/shard_map/pallas_call | solution.py:514
  277.3 1.6 shard_map.165
  (48 shorter events, 8.7 us)
Async XLA Ops:
  7.2 24.2 %copy-start.3 = (bf16[4096,64]{0,1:T(8,128)(2,1)S(1)}, bf16[4096,64]{0,1:T(8,128)(2,1)}, u32[]{:S(2)}) copy-start(bf16[4096,64]{0,1:T(8,128)(2,1)} %param.16) | copy-start | bytes 1572868
  10.8 35.6 %all-to-all-start = ((s32[128,1,128]{2,1,0:T(1,128)}), s32[128,1,128]{2,1,0:T(1,128)S(1)}, u32[]{:S(2)}, u32[]{:S(2)}) async-start(s32[128,1,128]{2,1,0:T(1,128)} %bitcast.58), calls=%async_computation | async-start | bytes 131072 | tf_op jit(solution)/shard_map/all_to_all | solution.py:527
  31.4 0.9 copy-start.4
  32.5 0.7 copy-start.9
  33.2 17.9 %copy-start.1 = (bf16[2,2048,128]{2,1,0:T(8,128)(2,1)S(1)}, bf16[2,2048,128]{2,1,0:T(8,128)(2,1)}, u32[]{:S(2)}) copy-start(bf16[2,2048,128]{2,1,0:T(8,128)(2,1)} %param.14) | copy-start | bytes 3145732
  33.8 0.6 copy-start.8
  47.1 8.5 %all-to-all-start.1 = ((s32[4,32,128]{2,1,0:T(8,128)}), s32[4,32,128]{2,1,0:T(8,128)S(1)}, u32[]{:S(2)}, u32[]{:S(2)}) async-start(s32[4,32,128]{2,1,0:T(8,128)} %bitcast.13), calls=%async_computation.1 | async-start | bytes 131072 | tf_op jit(solution)/shard_map/all_to_all | solution.py:527
  64.0 11.5 %copy-start.11 = (bf16[128,512]{1,0:T(8,128)(2,1)S(1)}, bf16[128,512]{1,0:T(8,128)(2,1)}, u32[]{:S(2)}) copy-start(bf16[128,512]{1,0:T(8,128)(2,1)} %dense_ref.1) | copy-start | bytes 393220
  64.0 11.5 %copy-start.10 = (bf16[256,1024]{1,0:T(8,128)(2,1)S(1)}, bf16[256,1024]{1,0:T(8,128)(2,1)}, u32[]{:S(2)}) copy-start(bf16[256,1024]{1,0:T(8,128)(2,1)} %param.24) | copy-start | bytes 1572868
  64.0 92.2 %all-to-all-start.2 = ((bf16[512,3,4,128]{3,2,1,0:T(4,128)(2,1)}), bf16[512,3,4,128]{3,2,1,0:T(4,128)(2,1)S(1)}, u32[]{:S(2)}, u32[]{:S(2)}) async-start(bf16[512,3,4,128]{3,2,1,0:T(4,128)(2,1)} %bitcast.18), calls=%async_computation.2 | async-start | bytes 3145728 | tf_op jit(solution)/shard_map/all_to_all | solution.py:527
  75.2 82.8 %all-gather.3.cloned.1.call-start = ((), (), s32[]{:S(2)}) async-start(), calls=%async_computation.6 | async-start | bytes 3276800 | tf_op jit(solution)/shard_map/all_gather | solution.py:569
  157.9 32.0 %copy-start = (bf16[1280,1024]{1,0:T(8,128)(2,1)S(1)}, bf16[1280,1024]{1,0:T(8,128)(2,1)}, u32[]{:S(2)}) copy-start(bf16[1280,1024]{1,0:T(8,128)(2,1)} %all-gather.3.cloned.1.call-done) | copy-start | bytes 7864324
  164.4 11.0 %copy-start.5 = (bf16[128,640]{1,0:T(8,128)(2,1)S(1)}, bf16[128,640]{1,0:T(8,128)(2,1)}, u32[]{:S(2)}) copy-start(bf16[128,640]{1,0:T(8,128)(2,1)} %get-tuple-element.21.s0) | copy-start | bytes 491524
  164.4 25.6 %copy-start.6 = (f32[1024]{0:T(1024)S(1)}, f32[1024]{0:T(1024)}, u32[]{:S(2)}) copy-start(f32[1024]{0:T(1024)} %param.26) | copy-start | bytes 12292
  164.4 55.5 %all-to-all-start.3 = ((bf16[512,3,2,128]{3,2,1,0:T(2,128)(2,1)}), bf16[512,3,2,128]{3,2,1,0:T(2,128)(2,1)}, u32[]{:S(2)}, u32[]{:S(2)}) async-start(bf16[512,3,2,128]{3,2,1,0:T(2,128)(2,1)} %bitcast.64), calls=%async_computation.3 | async-start | bytes 1572864 | tf_op jit(solution)/shard_map/all_to_all | solution.py:527
  175.4 9.9 %collective-permute-start = (bf16[128,640]{1,0:T(8,128)(2,1)S(1)}, bf16[128,640]{1,0:T(8,128)(2,1)S(1)}, u32[]{:S(2)}, u32[]{:S(2)}) collective-permute-start(bf16[128,640]{1,0:T(8,128)(2,1)S(1)} %copy-done.5), channel_id=1, source_target_pairs={{0,1},{1,2},{2,3},{3,0},{4,5},{5,6},{6,7},{7,4},{8,9},{9,10},{10,1... | collective-permute-start | bytes 491528 | tf_op jit(solution)/shard_map/ppermute | solution.py:532
  177.7 11.4 %collective-permute-start.1 = (bf16[128,640]{1,0:T(8,128)(2,1)S(1)}, bf16[128,640]{1,0:T(8,128)(2,1)S(1)}, u32[]{:S(2)}, u32[]{:S(2)}) collective-permute-start(bf16[128,640]{1,0:T(8,128)(2,1)S(1)} %copy-done.5), channel_id=1, source_target_pairs={{0,2},{1,3},{2,0},{3,1},{4,6},{5,7},{6,4},{7,5},{8,10},{9,11},{10,... | collective-permute-start | bytes 491528 | tf_op jit(solution)/shard_map/ppermute | solution.py:532
  182.1 7.9 %collective-permute-start.2 = (bf16[128,640]{1,0:T(8,128)(2,1)S(1)}, bf16[128,640]{1,0:T(8,128)(2,1)S(1)}, u32[]{:S(2)}, u32[]{:S(2)}) collective-permute-start(bf16[128,640]{1,0:T(8,128)(2,1)S(1)} %copy-done.5), channel_id=1, source_target_pairs={{0,3},{1,0},{2,1},{3,2},{4,7},{5,4},{6,5},{7,6},{8,11},{9,8},{10,9... | collective-permute-start | bytes 491528 | tf_op jit(solution)/shard_map/ppermute | solution.py:532
  192.1 7.4 %collective-permute-start.3 = (f32[4,16,8,256]{3,2,1,0:T(8,128)S(1)}, f32[4,16,8,256]{3,2,1,0:T(8,128)S(1)}, u32[]{:S(2)}, u32[]{:S(2)}) collective-permute-start(f32[4,16,8,256]{3,2,1,0:T(8,128)S(1)} %get-tuple-element.23), channel_id=1, source_target_pairs={{0,4},{4,0},{1,5},{5,1},{2,6},{6,2},{3,7},{7,3},{8,12},{12,8},{9,1... | collective-permute-start | bytes 1572872 | tf_op jit(solution)/shard_map/ppermute | solution.py:532
  199.6 9.3 %collective-permute-start.4 = (f32[16,8,256]{2,1,0:T(8,128)S(1)}, f32[16,8,256]{2,1,0:T(8,128)S(1)}, u32[]{:S(2)}, u32[]{:S(2)}) collective-permute-start(f32[16,8,256]{2,1,0:T(8,128)S(1)} %get-tuple-element.29), channel_id=1, source_target_pairs={{0,128},{128,256},{256,384},{384,0},{1,129},{129,257},{257,385},{3... | collective-permute-start | bytes 393224 | tf_op jit(solution)/shard_map/ppermute | solution.py:532
  201.5 9.9 %collective-permute-start.5 = (f32[16,8,256]{2,1,0:T(8,128)S(1)}, f32[16,8,256]{2,1,0:T(8,128)S(1)}, u32[]{:S(2)}, u32[]{:S(2)}) collective-permute-start(f32[16,8,256]{2,1,0:T(8,128)S(1)} %get-tuple-element.31), channel_id=1, source_target_pairs={{0,256},{128,384},{256,0},{384,128},{1,257},{129,385},{257,1},{385... | collective-permute-start | bytes 393224 | tf_op jit(solution)/shard_map/ppermute | solution.py:532
  205.9 7.9 %collective-permute-start.6 = (f32[16,8,256]{2,1,0:T(8,128)S(1)}, f32[16,8,256]{2,1,0:T(8,128)S(1)}, u32[]{:S(2)}, u32[]{:S(2)}) collective-permute-start(f32[16,8,256]{2,1,0:T(8,128)S(1)} %get-tuple-element.30), channel_id=1, source_target_pairs={{0,384},{128,0},{256,128},{384,256},{1,385},{129,1},{257,129},{385... | collective-permute-start | bytes 393224 | tf_op jit(solution)/shard_map/ppermute | solution.py:532
  237.5 23.4 %all-to-all-start.5 = ((bf16[32,8,256]{2,1,0:T(8,128)(2,1)}), bf16[32,8,256]{2,1,0:T(8,128)(2,1)S(1)}, u32[]{:S(2)}, u32[]{:S(2)}) async-start(bf16[32,8,256]{2,1,0:T(8,128)(2,1)} %broadcast_in_dim.22), calls=%async_computation.5 | async-start | bytes 262144 | tf_op jit(solution)/shard_map/all_to_all | solution.py:527
  245.0 26.8 %copy-start.2 = (bf16[2,2048,128]{2,1,0:T(8,128)(2,1)S(1)}, bf16[2,2048,128]{2,1,0:T(8,128)(2,1)}, u32[]{:S(2)}) copy-start(bf16[2,2048,128]{2,1,0:T(8,128)(2,1)} %param.14) | copy-start | bytes 3145732
  245.0 26.8 %copy-start.7 = (f32[2,2048]{1,0:T(2,128)S(1)}, f32[2,2048]{1,0:T(2,128)}, u32[]{:S(2)}) copy-start(f32[2,2048]{1,0:T(2,128)} %accum_ref.1) | copy-start | bytes 49156
  260.9 16.4 %collective-permute-start.7 = (bf16[32,8,256]{2,1,0:T(8,128)(2,1)S(1)}, bf16[32,8,256]{2,1,0:T(8,128)(2,1)S(1)}, u32[]{:S(2)}, u32[]{:S(2)}) collective-permute-start(bf16[32,8,256]{2,1,0:T(8,128)(2,1)S(1)} %all-to-all-done.5.y0), channel_id=1, source_target_pairs={{0,128},{128,256},{256,384},{384,0},{1,129},{129,257},{257,385},{3... | collective-permute-start | bytes 393224 | tf_op jit(solution)/shard_map/ppermute | solution.py:532
  265.3 12.0 %collective-permute-start.8 = (bf16[32,8,256]{2,1,0:T(8,128)(2,1)S(1)}, bf16[32,8,256]{2,1,0:T(8,128)(2,1)S(1)}, u32[]{:S(2)}, u32[]{:S(2)}) collective-permute-start(bf16[32,8,256]{2,1,0:T(8,128)(2,1)S(1)} %all-to-all-done.5.y0), channel_id=1, source_target_pairs={{0,256},{128,384},{256,0},{384,128},{1,257},{129,385},{257,1},{385... | collective-permute-start | bytes 393224 | tf_op jit(solution)/shard_map/ppermute | solution.py:532
  268.2 9.1 %collective-permute-start.9 = (bf16[32,8,256]{2,1,0:T(8,128)(2,1)S(1)}, bf16[32,8,256]{2,1,0:T(8,128)(2,1)S(1)}, u32[]{:S(2)}, u32[]{:S(2)}) collective-permute-start(bf16[32,8,256]{2,1,0:T(8,128)(2,1)S(1)} %all-to-all-done.5.y0), channel_id=1, source_target_pairs={{0,384},{128,0},{256,128},{384,256},{1,385},{129,1},{257,129},{385... | collective-permute-start | bytes 393224 | tf_op jit(solution)/shard_map/ppermute | solution.py:532
Sparse Core Ops, SparseCore 0:
  78.7 52.3 all-gather.2

commit v4 on v3

--- a/solution.py
+++ b/solution.py
@@ -30,7 +30,6 @@
 PART_ROWS, PART_COLS = 8, X // 4
 VMEM = 40 * 1024 * 1024
 MOST_VMEM = 60 * 1024 * 1024
-DENSE_VMEM = 57 * 1024 * 1024
 
 F32 = jnp.float32
 BF16 = jnp.bfloat16
@@ -154,6 +153,12 @@
     bag_ref[...] = dot(bag_s[...], own_s[...], NT).astype(I32)
 
 
+def turn_kernel(place_ref, arrived_ref, b0, b1, b2, b3, turned_s):
+    turned_s[...] = arrived_ref[...].T
+    for step, block in enumerate((b0, b1, b2, b3)):
+        block[...] = turned_s[aligned((place_ref[0] + step) & (PEERS - 1), BLOCK), :]
+
+
 def columns(codes, first):
     return jnp.concatenate([codes[:, r : r + 1] for r in range(first, first + GROUP)], axis=0)
 
@@ -174,7 +179,9 @@
         out_ref[:, h * D : (h + 1) * D] = row_ref[h * groups : (h + 1) * groups, :]
 
 
-def lookup_kernel(code_ref, fold_ref, cfold_ref, out_ref):
+def lookup_kernel(place_ref, c0, c1, c2, c3, fold_ref, cfold_ref, out_ref, code_ref):
+    for step, part in enumerate((c0, c1, c2, c3)):
+        code_ref[(place_ref[0] + PEERS - step) & (PEERS - 1)] = part[...]
     groups = fold_ref.shape[0]
     picks = [
         jnp.concatenate([code_ref[c, i * CAP : (i + 1) * CAP, :] for c in range(PEERS)], axis=0) - 1
@@ -217,21 +224,17 @@
 
 
 def dense_kernel(
-    bag_ref, reply_in, dense_ref, weight_in, bias_ref, head_ref, label_ref,
-    grads_ref, share_ref, weight_ref, reply_ref, sems, reply_sems,
+    place_ref, w0, w1, w2, w3, bag_ref, reply_ref, dense_ref, bias_ref, head_ref, label_ref,
+    grads_ref, share_ref, weight_ref, sems,
 ):
     wide = X // PEERS
-    replies = [
-        pltpu.make_async_copy(reply_in.at[c], reply_ref.at[c], reply_sems.at[c])
-        for c in range(PEERS)
-    ]
-    for reply in replies:
-        reply.start()
     fetches = [
         pltpu.make_async_copy(
-            weight_in.at[c, pl.ds(0, wide)], weight_ref.at[pl.ds(c * wide, wide)], sems.at[c]
+            part.at[pl.ds(0, wide)],
+            weight_ref.at[aligned((place_ref[0] + PEERS - step) & (PEERS - 1), wide)],
+            sems.at[step],
         )
-        for c in range(PEERS)
+        for step, part in enumerate((w0, w1, w2, w3))
     ]
     for fetch in fetches:
         fetch.start()
@@ -245,7 +248,6 @@
     bag_rows = half_iota((2 * B, span), 0, -1)
     pooled = jnp.zeros((2 * B, D), F32)
     for c in range(PEERS):
-        replies[c].wait()
         pooled += dot(ones_where(bag_rows == lanes_of(c * BLOCK)), reply_ref[c, 0])
     halves = [
         ones_where(bag_rows[:B] == lanes_of((i + 1) * CAP)) for i in range(2)
@@ -320,15 +322,17 @@
 
 
 def weight_kernel(
-    place_ref, s0, s1, s2, s3, joined_ref, head_ref, near_ref, far_ref,
+    place_ref, s0, s1, s2, s3, j0, j1, j2, j3, head_ref, near_ref, far_ref,
     cross_s, logit_s, dense_s, sum_s, sems,
 ):
     wide = X // PEERS
     fetches = [
         pltpu.make_async_copy(
-            joined_ref.at[c, pl.ds(wide, B // 2)], dense_s.at[c], sems.at[c]
+            part.at[pl.ds(wide, B // 2)],
+            dense_s.at[(place_ref[0] + PEERS - step) & (PEERS - 1)],
+            sems.at[step],
         )
-        for c in range(PEERS)
+        for step, part in enumerate((j0, j1, j2, j3))
     ]
     for fetch in fetches:
         fetch.start()
@@ -337,8 +341,9 @@
         cross_s[rows, : 2 * POOL] = share[:, : 2 * POOL]
         logit_s[rows, :] = share[:, 2 * POOL :]
     grad_logit = jnp.sum(logit_s[...].astype(F32), axis=1, keepdims=True)
+    for fetch in fetches:
+        fetch.wait()
     for c in range(PEERS):
-        fetches[c].wait()
         for half in range(2):
             first = c * B + half * (B // 2)
             cross_s[first : first + B // 2, 2 * POOL :] = dense_s[
@@ -354,15 +359,18 @@
                 (near_ref, far_ref)[far_core][far_y, z] = sum_s[at]
 
 
-def place_kernel(place_ref, y0, y1, y2, y3, out_ref):
-    for step, part in enumerate((y0, y1, y2, y3)):
+def place_kernel(parts_ref, out_ref):
+    for y in range(Y):
         for core in range(CORES):
-            parts = blocks_of(core, (place_ref[2] + Y - step) & (Y - 1))
-            for z, (rows, cols) in enumerate(parts):
-                out_ref[rows, cols] = part[z * CORES + core].astype(F32)
-
-
-def update_kernel(code_ref, grad_ref, table_ref, accum_ref, table_out, accum_out, sum_s):
+            for z, (rows, cols) in enumerate(blocks_of(core, y)):
+                out_ref[rows, cols] = parts_ref[y * CORES + core, z].astype(F32)
+
+
+def update_kernel(
+    place_ref, c0, c1, c2, c3, grad_ref, table_ref, accum_ref, table_out, accum_out, sum_s, code_ref
+):
+    for step, part in enumerate((c0, c1, c2, c3)):
+        code_ref[(place_ref[0] + PEERS - step) & (PEERS - 1)] = part[...]
     groups = table_ref.shape[0] // FOLD
     span = CAP * N_ROW
     total = None
@@ -445,36 +453,55 @@
     )(after, table)
 
 
-def look_up(codes, fold, cfold):
-    return call(
+def with_place(kernel, out_shape, scratch, place, arrays, flops, bytes_accessed):
+    return pl.pallas_call(
+        kernel,
+        out_shape=out_shape,
+        in_specs=[pl.BlockSpec(memory_space=pltpu.SMEM)]
+        + [pl.BlockSpec(memory_space=pltpu.VMEM)] * len(arrays),
+        scratch_shapes=scratch,
+        compiler_params=pltpu.CompilerParams(vmem_limit_bytes=VMEM),
+        cost_estimate=pl.CostEstimate(
+            flops=flops, bytes_accessed=bytes_accessed, transcendentals=0
+        ),
+    )(place, *arrays)
+
+
+def turn(place, arrived):
+    block = jax.ShapeDtypeStruct((BLOCK, N_ROW), I32)
+    scratch = [pltpu.VMEM((LANES, N_ROW), I32)]
+    return with_place(turn_kernel, (block,) * PEERS, scratch, place, (arrived,), 0, 200_000)
+
+
+def look_up(place, codes, fold, cfold):
+    return with_place(
         lookup_kernel,
         jax.ShapeDtypeStruct((N_ROW * 2 * PEERS * CAP, D), BF16),
-        flops=7 * 10**9,
-        bytes_accessed=3_200_000,
-    )(codes, fold, cfold)
-
-
-def dense_step(bags, replies, dense_in, weight, bias, head, labels):
-    vmem = pl.BlockSpec(memory_space=pltpu.VMEM)
-    hbm = pl.BlockSpec(memory_space=pltpu.HBM)
+        [pltpu.VMEM((PEERS, BLOCK, N_ROW), I32)],
+        place,
+        (*codes, fold, cfold),
+        7 * 10**9,
+        3_200_000,
+    )
+
+
+def dense_step(place, joined, bags, replies, dense_in, bias, head, labels):
+    arrays = (bags, replies, dense_in, bias, head, labels)
     return pl.pallas_call(
         dense_kernel,
         out_shape=(
             jax.ShapeDtypeStruct((N_ROW * PEERS * CAP, D), BF16),
             jax.ShapeDtypeStruct((B, SHARE), BF16),
         ),
-        in_specs=[vmem, hbm, vmem, hbm, vmem, vmem, vmem],
-        scratch_shapes=[
-            pltpu.VMEM((X, X), BF16),
-            pltpu.VMEM(replies.shape, BF16),
-            pltpu.SemaphoreType.DMA((PEERS,)),
-            pltpu.SemaphoreType.DMA((PEERS,)),
-        ],
-        compiler_params=pltpu.CompilerParams(vmem_limit_bytes=DENSE_VMEM),
+        in_specs=[pl.BlockSpec(memory_space=pltpu.SMEM)]
+        + [pl.BlockSpec(memory_space=pltpu.HBM)] * PEERS
+        + [pl.BlockSpec(memory_space=pltpu.VMEM)] * len(arrays),
+        scratch_shapes=[pltpu.VMEM((X, X), BF16), pltpu.SemaphoreType.DMA((PEERS,))],
+        compiler_params=pltpu.CompilerParams(vmem_limit_bytes=VMEM),
         cost_estimate=pl.CostEstimate(
             flops=2 * 10**9, bytes_accessed=5_000_000, transcendentals=0
         ),
-    )(bags, replies, dense_in, weight, bias, head, labels)
+    )(place, *joined, *arrays)
 
 
 def weight_part(place, shares, joined, head):
@@ -485,7 +512,8 @@
         out_shape=(half, half),
         in_specs=[pl.BlockSpec(memory_space=pltpu.SMEM)]
         + [vmem] * PEERS
-        + [pl.BlockSpec(memory_space=pltpu.HBM), vmem],
+        + [pl.BlockSpec(memory_space=pltpu.HBM)] * PEERS
+        + [vmem],
         scratch_shapes=[
             pltpu.VMEM((PEERS * B, X), BF16),
             pltpu.VMEM((PEERS * B, LANES), BF16),
@@ -495,32 +523,27 @@
         ],
         compiler_params=pltpu.CompilerParams(vmem_limit_bytes=VMEM),
         cost_estimate=pl.CostEstimate(flops=0, bytes_accessed=0, transcendentals=0),
-    )(place, *shares, joined, head)
-
-
-def put_in_place(place, parts):
-    return pl.pallas_call(
-        place_kernel,
-        out_shape=jax.ShapeDtypeStruct((X // PEERS, X), F32),
-        in_specs=[pl.BlockSpec(memory_space=pltpu.SMEM)]
-        + [pl.BlockSpec(memory_space=pltpu.VMEM)] * len(parts),
-        compiler_params=pltpu.CompilerParams(vmem_limit_bytes=VMEM),
-        cost_estimate=pl.CostEstimate(flops=0, bytes_accessed=0, transcendentals=0),
-    )(place, *parts)
-
-
-def update(codes, grads, table, accum):
+    )(place, *shares, *joined, head)
+
+
+def put_in_place(parts):
+    return call(place_kernel, jax.ShapeDtypeStruct((X // PEERS, X), F32))(parts)
+
+
+def update(place, codes, grads, table, accum):
     groups = table.shape[0] // FOLD
-    return call(
+    return with_place(
         update_kernel,
         (
             jax.ShapeDtypeStruct(table.shape, BF16),
             jax.ShapeDtypeStruct(accum.shape, F32),
         ),
-        [pltpu.VMEM((groups, FOLD * D), F32)],
-        flops=7 * 10**9,
-        bytes_accessed=3_000_000,
-    )(codes, grads, table, accum)
+        [pltpu.VMEM((groups, FOLD * D), F32), pltpu.VMEM((PEERS, BLOCK, N_ROW), I32)],
+        place,
+        (*codes, grads, table, accum),
+        7 * 10**9,
+        3_000_000,
+    )
 
 
 def exchange(array, axes):
@@ -532,16 +555,16 @@
     return lax.ppermute(array, axis, [(i, (i + step) % size) for i in range(size)])
 
 
-def sum_over_rows(place, near, far, after):
+def sum_over_rows(near, far, after):
     total = near + shifted(far, "core", 1)
     own = total[0]
     for step in range(1, Y):
         own = own + shifted(total[step], "y", step)
     own, after = lax.optimization_barrier((own, after))
     own = jnp.sum(exchange(own, "z"), axis=0).astype(BF16)
-    own = exchange(jnp.broadcast_to(own[None], (Z * CORES, *own.shape)), ("z", "core"))
-    parts = [own] + [shifted(own, "y", step) for step in range(1, Y)]
-    return put_in_place(place, parts), after
+    own = exchange(jnp.broadcast_to(own[None], (Z, *own.shape)), "z")
+    parts = exchange(jnp.broadcast_to(own[None], (Y * CORES, *own.shape)), ("y", "core"))
+    return put_in_place(parts), after
 
 
 def by_peer(array, rows):
@@ -566,7 +589,7 @@
 ):
     packed = jnp.concatenate([dense_in[: B // 2], dense_in[B // 2 :]], axis=1)
     joined = jnp.concatenate([cross_weight, packed], axis=0)
-    joined = lax.all_gather(joined, COL, axis=0)
+    place = jnp.stack([lax.axis_index(axis) for axis in (COL, "core", "y")]).astype(I32)
     head = head_weight[None, :]
     requests, places = build_index(
         row_owner[:, :, 0].T,
@@ -579,28 +602,30 @@
     arrived = exchange(requests, ROW)
     bags = build_bags(places)
     cfold = fold_after(fold_cols_kernel, requests, col_table.T, FOLD * SLICE)
-    arrived, bags, cfold = lax.optimization_barrier((arrived, bags, cfold))
-    codes = exchange(arrived.T.reshape(PEERS, BLOCK, N_ROW), COL)
+    blocks = turn(place, arrived)
+    codes = [blocks[0]] + [shifted(blocks[step], COL, step) for step in range(1, PEERS)]
     flat_table = row_tables.reshape(-1, D)
     fold = fold_after(fold_rows_kernel, arrived, flat_table, FOLD * D)
-    replies = look_up(codes, fold, cfold)
+    replies = look_up(place, codes, fold, cfold)
+    replies, joined = lax.optimization_barrier((replies, joined))
+    joined = [joined] + [shifted(joined, COL, step) for step in range(1, PEERS)]
     replies = by_peer(exchange(replies.reshape(OWNERS, 3, 4, D), ALL), 2 * CAP)
     grads, share = dense_step(
+        place,
+        joined,
         bags,
         replies.reshape(PEERS, 2, CAP * N_ROW, D),
         dense_in,
-        joined,
         cross_bias[None, :],
         head,
         labels[None, :],
     )
     shares = [share] + [shifted(share, COL, step) for step in range(1, PEERS)]
-    place = jnp.stack([lax.axis_index(axis) for axis in (COL, "core", "y")]).astype(I32)
     grads = exchange(grads.reshape(OWNERS, 3, 2, D), ALL)
     near, far = weight_part(place, shares, joined, head)
-    weight_grad, grads = sum_over_rows(place, near, far, grads)
+    weight_grad, grads = sum_over_rows(near, far, grads)
     grads = by_peer(grads, CAP).reshape(PEERS, CAP * N_ROW, D)
-    new_tables, new_accum = update(codes, grads, flat_table, row_accum)
+    new_tables, new_accum = update(place, codes, grads, flat_table, row_accum)
     return (new_tables.reshape(row_tables.shape), new_accum, weight_grad)
 
 

time: 288 us -> 273 us (0.948)
  between operations: 14.4 us -> 1.06 us
  starting transfers between devices: 90.3 us -> 100 us
  waiting for transfers between devices: 127 us -> 118 us
    all_to_all x5, waiting for transfers between devices: 116 us -> 103 us  [exchange(): return lax.all_to_all(array, axes, split_axis=0, concat_axis=0, tiled=True)]
    ppermute x10 -> x13, starting transfers between devices: 35.8 us -> 42.4 us  [shifted(): lax.ppermute(array, axis, [(i, (i + step) % size) for i in range(size)])]
    ppermute x10 -> x13, waiting for transfers between devices: 11.2 us -> 15.5 us  [shifted(): lax.ppermute(array, axis, [(i, (i + step) % size) for i in range(size)])]
    all_to_all x5, starting transfers between devices: 54.3 us -> 57.7 us  [exchange(): return lax.all_to_all(array, axes, split_axis=0, concat_axis=0, tiled=True)]
    pallas_call x3 -> x4, Pallas kernels: 15.5 us -> 16.6 us  [the longest x3 15.6 us: with_place(): pl.pallas_call(kernel, out_shape=out_shape, in_specs=[pl.BlockSpec(memory...]
  transfers between devices with their start and end apart: 16 -> 18, of which waited for: 10 -> 11; matrix products, arithmetic and copies ran while one was open for 2% -> 1% of each run, Pallas kernels for 3% -> 3%
where the time goes in v4:
time: 273 us; the launch traced here: 272 us
  waiting for transfers between devices  118 us (43%)
  starting transfers between devices  100 us (37%)
  Pallas kernels  27.9 us (10%)
  blocking collectives  19.5 us (7%)
  local copies, waits for them, and re-layouts  5.25 us (2%)
    all_to_all x5, waiting for transfers between devices, exchange(): return lax.all_to_all(array, axes, split_axis=0, concat_axis=0, tiled=True)  103 us
    all_to_all x5, starting transfers between devices, exchange(): return lax.all_to_all(array, axes, split_axis=0, concat_axis=0, tiled=True)  57.7 us
    ppermute x13, starting transfers between devices, shifted(): lax.ppermute(array, axis, [(i, (i + step) % size) for i in range(size)])  42.4 us
    all_to_all x1, blocking collectives, exchange(): return lax.all_to_all(array, axes, split_axis=0, concat_axis=0, tiled=True)  19.5 us
    pallas_call x3, Pallas kernels, with_place(): pl.pallas_call(kernel, out_shape=out_shape, in_specs=[pl.BlockSpec(memory...  15.6 us
    ppermute x13, waiting for transfers between devices, shifted(): lax.ppermute(array, axis, [(i, (i + step) % size) for i in range(size)])  15.5 us
  transfers between devices with their start and end apart: 18, of which 11 were waited for; matrix products, arithmetic and copies ran while one was open for 1% of the time, Pallas kernels for 3%

profile of v4, /device:TPU:1, one launch (start us, length us, event | category | flops | bytes accessed | tf_op | source)
XLA Modules:
  0.0 272.3 jit_solution(17297055922777425302)
XLA Ops:
  0.7 3.6 %shard_map.157 = (s32[128,128]{1,0:T(8,128)}, s32[48,128]{1,0:T(8,128)}) custom-call(s32[16,128]{1,0:T(8,128)} %bitcast.61, s32[16,128]{1,0:T(8,128)} %bitcast.62, s32[2,128]{1,0:T(2,128)} %bitcast.65, s32[8,128]{1,0:T(8,128)} %bitcast.63, s32[8,128]{1,0:T(8,128)} %bitcast.64, s32[1,128]{1,0:T(1,128)} %bitcast.66), custom_call_target="tpu_custom_call" | custom-call | flops 2000000000 | bytes 200000 | tf_op jit(solution)/shard_map/pallas_call | solution.py:426
  4.3 20.7 %all-to-all-start = ((s32[128,1,128]{2,1,0:T(1,128)}), s32[128,1,128]{2,1,0:T(1,128)S(1)}, u32[]{:S(2)}, u32[]{:S(2)}) async-start(s32[128,1,128]{2,1,0:T(1,128)} %bitcast.54), calls=%async_computation | async-start | bytes 131072 | tf_op jit(solution)/shard_map/all_to_all | solution.py:550
  25.1 14.9 %all-to-all-done = s32[128,1,128]{2,1,0:T(1,128)S(1)} async-done(((s32[128,1,128]{2,1,0:T(1,128)}), s32[128,1,128]{2,1,0:T(1,128)S(1)}, u32[]{:S(2)}, u32[]{:S(2)}) %all-to-all-start) | async-done | bytes 65568 | tf_op jit(solution)/shard_map/all_to_all | solution.py:550
  40.6 3.1 %collective-permute-start = (s32[32,128]{1,0:T(8,128)S(1)}, s32[32,128]{1,0:T(8,128)S(1)}, u32[]{:S(2)}, u32[]{:S(2)}) collective-permute-start(s32[32,128]{1,0:T(8,128)S(1)} %get-tuple-element.21), channel_id=1, source_target_pairs={{0,1},{1,2},{2,3},{3,0},{4,5},{5,6},{6,7},{7,4},{8,9},{9,10},{10,1... | collective-permute-start | bytes 49160 | tf_op jit(solution)/shard_map/ppermute | solution.py:555
  43.8 4.4 %collective-permute-start.1 = (s32[32,128]{1,0:T(8,128)S(1)}, s32[32,128]{1,0:T(8,128)S(1)}, u32[]{:S(2)}, u32[]{:S(2)}) collective-permute-start(s32[32,128]{1,0:T(8,128)S(1)} %get-tuple-element.22), channel_id=1, source_target_pairs={{0,2},{1,3},{2,0},{3,1},{4,6},{5,7},{6,4},{7,5},{8,10},{9,11},{10,... | collective-permute-start | bytes 49160 | tf_op jit(solution)/shard_map/ppermute | solution.py:555
  48.1 3.1 %collective-permute-start.2 = (s32[32,128]{1,0:T(8,128)S(1)}, s32[32,128]{1,0:T(8,128)S(1)}, u32[]{:S(2)}, u32[]{:S(2)}) collective-permute-start(s32[32,128]{1,0:T(8,128)S(1)} %get-tuple-element.23), channel_id=1, source_target_pairs={{0,3},{1,0},{2,1},{3,2},{4,7},{5,4},{6,5},{7,6},{8,11},{9,8},{10,9... | collective-permute-start | bytes 49160 | tf_op jit(solution)/shard_map/ppermute | solution.py:555
  52.6 8.9 %shard_map.161 = bf16[6144,128]{1,0:T(8,128)(2,1)} custom-call(s32[3]{0:T(128)S(1)} %pad_add_fusion.place_ref, s32[32,128]{1,0:T(8,128)S(1)} %get-tuple-element.20.c0, s32[32,128]{1,0:T(8,128)S(1)} %collective-permute-done.c1, s32[32,128]{1,0:T(8,128)S(1)} %collective-permute-done.1.c2, s32[32,128]{1,0:T(8,128)S(1)} %collective-permute-done.2.c3, ...), custom_call_target="tpu_custom_call" | custom-call | flops 7000000000 | bytes 3200000 | tf_op jit(solution)/shard_map/pallas_call | solution.py:457
  61.6 14.0 %all-to-all-start.1 = ((bf16[512,3,4,128]{3,2,1,0:T(4,128)(2,1)}), bf16[512,3,4,128]{3,2,1,0:T(4,128)(2,1)}, u32[]{:S(2)}, u32[]{:S(2)}) async-start(bf16[512,3,4,128]{3,2,1,0:T(4,128)(2,1)} %bitcast.16), calls=%async_computation.1 | async-start | bytes 3145728 | tf_op jit(solution)/shard_map/all_to_all | solution.py:550
  75.6 4.5 %collective-permute-start.5 = (bf16[320,1024]{1,0:T(8,128)(2,1)S(1)}, bf16[320,1024]{1,0:T(8,128)(2,1)S(1)}, u32[]{:S(2)}, u32[]{:S(2)}) collective-permute-start(bf16[320,1024]{1,0:T(8,128)(2,1)S(1)} %maximum_maximum_fusion.w0.j0), channel_id=1, source_target_pairs={{0,3},{1,0},{2,1},{3,2},{4,7},{5,4},{6,5},{7,6},{8,11},{9,8},{10,9... | collective-permute-start | bytes 1966088 | tf_op jit(solution)/shard_map/ppermute | solution.py:555
  80.2 2.5 collective-permute-start.4
  82.6 2.5 collective-permute-start.3
  85.7 69.1 %all-to-all-done.1 = bf16[512,3,4,128]{3,2,1,0:T(4,128)(2,1)} async-done(((bf16[512,3,4,128]{3,2,1,0:T(4,128)(2,1)}), bf16[512,3,4,128]{3,2,1,0:T(4,128)(2,1)}, u32[]{:S(2)}, u32[]{:S(2)}) %all-to-all-start.1) | async-done | bytes 1572896 | tf_op jit(solution)/shard_map/all_to_all | solution.py:550
  157.3 4.3 %shard_map.163 = (bf16[3072,128]{1,0:T(8,128)(2,1)}, bf16[128,640]{1,0:T(8,128)(2,1)S(1)}) custom-call(s32[3]{0:T(128)S(1)} %pad_add_fusion.place_ref, bf16[320,1024]{1,0:T(8,128)(2,1)S(1)} %maximum_maximum_fusion.w0.j0, bf16[320,1024]{1,0:T(8,128)(2,1)} %collective-permute-done.3.w1.j1, bf16[320,1024]{1,0:T(8,128)(2,1)S(1)} %collective-permute-done.4.w2.j2, ...), custom_call_target="tpu_custom_call" | custom-call | flops 2000000000 | bytes 5000000 | tf_op jit(solution)/shard_map/pallas_call | solution.py:490
  161.6 10.8 %all-to-all-start.2 = ((bf16[512,3,2,128]{3,2,1,0:T(2,128)(2,1)}), bf16[512,3,2,128]{3,2,1,0:T(2,128)(2,1)}, u32[]{:S(2)}, u32[]{:S(2)}) async-start(bf16[512,3,2,128]{3,2,1,0:T(2,128)(2,1)} %bitcast.27), calls=%async_computation.2 | async-start | bytes 1572864 | tf_op jit(solution)/shard_map/all_to_all | solution.py:550
  172.4 3.6 %collective-permute-start.8 = (bf16[128,640]{1,0:T(8,128)(2,1)S(1)}, bf16[128,640]{1,0:T(8,128)(2,1)S(1)}, u32[]{:S(2)}, u32[]{:S(2)}) collective-permute-start(bf16[128,640]{1,0:T(8,128)(2,1)S(1)} %get-tuple-element.27.s0), channel_id=1, source_target_pairs={{0,3},{1,0},{2,1},{3,2},{4,7},{5,4},{6,5},{7,6},{8,11},{9,8},{10,9... | collective-permute-start | bytes 491528 | tf_op jit(solution)/shard_map/ppermute | solution.py:555
  176.0 2.5 collective-permute-start.7
  178.5 2.5 collective-permute-start.6
  181.0 3.4 %collective-permute-done.7.s2 = bf16[128,640]{1,0:T(8,128)(2,1)S(1)} collective-permute-done((bf16[128,640]{1,0:T(8,128)(2,1)S(1)}, bf16[128,640]{1,0:T(8,128)(2,1)S(1)}, u32[]{:S(2)}, u32[]{:S(2)}) %collective-permute-start.7) | collective-permute-done | bytes 163872 | tf_op jit(solution)/shard_map/ppermute | solution.py:555
  184.4 5.3 %collective-permute-done.6.s1 = bf16[128,640]{1,0:T(8,128)(2,1)S(1)} collective-permute-done((bf16[128,640]{1,0:T(8,128)(2,1)S(1)}, bf16[128,640]{1,0:T(8,128)(2,1)S(1)}, u32[]{:S(2)}, u32[]{:S(2)}) %collective-permute-start.6) | collective-permute-done | bytes 163872 | tf_op jit(solution)/shard_map/ppermute | solution.py:555
  189.7 2.3 shard_map.164
  192.0 3.8 %collective-permute-start.9 = (f32[4,16,8,256]{3,2,1,0:T(8,128)S(1)}, f32[4,16,8,256]{3,2,1,0:T(8,128)S(1)}, u32[]{:S(2)}, u32[]{:S(2)}) collective-permute-start(f32[4,16,8,256]{3,2,1,0:T(8,128)S(1)} %get-tuple-element.29), channel_id=1, source_target_pairs={{0,4},{4,0},{1,5},{5,1},{2,6},{6,2},{3,7},{7,3},{8,12},{12,8},{9,1... | collective-permute-start | bytes 1572872 | tf_op jit(solution)/shard_map/ppermute | solution.py:555
  197.4 3.2 %collective-permute-start.10 = (f32[16,8,256]{2,1,0:T(8,128)S(1)}, f32[16,8,256]{2,1,0:T(8,128)S(1)}, u32[]{:S(2)}, u32[]{:S(2)}) collective-permute-start(f32[16,8,256]{2,1,0:T(8,128)S(1)} %get-tuple-element.35), channel_id=1, source_target_pairs={{0,128},{128,256},{256,384},{384,0},{1,129},{129,257},{257,385},{3... | collective-permute-start | bytes 393224 | tf_op jit(solution)/shard_map/ppermute | solution.py:555
  200.6 3.3 %collective-permute-start.12 = (f32[16,8,256]{2,1,0:T(8,128)S(1)}, f32[16,8,256]{2,1,0:T(8,128)S(1)}, u32[]{:S(2)}, u32[]{:S(2)}) collective-permute-start(f32[16,8,256]{2,1,0:T(8,128)S(1)} %get-tuple-element.36), channel_id=1, source_target_pairs={{0,384},{128,0},{256,128},{384,256},{1,385},{129,1},{257,129},{385... | collective-permute-start | bytes 393224 | tf_op jit(solution)/shard_map/ppermute | solution.py:555
  203.9 3.5 %collective-permute-start.11 = (f32[16,8,256]{2,1,0:T(8,128)S(1)}, f32[16,8,256]{2,1,0:T(8,128)S(1)}, u32[]{:S(2)}, u32[]{:S(2)}) collective-permute-start(f32[16,8,256]{2,1,0:T(8,128)S(1)} %get-tuple-element.37), channel_id=1, source_target_pairs={{0,256},{128,384},{256,0},{384,128},{1,257},{129,385},{257,1},{385... | collective-permute-start | bytes 393224 | tf_op jit(solution)/shard_map/ppermute | solution.py:555
  207.6 4.4 %collective-permute-done.11 = f32[16,8,256]{2,1,0:T(8,128)S(1)} collective-permute-done((f32[16,8,256]{2,1,0:T(8,128)S(1)}, f32[16,8,256]{2,1,0:T(8,128)S(1)}, u32[]{:S(2)}, u32[]{:S(2)}) %collective-permute-start.11) | collective-permute-done | bytes 131104 | tf_op jit(solution)/shard_map/ppermute | solution.py:555
  212.0 5.1 %all-to-all-done.2 = bf16[512,3,2,128]{3,2,1,0:T(2,128)(2,1)} async-done(((bf16[512,3,2,128]{3,2,1,0:T(2,128)(2,1)}), bf16[512,3,2,128]{3,2,1,0:T(2,128)(2,1)}, u32[]{:S(2)}, u32[]{:S(2)}) %all-to-all-start.2) | async-done | bytes 786464 | tf_op jit(solution)/shard_map/all_to_all | solution.py:550
  217.1 19.5 %all_to_all.36 = f32[16,8,256]{2,1,0:T(8,128)S(1)} all-to-all(f32[16,8,256]{2,1,0:T(8,128)S(1)} %fusion.2), channel_id=1, replica_groups=mesh['y'=4,'z'=16,'core'=2,'x'=4] {'z'}, dimensions={0} | all-to-all | bytes 262144 | tf_op jit(solution)/shard_map/all_to_all | solution.py:550
  237.2 4.0 %all-to-all-start.4 = ((bf16[16,8,256]{2,1,0:T(8,128)(2,1)}), bf16[16,8,256]{2,1,0:T(8,128)(2,1)S(1)}, u32[]{:S(2)}, u32[]{:S(2)}) async-start(bf16[16,8,256]{2,1,0:T(8,128)(2,1)} %broadcast_in_dim.28), calls=%async_computation.4 | async-start | bytes 131072 | tf_op jit(solution)/shard_map/all_to_all | solution.py:550
  242.6 10.1 %all-to-all-done.4 = bf16[16,8,256]{2,1,0:T(8,128)(2,1)S(1)} async-done(((bf16[16,8,256]{2,1,0:T(8,128)(2,1)}), bf16[16,8,256]{2,1,0:T(8,128)(2,1)S(1)}, u32[]{:S(2)}, u32[]{:S(2)}) %all-to-all-start.4) | async-done | bytes 65568 | tf_op jit(solution)/shard_map/all_to_all | solution.py:550
  253.6 8.1 %all-to-all-start.5 = ((bf16[8,16,8,256]{3,2,1,0:T(8,128)(2,1)}), bf16[8,16,8,256]{3,2,1,0:T(8,128)(2,1)S(1)}, u32[]{:S(2)}, u32[]{:S(2)}) async-start(bf16[8,16,8,256]{3,2,1,0:T(8,128)(2,1)} %broadcast_in_dim.29), calls=%async_computation.5 | async-start | bytes 1048576 | tf_op jit(solution)/shard_map/all_to_all | solution.py:550
  261.8 6.0 %shard_map.165 = (bf16[4096,128]{1,0:T(8,128)(2,1)}, f32[2,2048]{1,0:T(2,128)}) custom-call(s32[3]{0:T(128)S(1)} %pad_add_fusion.place_ref, s32[32,128]{1,0:T(8,128)S(1)} %get-tuple-element.20.c0, s32[32,128]{1,0:T(8,128)S(1)} %collective-permute-done.c1, s32[32,128]{1,0:T(8,128)S(1)} %collective-permute-done.1.c2, s32[32,128]{1,0:T(8,128)S(1)} %collective-permute-done.2.c3, ...), custom_call_target="tpu_custom_call" | custom-call | flops 7000000000 | bytes 3000000 | tf_op jit(solution)/shard_map/pallas_call | solution.py:457
  267.8 3.5 %all-to-all-done.5.parts_ref = bf16[8,16,8,256]{3,2,1,0:T(8,128)(2,1)S(1)} async-done(((bf16[8,16,8,256]{3,2,1,0:T(8,128)(2,1)}), bf16[8,16,8,256]{3,2,1,0:T(8,128)(2,1)S(1)}, u32[]{:S(2)}, u32[]{:S(2)}) %all-to-all-start.5) | async-done | bytes 524320 | tf_op jit(solution)/shard_map/all_to_all | solution.py:550
  (48 shorter events, 10.6 us)
Async XLA Ops:
  0.6 24.5 %copy-start.3 = (bf16[128,512]{1,0:T(8,128)(2,1)S(1)}, bf16[128,512]{1,0:T(8,128)(2,1)}, u32[]{:S(2)}) copy-start(bf16[128,512]{1,0:T(8,128)(2,1)} %dense_ref.1) | copy-start | bytes 393220
  0.6 50.6 %copy-start.9 = (bf16[256,1024]{1,0:T(8,128)(2,1)S(1)}, bf16[256,1024]{1,0:T(8,128)(2,1)}, u32[]{:S(2)}) copy-start(bf16[256,1024]{1,0:T(8,128)(2,1)} %param.24) | copy-start | bytes 1572868
  4.3 47.0 %copy-start.1 = (bf16[4096,64]{0,1:T(8,128)(2,1)S(1)}, bf16[4096,64]{0,1:T(8,128)(2,1)}, u32[]{:S(2)}) copy-start(bf16[4096,64]{0,1:T(8,128)(2,1)} %param.16) | copy-start | bytes 1572868
  4.3 47.0 %copy-start.2 = (s32[128,128]{1,0:T(8,128)S(1)}, s32[128,128]{1,0:T(8,128)}, u32[]{:S(2)}) copy-start(s32[128,128]{1,0:T(8,128)} %get-tuple-element.19.after_ref) | copy-start | bytes 196612
  4.3 35.7 %all-to-all-start = ((s32[128,1,128]{2,1,0:T(1,128)}), s32[128,1,128]{2,1,0:T(1,128)S(1)}, u32[]{:S(2)}, u32[]{:S(2)}) async-start(s32[128,1,128]{2,1,0:T(1,128)} %bitcast.54), calls=%async_computation | async-start | bytes 131072 | tf_op jit(solution)/shard_map/all_to_all | solution.py:550
  25.1 26.4 %copy-start = (bf16[2,2048,128]{2,1,0:T(8,128)(2,1)S(1)}, bf16[2,2048,128]{2,1,0:T(8,128)(2,1)}, u32[]{:S(2)}) copy-start(bf16[2,2048,128]{2,1,0:T(8,128)(2,1)} %param.14) | copy-start | bytes 3145732
  40.6 11.2 %collective-permute-start = (s32[32,128]{1,0:T(8,128)S(1)}, s32[32,128]{1,0:T(8,128)S(1)}, u32[]{:S(2)}, u32[]{:S(2)}) collective-permute-start(s32[32,128]{1,0:T(8,128)S(1)} %get-tuple-element.21), channel_id=1, source_target_pairs={{0,1},{1,2},{2,3},{3,0},{4,5},{5,6},{6,7},{7,4},{8,9},{9,10},{10,1... | collective-permute-start | bytes 49160 | tf_op jit(solution)/shard_map/ppermute | solution.py:555
  43.8 8.0 %collective-permute-start.1 = (s32[32,128]{1,0:T(8,128)S(1)}, s32[32,128]{1,0:T(8,128)S(1)}, u32[]{:S(2)}, u32[]{:S(2)}) collective-permute-start(s32[32,128]{1,0:T(8,128)S(1)} %get-tuple-element.22), channel_id=1, source_target_pairs={{0,2},{1,3},{2,0},{3,1},{4,6},{5,7},{6,4},{7,5},{8,10},{9,11},{10,... | collective-permute-start | bytes 49160 | tf_op jit(solution)/shard_map/ppermute | solution.py:555
  48.1 4.5 %collective-permute-start.2 = (s32[32,128]{1,0:T(8,128)S(1)}, s32[32,128]{1,0:T(8,128)S(1)}, u32[]{:S(2)}, u32[]{:S(2)}) collective-permute-start(s32[32,128]{1,0:T(8,128)S(1)} %get-tuple-element.23), channel_id=1, source_target_pairs={{0,3},{1,0},{2,1},{3,2},{4,7},{5,4},{6,5},{7,6},{8,11},{9,8},{10,9... | collective-permute-start | bytes 49160 | tf_op jit(solution)/shard_map/ppermute | solution.py:555
  61.6 23.6 %copy-start.8 = (s32[48,128]{1,0:T(8,128)S(1)}, s32[48,128]{1,0:T(8,128)}, u32[]{:S(2)}) copy-start(s32[48,128]{1,0:T(8,128)} %get-tuple-element.25.place_ref) | copy-start | bytes 73732
  61.6 93.3 %all-to-all-start.1 = ((bf16[512,3,4,128]{3,2,1,0:T(4,128)(2,1)}), bf16[512,3,4,128]{3,2,1,0:T(4,128)(2,1)}, u32[]{:S(2)}, u32[]{:S(2)}) async-start(bf16[512,3,4,128]{3,2,1,0:T(4,128)(2,1)} %bitcast.16), calls=%async_computation.1 | async-start | bytes 3145728 | tf_op jit(solution)/shard_map/all_to_all | solution.py:550
  75.6 81.4 %collective-permute-start.5 = (bf16[320,1024]{1,0:T(8,128)(2,1)S(1)}, bf16[320,1024]{1,0:T(8,128)(2,1)S(1)}, u32[]{:S(2)}, u32[]{:S(2)}) collective-permute-start(bf16[320,1024]{1,0:T(8,128)(2,1)S(1)} %maximum_maximum_fusion.w0.j0), channel_id=1, source_target_pairs={{0,3},{1,0},{2,1},{3,2},{4,7},{5,4},{6,5},{7,6},{8,11},{9,8},{10,9... | collective-permute-start | bytes 1966088 | tf_op jit(solution)/shard_map/ppermute | solution.py:555
  80.2 76.8 %collective-permute-start.4 = (bf16[320,1024]{1,0:T(8,128)(2,1)S(1)}, bf16[320,1024]{1,0:T(8,128)(2,1)S(1)}, u32[]{:S(2)}, u32[]{:S(2)}) collective-permute-start(bf16[320,1024]{1,0:T(8,128)(2,1)S(1)} %maximum_maximum_fusion.w0.j0), channel_id=1, source_target_pairs={{0,2},{1,3},{2,0},{3,1},{4,6},{5,7},{6,4},{7,5},{8,10},{9,11},{10,... | collective-permute-start | bytes 1966088 | tf_op jit(solution)/shard_map/ppermute | solution.py:555
  82.6 74.4 %collective-permute-start.3 = (bf16[320,1024]{1,0:T(8,128)(2,1)S(1)}, bf16[320,1024]{1,0:T(8,128)(2,1)}, u32[]{:S(2)}, u32[]{:S(2)}) collective-permute-start(bf16[320,1024]{1,0:T(8,128)(2,1)S(1)} %maximum_maximum_fusion.w0.j0), channel_id=1, source_target_pairs={{0,1},{1,2},{2,3},{3,0},{4,5},{5,6},{6,7},{7,4},{8,9},{9,10},{10,1... | collective-permute-start | bytes 1966088 | tf_op jit(solution)/shard_map/ppermute | solution.py:555
  156.6 0.7 copy-start.4
  156.6 0.7 copy-start.6
  156.6 0.7 copy-start.7
  161.6 55.5 %all-to-all-start.2 = ((bf16[512,3,2,128]{3,2,1,0:T(2,128)(2,1)}), bf16[512,3,2,128]{3,2,1,0:T(2,128)(2,1)}, u32[]{:S(2)}, u32[]{:S(2)}) async-start(bf16[512,3,2,128]{3,2,1,0:T(2,128)(2,1)} %bitcast.27), calls=%async_computation.2 | async-start | bytes 1572864 | tf_op jit(solution)/shard_map/all_to_all | solution.py:550
  172.4 8.6 %collective-permute-start.8 = (bf16[128,640]{1,0:T(8,128)(2,1)S(1)}, bf16[128,640]{1,0:T(8,128)(2,1)S(1)}, u32[]{:S(2)}, u32[]{:S(2)}) collective-permute-start(bf16[128,640]{1,0:T(8,128)(2,1)S(1)} %get-tuple-element.27.s0), channel_id=1, source_target_pairs={{0,3},{1,0},{2,1},{3,2},{4,7},{5,4},{6,5},{7,6},{8,11},{9,8},{10,9... | collective-permute-start | bytes 491528 | tf_op jit(solution)/shard_map/ppermute | solution.py:555
  176.0 8.4 %collective-permute-start.7 = (bf16[128,640]{1,0:T(8,128)(2,1)S(1)}, bf16[128,640]{1,0:T(8,128)(2,1)S(1)}, u32[]{:S(2)}, u32[]{:S(2)}) collective-permute-start(bf16[128,640]{1,0:T(8,128)(2,1)S(1)} %get-tuple-element.27.s0), channel_id=1, source_target_pairs={{0,2},{1,3},{2,0},{3,1},{4,6},{5,7},{6,4},{7,5},{8,10},{9,11},{10,... | collective-permute-start | bytes 491528 | tf_op jit(solution)/shard_map/ppermute | solution.py:555
  178.5 11.2 %collective-permute-start.6 = (bf16[128,640]{1,0:T(8,128)(2,1)S(1)}, bf16[128,640]{1,0:T(8,128)(2,1)S(1)}, u32[]{:S(2)}, u32[]{:S(2)}) collective-permute-start(bf16[128,640]{1,0:T(8,128)(2,1)S(1)} %get-tuple-element.27.s0), channel_id=1, source_target_pairs={{0,1},{1,2},{2,3},{3,0},{4,5},{5,6},{6,7},{7,4},{8,9},{9,10},{10,1... | collective-permute-start | bytes 491528 | tf_op jit(solution)/shard_map/ppermute | solution.py:555
  192.0 5.4 %collective-permute-start.9 = (f32[4,16,8,256]{3,2,1,0:T(8,128)S(1)}, f32[4,16,8,256]{3,2,1,0:T(8,128)S(1)}, u32[]{:S(2)}, u32[]{:S(2)}) collective-permute-start(f32[4,16,8,256]{3,2,1,0:T(8,128)S(1)} %get-tuple-element.29), channel_id=1, source_target_pairs={{0,4},{4,0},{1,5},{5,1},{2,6},{6,2},{3,7},{7,3},{8,12},{12,8},{9,1... | collective-permute-start | bytes 1572872 | tf_op jit(solution)/shard_map/ppermute | solution.py:555
  197.4 10.0 %collective-permute-start.10 = (f32[16,8,256]{2,1,0:T(8,128)S(1)}, f32[16,8,256]{2,1,0:T(8,128)S(1)}, u32[]{:S(2)}, u32[]{:S(2)}) collective-permute-start(f32[16,8,256]{2,1,0:T(8,128)S(1)} %get-tuple-element.35), channel_id=1, source_target_pairs={{0,128},{128,256},{256,384},{384,0},{1,129},{129,257},{257,385},{3... | collective-permute-start | bytes 393224 | tf_op jit(solution)/shard_map/ppermute | solution.py:555
  200.6 7.0 %collective-permute-start.12 = (f32[16,8,256]{2,1,0:T(8,128)S(1)}, f32[16,8,256]{2,1,0:T(8,128)S(1)}, u32[]{:S(2)}, u32[]{:S(2)}) collective-permute-start(f32[16,8,256]{2,1,0:T(8,128)S(1)} %get-tuple-element.36), channel_id=1, source_target_pairs={{0,384},{128,0},{256,128},{384,256},{1,385},{129,1},{257,129},{385... | collective-permute-start | bytes 393224 | tf_op jit(solution)/shard_map/ppermute | solution.py:555
  203.9 8.0 %collective-permute-start.11 = (f32[16,8,256]{2,1,0:T(8,128)S(1)}, f32[16,8,256]{2,1,0:T(8,128)S(1)}, u32[]{:S(2)}, u32[]{:S(2)}) collective-permute-start(f32[16,8,256]{2,1,0:T(8,128)S(1)} %get-tuple-element.37), channel_id=1, source_target_pairs={{0,256},{128,384},{256,0},{384,128},{1,257},{129,385},{257,1},{385... | collective-permute-start | bytes 393224 | tf_op jit(solution)/shard_map/ppermute | solution.py:555
  237.2 15.6 %all-to-all-start.4 = ((bf16[16,8,256]{2,1,0:T(8,128)(2,1)}), bf16[16,8,256]{2,1,0:T(8,128)(2,1)S(1)}, u32[]{:S(2)}, u32[]{:S(2)}) async-start(bf16[16,8,256]{2,1,0:T(8,128)(2,1)} %broadcast_in_dim.28), calls=%async_computation.4 | async-start | bytes 131072 | tf_op jit(solution)/shard_map/all_to_all | solution.py:550
  242.5 19.3 %copy-start.5 = (f32[2,2048]{1,0:T(2,128)S(1)}, f32[2,2048]{1,0:T(2,128)}, u32[]{:S(2)}) copy-start(f32[2,2048]{1,0:T(2,128)} %accum_ref.1) | copy-start | bytes 49156
  253.6 17.6 %all-to-all-start.5 = ((bf16[8,16,8,256]{3,2,1,0:T(8,128)(2,1)}), bf16[8,16,8,256]{3,2,1,0:T(8,128)(2,1)S(1)}, u32[]{:S(2)}, u32[]{:S(2)}) async-start(bf16[8,16,8,256]{3,2,1,0:T(8,128)(2,1)} %broadcast_in_dim.29), calls=%async_computation.5 | async-start | bytes 1048576 | tf_op jit(solution)/shard_map/all_to_all | solution.py:550

commit v5 on v4

--- a/solution.py
+++ b/solution.py
@@ -153,12 +153,6 @@
     bag_ref[...] = dot(bag_s[...], own_s[...], NT).astype(I32)
 
 
-def turn_kernel(place_ref, arrived_ref, b0, b1, b2, b3, turned_s):
-    turned_s[...] = arrived_ref[...].T
-    for step, block in enumerate((b0, b1, b2, b3)):
-        block[...] = turned_s[aligned((place_ref[0] + step) & (PEERS - 1), BLOCK), :]
-
-
 def columns(codes, first):
     return jnp.concatenate([codes[:, r : r + 1] for r in range(first, first + GROUP)], axis=0)
 
@@ -179,9 +173,7 @@
         out_ref[:, h * D : (h + 1) * D] = row_ref[h * groups : (h + 1) * groups, :]
 
 
-def lookup_kernel(place_ref, c0, c1, c2, c3, fold_ref, cfold_ref, out_ref, code_ref):
-    for step, part in enumerate((c0, c1, c2, c3)):
-        code_ref[(place_ref[0] + PEERS - step) & (PEERS - 1)] = part[...]
+def lookup_kernel(code_ref, fold_ref, cfold_ref, out_ref):
     groups = fold_ref.shape[0]
     picks = [
         jnp.concatenate([code_ref[c, i * CAP : (i + 1) * CAP, :] for c in range(PEERS)], axis=0) - 1
@@ -366,11 +358,7 @@
                 out_ref[rows, cols] = parts_ref[y * CORES + core, z].astype(F32)
 
 
-def update_kernel(
-    place_ref, c0, c1, c2, c3, grad_ref, table_ref, accum_ref, table_out, accum_out, sum_s, code_ref
-):
-    for step, part in enumerate((c0, c1, c2, c3)):
-        code_ref[(place_ref[0] + PEERS - step) & (PEERS - 1)] = part[...]
+def update_kernel(code_ref, grad_ref, table_ref, accum_ref, table_out, accum_out, sum_s):
     groups = table_ref.shape[0] // FOLD
     span = CAP * N_ROW
     total = None
@@ -453,36 +441,13 @@
     )(after, table)
 
 
-def with_place(kernel, out_shape, scratch, place, arrays, flops, bytes_accessed):
-    return pl.pallas_call(
-        kernel,
-        out_shape=out_shape,
-        in_specs=[pl.BlockSpec(memory_space=pltpu.SMEM)]
-        + [pl.BlockSpec(memory_space=pltpu.VMEM)] * len(arrays),
-        scratch_shapes=scratch,
-        compiler_params=pltpu.CompilerParams(vmem_limit_bytes=VMEM),
-        cost_estimate=pl.CostEstimate(
-            flops=flops, bytes_accessed=bytes_accessed, transcendentals=0
-        ),
-    )(place, *arrays)
-
-
-def turn(place, arrived):
-    block = jax.ShapeDtypeStruct((BLOCK, N_ROW), I32)
-    scratch = [pltpu.VMEM((LANES, N_ROW), I32)]
-    return with_place(turn_kernel, (block,) * PEERS, scratch, place, (arrived,), 0, 200_000)
-
-
-def look_up(place, codes, fold, cfold):
-    return with_place(
+def look_up(codes, fold, cfold):
+    return call(
         lookup_kernel,
         jax.ShapeDtypeStruct((N_ROW * 2 * PEERS * CAP, D), BF16),
-        [pltpu.VMEM((PEERS, BLOCK, N_ROW), I32)],
-        place,
-        (*codes, fold, cfold),
-        7 * 10**9,
-        3_200_000,
-    )
+        flops=7 * 10**9,
+        bytes_accessed=3_200_000,
+    )(codes, fold, cfold)
 
 
 def dense_step(place, joined, bags, replies, dense_in, bias, head, labels):
@@ -530,20 +495,18 @@
     return call(place_kernel, jax.ShapeDtypeStruct((X // PEERS, X), F32))(parts)
 
 
-def update(place, codes, grads, table, accum):
+def update(codes, grads, table, accum):
     groups = table.shape[0] // FOLD
-    return with_place(
+    return call(
         update_kernel,
         (
             jax.ShapeDtypeStruct(table.shape, BF16),
             jax.ShapeDtypeStruct(accum.shape, F32),
         ),
-        [pltpu.VMEM((groups, FOLD * D), F32), pltpu.VMEM((PEERS, BLOCK, N_ROW), I32)],
-        place,
-        (*codes, grads, table, accum),
-        7 * 10**9,
-        3_000_000,
-    )
+        [pltpu.VMEM((groups, FOLD * D), F32)],
+        flops=7 * 10**9,
+        bytes_accessed=3_000_000,
+    )(codes, grads, table, accum)
 
 
 def exchange(array, axes):
@@ -602,11 +565,11 @@
     arrived = exchange(requests, ROW)
     bags = build_bags(places)
     cfold = fold_after(fold_cols_kernel, requests, col_table.T, FOLD * SLICE)
-    blocks = turn(place, arrived)
-    codes = [blocks[0]] + [shifted(blocks[step], COL, step) for step in range(1, PEERS)]
+    arrived, bags, cfold, place = lax.optimization_barrier((arrived, bags, cfold, place))
+    codes = exchange(arrived.T.reshape(PEERS, BLOCK, N_ROW), COL)
     flat_table = row_tables.reshape(-1, D)
     fold = fold_after(fold_rows_kernel, arrived, flat_table, FOLD * D)
-    replies = look_up(place, codes, fold, cfold)
+    replies = look_up(codes, fold, cfold)
     replies, joined = lax.optimization_barrier((replies, joined))
     joined = [joined] + [shifted(joined, COL, step) for step in range(1, PEERS)]
     replies = by_peer(exchange(replies.reshape(OWNERS, 3, 4, D), ALL), 2 * CAP)
@@ -625,7 +588,7 @@
     near, far = weight_part(place, shares, joined, head)
     weight_grad, grads = sum_over_rows(near, far, grads)
     grads = by_peer(grads, CAP).reshape(PEERS, CAP * N_ROW, D)
-    new_tables, new_accum = update(place, codes, grads, flat_table, row_accum)
+    new_tables, new_accum = update(codes, grads, flat_table, row_accum)
     return (new_tables.reshape(row_tables.shape), new_accum, weight_grad)
 
 

time: 273 us -> 269 us (0.985)
  starting transfers between devices: 100 us -> 93.1 us
    ppermute x13 -> x10, starting transfers between devices: 42.4 us -> 32.1 us  [shifted(): lax.ppermute(array, axis, [(i, (i + step) % size) for i in range(size)])]
    all_to_all x5 -> x6, starting transfers between devices: 57.7 us -> 61 us  [exchange(): return lax.all_to_all(array, axes, split_axis=0, concat_axis=0, tiled=True)]
    all_to_all x5 -> x6, waiting for transfers between devices: 103 us -> 106 us  [exchange(): return lax.all_to_all(array, axes, split_axis=0, concat_axis=0, tiled=True)]
    pallas_call x3 -> x2, Pallas kernels: 15.6 us -> 13.8 us  [the longest x1 8.39 us: look_up(): call(lookup_kernel, jax.ShapeDtypeStruct((N_ROW * 2 * PEERS * CAP, D), BF...]
    ppermute x13 -> x10, waiting for transfers between devices: 15.5 us -> 14.7 us  [shifted(): lax.ppermute(array, axis, [(i, (i + step) % size) for i in range(size)])]
  transfers between devices with their start and end apart: 18 -> 16, of which waited for: 11 -> 11; matrix products, arithmetic and copies ran while one was open for 1% -> 1% of each run, Pallas kernels for 3% -> 3%
where the time goes in v5:
time: 269 us; the launch traced here: 268 us
  waiting for transfers between devices  120 us (45%)
  starting transfers between devices  93.1 us (35%)
  Pallas kernels  26.1 us (10%)
  blocking collectives  19.5 us (7%)
  local copies, waits for them, and re-layouts  7.51 us (3%)
    all_to_all x6, waiting for transfers between devices, exchange(): return lax.all_to_all(array, axes, split_axis=0, concat_axis=0, tiled=True)  106 us
    all_to_all x6, starting transfers between devices, exchange(): return lax.all_to_all(array, axes, split_axis=0, concat_axis=0, tiled=True)  61 us
    ppermute x10, starting transfers between devices, shifted(): lax.ppermute(array, axis, [(i, (i + step) % size) for i in range(size)])  32.1 us
    all_to_all x1, blocking collectives, exchange(): return lax.all_to_all(array, axes, split_axis=0, concat_axis=0, tiled=True)  19.5 us
    ppermute x10, waiting for transfers between devices, shifted(): lax.ppermute(array, axis, [(i, (i + step) % size) for i in range(size)])  14.7 us
    pallas_call x1, Pallas kernels, look_up(): call(lookup_kernel, jax.ShapeDtypeStruct((N_ROW * 2 * PEERS * CAP, D), BF...  8.39 us
    pallas_call x1, Pallas kernels, update(): call(update_kernel, (jax.ShapeDtypeStruct(table.shape, BF16), jax.ShapeDt...  5.45 us
  transfers between devices with their start and end apart: 16, of which 11 were waited for; matrix products, arithmetic and copies ran while one was open for 1% of the time, Pallas kernels for 3%

profile of v5, /device:TPU:1, one launch (start us, length us, event | category | flops | bytes accessed | tf_op | source)
XLA Modules:
  0.0 267.7 jit_solution(15423597519699282591)
XLA Ops:
  0.6 3.6 %shard_map.157 = (s32[128,128]{1,0:T(8,128)}, s32[48,128]{1,0:T(8,128)}) custom-call(s32[16,128]{1,0:T(8,128)} %bitcast.63, s32[16,128]{1,0:T(8,128)} %bitcast.64, s32[2,128]{1,0:T(2,128)} %bitcast.67, s32[8,128]{1,0:T(8,128)} %bitcast.65, s32[8,128]{1,0:T(8,128)} %bitcast.66, s32[1,128]{1,0:T(1,128)} %bitcast.68), custom_call_target="tpu_custom_call" | custom-call | flops 2000000000 | bytes 200000 | tf_op jit(solution)/shard_map/pallas_call | solution.py:414
  4.2 20.6 %all-to-all-start = ((s32[128,1,128]{2,1,0:T(1,128)}), s32[128,1,128]{2,1,0:T(1,128)S(1)}, u32[]{:S(2)}, u32[]{:S(2)}) async-start(s32[128,1,128]{2,1,0:T(1,128)} %bitcast.56), calls=%async_computation | async-start | bytes 131072 | tf_op jit(solution)/shard_map/all_to_all | solution.py:513
  27.1 12.7 %all-to-all-done = s32[128,1,128]{2,1,0:T(1,128)S(1)} async-done(((s32[128,1,128]{2,1,0:T(1,128)}), s32[128,1,128]{2,1,0:T(1,128)S(1)}, u32[]{:S(2)}, u32[]{:S(2)}) %all-to-all-start) | async-done | bytes 65568 | tf_op jit(solution)/shard_map/all_to_all | solution.py:513
  40.5 4.0 %all-to-all-start.1 = ((s32[4,32,128]{2,1,0:T(8,128)}), s32[4,32,128]{2,1,0:T(8,128)S(1)}, u32[]{:S(2)}, u32[]{:S(2)}) async-start(s32[4,32,128]{2,1,0:T(8,128)} %bitcast.16), calls=%async_computation.1 | async-start | bytes 131072 | tf_op jit(solution)/shard_map/all_to_all | solution.py:513
  44.9 4.1 %all-to-all-done.1.code_ref = s32[4,32,128]{2,1,0:T(8,128)S(1)} async-done(((s32[4,32,128]{2,1,0:T(8,128)}), s32[4,32,128]{2,1,0:T(8,128)S(1)}, u32[]{:S(2)}, u32[]{:S(2)}) %all-to-all-start.1) | async-done | bytes 65568 | tf_op jit(solution)/shard_map/all_to_all | solution.py:513
  49.0 8.4 %shard_map.161 = bf16[6144,128]{1,0:T(8,128)(2,1)} custom-call(s32[4,32,128]{2,1,0:T(8,128)S(1)} %all-to-all-done.1.code_ref, bf16[512,1024]{1,0:T(8,128)(2,1)S(1)} %shard_map.160.fold_ref, bf16[512,512]{1,0:T(8,128)(2,1)S(1)} %shard_map.159.cfold_ref), custom_call_target="tpu_custom_call" | custom-call | flops 7000000000 | bytes 3200000 | tf_op jit(solution)/shard_map/pallas_call | solution.py:445
  57.4 13.5 %all-to-all-start.2 = ((bf16[512,3,4,128]{3,2,1,0:T(4,128)(2,1)}), bf16[512,3,4,128]{3,2,1,0:T(4,128)(2,1)}, u32[]{:S(2)}, u32[]{:S(2)}) async-start(bf16[512,3,4,128]{3,2,1,0:T(4,128)(2,1)} %bitcast.18), calls=%async_computation.2 | async-start | bytes 3145728 | tf_op jit(solution)/shard_map/all_to_all | solution.py:513
  70.8 4.5 %collective-permute-start.2 = (bf16[320,1024]{1,0:T(8,128)(2,1)S(1)}, bf16[320,1024]{1,0:T(8,128)(2,1)S(1)}, u32[]{:S(2)}, u32[]{:S(2)}) collective-permute-start(bf16[320,1024]{1,0:T(8,128)(2,1)S(1)} %maximum_maximum_fusion.w0.j0), channel_id=1, source_target_pairs={{0,3},{1,0},{2,1},{3,2},{4,7},{5,4},{6,5},{7,6},{8,11},{9,8},{10,9... | collective-permute-start | bytes 1966088 | tf_op jit(solution)/shard_map/ppermute | solution.py:518
  75.4 2.5 collective-permute-start.1
  77.9 2.7 %collective-permute-start = (bf16[320,1024]{1,0:T(8,128)(2,1)S(1)}, bf16[320,1024]{1,0:T(8,128)(2,1)}, u32[]{:S(2)}, u32[]{:S(2)}) collective-permute-start(bf16[320,1024]{1,0:T(8,128)(2,1)S(1)} %maximum_maximum_fusion.w0.j0), channel_id=1, source_target_pairs={{0,1},{1,2},{2,3},{3,0},{4,5},{5,6},{6,7},{7,4},{8,9},{9,10},{10,1... | collective-permute-start | bytes 1966088 | tf_op jit(solution)/shard_map/ppermute | solution.py:518
  80.6 69.5 %all-to-all-done.2 = bf16[512,3,4,128]{3,2,1,0:T(4,128)(2,1)} async-done(((bf16[512,3,4,128]{3,2,1,0:T(4,128)(2,1)}), bf16[512,3,4,128]{3,2,1,0:T(4,128)(2,1)}, u32[]{:S(2)}, u32[]{:S(2)}) %all-to-all-start.2) | async-done | bytes 1572896 | tf_op jit(solution)/shard_map/all_to_all | solution.py:513
  150.1 1.7 copy.25
  152.7 4.3 %shard_map.162 = (bf16[3072,128]{1,0:T(8,128)(2,1)}, bf16[128,640]{1,0:T(8,128)(2,1)S(1)}) custom-call(s32[3]{0:T(128)S(1)} %pad_add_fusion.place_ref, bf16[320,1024]{1,0:T(8,128)(2,1)S(1)} %maximum_maximum_fusion.w0.j0, bf16[320,1024]{1,0:T(8,128)(2,1)} %collective-permute-done.w1.j1, bf16[320,1024]{1,0:T(8,128)(2,1)S(1)} %collective-permute-done.1.w2.j2, ...), custom_call_target="tpu_custom_call" | custom-call | flops 2000000000 | bytes 5000000 | tf_op jit(solution)/shard_map/pallas_call | solution.py:455
  157.0 10.8 %all-to-all-start.3 = ((bf16[512,3,2,128]{3,2,1,0:T(2,128)(2,1)}), bf16[512,3,2,128]{3,2,1,0:T(2,128)(2,1)}, u32[]{:S(2)}, u32[]{:S(2)}) async-start(bf16[512,3,2,128]{3,2,1,0:T(2,128)(2,1)} %bitcast.29), calls=%async_computation.3 | async-start | bytes 1572864 | tf_op jit(solution)/shard_map/all_to_all | solution.py:513
  167.8 3.6 %collective-permute-start.5 = (bf16[128,640]{1,0:T(8,128)(2,1)S(1)}, bf16[128,640]{1,0:T(8,128)(2,1)S(1)}, u32[]{:S(2)}, u32[]{:S(2)}) collective-permute-start(bf16[128,640]{1,0:T(8,128)(2,1)S(1)} %get-tuple-element.27.s0), channel_id=1, source_target_pairs={{0,3},{1,0},{2,1},{3,2},{4,7},{5,4},{6,5},{7,6},{8,11},{9,8},{10,9... | collective-permute-start | bytes 491528 | tf_op jit(solution)/shard_map/ppermute | solution.py:518
  171.4 2.5 collective-permute-start.4
  173.9 2.5 collective-permute-start.3
  176.4 3.4 %collective-permute-done.4.s2 = bf16[128,640]{1,0:T(8,128)(2,1)S(1)} collective-permute-done((bf16[128,640]{1,0:T(8,128)(2,1)S(1)}, bf16[128,640]{1,0:T(8,128)(2,1)S(1)}, u32[]{:S(2)}, u32[]{:S(2)}) %collective-permute-start.4) | collective-permute-done | bytes 163872 | tf_op jit(solution)/shard_map/ppermute | solution.py:518
  179.8 5.3 %collective-permute-done.3.s1 = bf16[128,640]{1,0:T(8,128)(2,1)S(1)} collective-permute-done((bf16[128,640]{1,0:T(8,128)(2,1)S(1)}, bf16[128,640]{1,0:T(8,128)(2,1)S(1)}, u32[]{:S(2)}, u32[]{:S(2)}) %collective-permute-start.3) | collective-permute-done | bytes 163872 | tf_op jit(solution)/shard_map/ppermute | solution.py:518
  185.1 2.3 shard_map.163
  187.4 3.8 %collective-permute-start.6 = (f32[4,16,8,256]{3,2,1,0:T(8,128)S(1)}, f32[4,16,8,256]{3,2,1,0:T(8,128)S(1)}, u32[]{:S(2)}, u32[]{:S(2)}) collective-permute-start(f32[4,16,8,256]{3,2,1,0:T(8,128)S(1)} %get-tuple-element.29), channel_id=1, source_target_pairs={{0,4},{4,0},{1,5},{5,1},{2,6},{6,2},{3,7},{7,3},{8,12},{12,8},{9,1... | collective-permute-start | bytes 1572872 | tf_op jit(solution)/shard_map/ppermute | solution.py:518
  192.8 3.2 %collective-permute-start.7 = (f32[16,8,256]{2,1,0:T(8,128)S(1)}, f32[16,8,256]{2,1,0:T(8,128)S(1)}, u32[]{:S(2)}, u32[]{:S(2)}) collective-permute-start(f32[16,8,256]{2,1,0:T(8,128)S(1)} %get-tuple-element.35), channel_id=1, source_target_pairs={{0,128},{128,256},{256,384},{384,0},{1,129},{129,257},{257,385},{3... | collective-permute-start | bytes 393224 | tf_op jit(solution)/shard_map/ppermute | solution.py:518
  196.0 3.3 %collective-permute-start.9 = (f32[16,8,256]{2,1,0:T(8,128)S(1)}, f32[16,8,256]{2,1,0:T(8,128)S(1)}, u32[]{:S(2)}, u32[]{:S(2)}) collective-permute-start(f32[16,8,256]{2,1,0:T(8,128)S(1)} %get-tuple-element.36), channel_id=1, source_target_pairs={{0,384},{128,0},{256,128},{384,256},{1,385},{129,1},{257,129},{385... | collective-permute-start | bytes 393224 | tf_op jit(solution)/shard_map/ppermute | solution.py:518
  199.3 3.5 %collective-permute-start.8 = (f32[16,8,256]{2,1,0:T(8,128)S(1)}, f32[16,8,256]{2,1,0:T(8,128)S(1)}, u32[]{:S(2)}, u32[]{:S(2)}) collective-permute-start(f32[16,8,256]{2,1,0:T(8,128)S(1)} %get-tuple-element.37), channel_id=1, source_target_pairs={{0,256},{128,384},{256,0},{384,128},{1,257},{129,385},{257,1},{385... | collective-permute-start | bytes 393224 | tf_op jit(solution)/shard_map/ppermute | solution.py:518
  203.0 4.4 %collective-permute-done.8 = f32[16,8,256]{2,1,0:T(8,128)S(1)} collective-permute-done((f32[16,8,256]{2,1,0:T(8,128)S(1)}, f32[16,8,256]{2,1,0:T(8,128)S(1)}, u32[]{:S(2)}, u32[]{:S(2)}) %collective-permute-start.8) | collective-permute-done | bytes 131104 | tf_op jit(solution)/shard_map/ppermute | solution.py:518
  207.4 5.1 %all-to-all-done.3 = bf16[512,3,2,128]{3,2,1,0:T(2,128)(2,1)} async-done(((bf16[512,3,2,128]{3,2,1,0:T(2,128)(2,1)}), bf16[512,3,2,128]{3,2,1,0:T(2,128)(2,1)}, u32[]{:S(2)}, u32[]{:S(2)}) %all-to-all-start.3) | async-done | bytes 786464 | tf_op jit(solution)/shard_map/all_to_all | solution.py:513
  212.5 19.5 %all_to_all.42 = f32[16,8,256]{2,1,0:T(8,128)S(1)} all-to-all(f32[16,8,256]{2,1,0:T(8,128)S(1)} %fusion.2), channel_id=1, replica_groups=mesh['y'=4,'z'=16,'core'=2,'x'=4] {'z'}, dimensions={0} | all-to-all | bytes 262144 | tf_op jit(solution)/shard_map/all_to_all | solution.py:513
  232.6 4.0 %all-to-all-start.5 = ((bf16[16,8,256]{2,1,0:T(8,128)(2,1)}), bf16[16,8,256]{2,1,0:T(8,128)(2,1)S(1)}, u32[]{:S(2)}, u32[]{:S(2)}) async-start(bf16[16,8,256]{2,1,0:T(8,128)(2,1)} %broadcast_in_dim.28), calls=%async_computation.5 | async-start | bytes 131072 | tf_op jit(solution)/shard_map/all_to_all | solution.py:513
  238.0 10.1 %all-to-all-done.5 = bf16[16,8,256]{2,1,0:T(8,128)(2,1)S(1)} async-done(((bf16[16,8,256]{2,1,0:T(8,128)(2,1)}), bf16[16,8,256]{2,1,0:T(8,128)(2,1)S(1)}, u32[]{:S(2)}, u32[]{:S(2)}) %all-to-all-start.5) | async-done | bytes 65568 | tf_op jit(solution)/shard_map/all_to_all | solution.py:513
  249.0 8.1 %all-to-all-start.6 = ((bf16[8,16,8,256]{3,2,1,0:T(8,128)(2,1)}), bf16[8,16,8,256]{3,2,1,0:T(8,128)(2,1)S(1)}, u32[]{:S(2)}, u32[]{:S(2)}) async-start(bf16[8,16,8,256]{3,2,1,0:T(8,128)(2,1)} %broadcast_in_dim.29), calls=%async_computation.6 | async-start | bytes 1048576 | tf_op jit(solution)/shard_map/all_to_all | solution.py:513
  257.2 5.5 %shard_map.164 = (bf16[4096,128]{1,0:T(8,128)(2,1)}, f32[2,2048]{1,0:T(2,128)}) custom-call(s32[4,32,128]{2,1,0:T(8,128)S(1)} %all-to-all-done.1.code_ref, bf16[4,768,128]{2,1,0:T(8,128)(2,1)S(1)} %bitcast.52, bf16[4096,128]{1,0:T(8,128)(2,1)S(1)} %bitcast.51, f32[2,2048]{1,0:T(2,128)S(1)} %copy-done.5), custom_call_target="tpu_custom_call" | custom-call | flops 7000000000 | bytes 3000000 | tf_op jit(solution)/shard_map/pallas_call | solution.py:500
  262.6 4.0 %all-to-all-done.6.parts_ref = bf16[8,16,8,256]{3,2,1,0:T(8,128)(2,1)S(1)} async-done(((bf16[8,16,8,256]{3,2,1,0:T(8,128)(2,1)}), bf16[8,16,8,256]{3,2,1,0:T(8,128)(2,1)S(1)}, u32[]{:S(2)}, u32[]{:S(2)}) %all-to-all-start.6) | async-done | bytes 524320 | tf_op jit(solution)/shard_map/all_to_all | solution.py:513
  (48 shorter events, 9.8 us)
Async XLA Ops:
  4.2 35.6 %all-to-all-start = ((s32[128,1,128]{2,1,0:T(1,128)}), s32[128,1,128]{2,1,0:T(1,128)S(1)}, u32[]{:S(2)}, u32[]{:S(2)}) async-start(s32[128,1,128]{2,1,0:T(1,128)} %bitcast.56), calls=%async_computation | async-start | bytes 131072 | tf_op jit(solution)/shard_map/all_to_all | solution.py:513
  24.9 0.7 copy-start.10
  25.6 1.2 copy-start.1
  25.6 1.2 copy-start.2
  25.6 1.4 copy-start.3
  26.2 0.6 copy-start.8
  26.8 17.7 %copy-start.11 = (bf16[256,1024]{1,0:T(8,128)(2,1)S(1)}, bf16[256,1024]{1,0:T(8,128)(2,1)}, u32[]{:S(2)}) copy-start(bf16[256,1024]{1,0:T(8,128)(2,1)} %param.24) | copy-start | bytes 1572868
  26.8 17.7 %copy-start = (bf16[2,2048,128]{2,1,0:T(8,128)(2,1)S(1)}, bf16[2,2048,128]{2,1,0:T(8,128)(2,1)}, u32[]{:S(2)}) copy-start(bf16[2,2048,128]{2,1,0:T(8,128)(2,1)} %param.14) | copy-start | bytes 3145732
  40.5 8.5 %all-to-all-start.1 = ((s32[4,32,128]{2,1,0:T(8,128)}), s32[4,32,128]{2,1,0:T(8,128)S(1)}, u32[]{:S(2)}, u32[]{:S(2)}) async-start(s32[4,32,128]{2,1,0:T(8,128)} %bitcast.16), calls=%async_computation.1 | async-start | bytes 131072 | tf_op jit(solution)/shard_map/all_to_all | solution.py:513
  57.4 92.7 %all-to-all-start.2 = ((bf16[512,3,4,128]{3,2,1,0:T(4,128)(2,1)}), bf16[512,3,4,128]{3,2,1,0:T(4,128)(2,1)}, u32[]{:S(2)}, u32[]{:S(2)}) async-start(bf16[512,3,4,128]{3,2,1,0:T(4,128)(2,1)} %bitcast.18), calls=%async_computation.2 | async-start | bytes 3145728 | tf_op jit(solution)/shard_map/all_to_all | solution.py:513
  70.8 81.4 %collective-permute-start.2 = (bf16[320,1024]{1,0:T(8,128)(2,1)S(1)}, bf16[320,1024]{1,0:T(8,128)(2,1)S(1)}, u32[]{:S(2)}, u32[]{:S(2)}) collective-permute-start(bf16[320,1024]{1,0:T(8,128)(2,1)S(1)} %maximum_maximum_fusion.w0.j0), channel_id=1, source_target_pairs={{0,3},{1,0},{2,1},{3,2},{4,7},{5,4},{6,5},{7,6},{8,11},{9,8},{10,9... | collective-permute-start | bytes 1966088 | tf_op jit(solution)/shard_map/ppermute | solution.py:518
  75.4 76.8 %collective-permute-start.1 = (bf16[320,1024]{1,0:T(8,128)(2,1)S(1)}, bf16[320,1024]{1,0:T(8,128)(2,1)S(1)}, u32[]{:S(2)}, u32[]{:S(2)}) collective-permute-start(bf16[320,1024]{1,0:T(8,128)(2,1)S(1)} %maximum_maximum_fusion.w0.j0), channel_id=1, source_target_pairs={{0,2},{1,3},{2,0},{3,1},{4,6},{5,7},{6,4},{7,5},{8,10},{9,11},{10,... | collective-permute-start | bytes 1966088 | tf_op jit(solution)/shard_map/ppermute | solution.py:518
  77.9 74.4 %collective-permute-start = (bf16[320,1024]{1,0:T(8,128)(2,1)S(1)}, bf16[320,1024]{1,0:T(8,128)(2,1)}, u32[]{:S(2)}, u32[]{:S(2)}) collective-permute-start(bf16[320,1024]{1,0:T(8,128)(2,1)S(1)} %maximum_maximum_fusion.w0.j0), channel_id=1, source_target_pairs={{0,1},{1,2},{2,3},{3,0},{4,5},{5,6},{6,7},{7,4},{8,9},{9,10},{10,1... | collective-permute-start | bytes 1966088 | tf_op jit(solution)/shard_map/ppermute | solution.py:518
  151.8 0.7 copy-start.4
  151.8 0.7 copy-start.6
  151.8 0.7 copy-start.7
  151.8 0.9 copy-start.9
  157.0 55.5 %all-to-all-start.3 = ((bf16[512,3,2,128]{3,2,1,0:T(2,128)(2,1)}), bf16[512,3,2,128]{3,2,1,0:T(2,128)(2,1)}, u32[]{:S(2)}, u32[]{:S(2)}) async-start(bf16[512,3,2,128]{3,2,1,0:T(2,128)(2,1)} %bitcast.29), calls=%async_computation.3 | async-start | bytes 1572864 | tf_op jit(solution)/shard_map/all_to_all | solution.py:513
  167.8 8.6 %collective-permute-start.5 = (bf16[128,640]{1,0:T(8,128)(2,1)S(1)}, bf16[128,640]{1,0:T(8,128)(2,1)S(1)}, u32[]{:S(2)}, u32[]{:S(2)}) collective-permute-start(bf16[128,640]{1,0:T(8,128)(2,1)S(1)} %get-tuple-element.27.s0), channel_id=1, source_target_pairs={{0,3},{1,0},{2,1},{3,2},{4,7},{5,4},{6,5},{7,6},{8,11},{9,8},{10,9... | collective-permute-start | bytes 491528 | tf_op jit(solution)/shard_map/ppermute | solution.py:518
  171.4 8.4 %collective-permute-start.4 = (bf16[128,640]{1,0:T(8,128)(2,1)S(1)}, bf16[128,640]{1,0:T(8,128)(2,1)S(1)}, u32[]{:S(2)}, u32[]{:S(2)}) collective-permute-start(bf16[128,640]{1,0:T(8,128)(2,1)S(1)} %get-tuple-element.27.s0), channel_id=1, source_target_pairs={{0,2},{1,3},{2,0},{3,1},{4,6},{5,7},{6,4},{7,5},{8,10},{9,11},{10,... | collective-permute-start | bytes 491528 | tf_op jit(solution)/shard_map/ppermute | solution.py:518
  173.9 11.2 %collective-permute-start.3 = (bf16[128,640]{1,0:T(8,128)(2,1)S(1)}, bf16[128,640]{1,0:T(8,128)(2,1)S(1)}, u32[]{:S(2)}, u32[]{:S(2)}) collective-permute-start(bf16[128,640]{1,0:T(8,128)(2,1)S(1)} %get-tuple-element.27.s0), channel_id=1, source_target_pairs={{0,1},{1,2},{2,3},{3,0},{4,5},{5,6},{6,7},{7,4},{8,9},{9,10},{10,1... | collective-permute-start | bytes 491528 | tf_op jit(solution)/shard_map/ppermute | solution.py:518
  187.4 5.4 %collective-permute-start.6 = (f32[4,16,8,256]{3,2,1,0:T(8,128)S(1)}, f32[4,16,8,256]{3,2,1,0:T(8,128)S(1)}, u32[]{:S(2)}, u32[]{:S(2)}) collective-permute-start(f32[4,16,8,256]{3,2,1,0:T(8,128)S(1)} %get-tuple-element.29), channel_id=1, source_target_pairs={{0,4},{4,0},{1,5},{5,1},{2,6},{6,2},{3,7},{7,3},{8,12},{12,8},{9,1... | collective-permute-start | bytes 1572872 | tf_op jit(solution)/shard_map/ppermute | solution.py:518
  192.8 10.0 %collective-permute-start.7 = (f32[16,8,256]{2,1,0:T(8,128)S(1)}, f32[16,8,256]{2,1,0:T(8,128)S(1)}, u32[]{:S(2)}, u32[]{:S(2)}) collective-permute-start(f32[16,8,256]{2,1,0:T(8,128)S(1)} %get-tuple-element.35), channel_id=1, source_target_pairs={{0,128},{128,256},{256,384},{384,0},{1,129},{129,257},{257,385},{3... | collective-permute-start | bytes 393224 | tf_op jit(solution)/shard_map/ppermute | solution.py:518
  196.0 7.0 %collective-permute-start.9 = (f32[16,8,256]{2,1,0:T(8,128)S(1)}, f32[16,8,256]{2,1,0:T(8,128)S(1)}, u32[]{:S(2)}, u32[]{:S(2)}) collective-permute-start(f32[16,8,256]{2,1,0:T(8,128)S(1)} %get-tuple-element.36), channel_id=1, source_target_pairs={{0,384},{128,0},{256,128},{384,256},{1,385},{129,1},{257,129},{385... | collective-permute-start | bytes 393224 | tf_op jit(solution)/shard_map/ppermute | solution.py:518
  199.3 8.0 %collective-permute-start.8 = (f32[16,8,256]{2,1,0:T(8,128)S(1)}, f32[16,8,256]{2,1,0:T(8,128)S(1)}, u32[]{:S(2)}, u32[]{:S(2)}) collective-permute-start(f32[16,8,256]{2,1,0:T(8,128)S(1)} %get-tuple-element.37), channel_id=1, source_target_pairs={{0,256},{128,384},{256,0},{384,128},{1,257},{129,385},{257,1},{385... | collective-permute-start | bytes 393224 | tf_op jit(solution)/shard_map/ppermute | solution.py:518
  232.6 15.6 %all-to-all-start.5 = ((bf16[16,8,256]{2,1,0:T(8,128)(2,1)}), bf16[16,8,256]{2,1,0:T(8,128)(2,1)S(1)}, u32[]{:S(2)}, u32[]{:S(2)}) async-start(bf16[16,8,256]{2,1,0:T(8,128)(2,1)} %broadcast_in_dim.28), calls=%async_computation.5 | async-start | bytes 131072 | tf_op jit(solution)/shard_map/all_to_all | solution.py:513
  237.9 19.3 %copy-start.5 = (f32[2,2048]{1,0:T(2,128)S(1)}, f32[2,2048]{1,0:T(2,128)}, u32[]{:S(2)}) copy-start(f32[2,2048]{1,0:T(2,128)} %accum_ref.1) | copy-start | bytes 49156
  249.0 17.6 %all-to-all-start.6 = ((bf16[8,16,8,256]{3,2,1,0:T(8,128)(2,1)}), bf16[8,16,8,256]{3,2,1,0:T(8,128)(2,1)S(1)}, u32[]{:S(2)}, u32[]{:S(2)}) async-start(bf16[8,16,8,256]{3,2,1,0:T(8,128)(2,1)} %broadcast_in_dim.29), calls=%async_computation.6 | async-start | bytes 1048576 | tf_op jit(solution)/shard_map/all_to_all | solution.py:513

commit v6 on v5

--- a/solution.py
+++ b/solution.py
@@ -27,8 +27,9 @@
 STEPS = 3 * L
 FOLD = 8
 GROUP = 16
+WIDE_GROUP = 32
 PART_ROWS, PART_COLS = 8, X // 4
-VMEM = 40 * 1024 * 1024
+VMEM = 24 * 1024 * 1024
 MOST_VMEM = 60 * 1024 * 1024
 
 F32 = jnp.float32
@@ -153,8 +154,8 @@
     bag_ref[...] = dot(bag_s[...], own_s[...], NT).astype(I32)
 
 
-def columns(codes, first):
-    return jnp.concatenate([codes[:, r : r + 1] for r in range(first, first + GROUP)], axis=0)
+def columns(codes, first, count=GROUP):
+    return jnp.concatenate([codes[:, r : r + 1] for r in range(first, first + count)], axis=0)
 
 
 def fold_cols_kernel(after_ref, col_ref, out_ref):
@@ -182,23 +183,25 @@
     inner = [(pick & (groups - 1)) - groups // 2 for pick in picks]
     outer = [pick // groups for pick in picks]
     wide = PEERS * CAP
-    size = GROUP * wide
-    lane = half_iota((size, groups), 1, groups // 2)
+    size = WIDE_GROUP * wide
     left = iota((size, D), 1) < SLICE
-    for first in range(0, N_ROW, GROUP):
-
-        def found(i, table_ref):
-            return dot(ones_where(to_half(columns(inner[i], first)) == lane), table_ref[...])
-
-        full = found(0, fold_ref)
-        part = jnp.broadcast_to(columns(outer[0], first), (size, D))
+    for first in range(0, N_ROW, WIDE_GROUP):
+
+        def take(which, table_ref):
+            row = jnp.concatenate([columns(inner[i], first, WIDE_GROUP) for i in which], axis=0)
+            lane = half_iota((row.shape[0], groups), 1, groups // 2)
+            return dot(ones_where(to_half(row) == lane), table_ref[...])
+
+        full = take((0,), fold_ref)
+        part = jnp.broadcast_to(columns(outer[0], first, WIDE_GROUP), (size, D))
         rows = jnp.zeros((size, D), F32)
         for h in range(FOLD):
             rows = jnp.where(part == h, full[:, h * D : (h + 1) * D], rows)
+        both = take((1, 2), cfold_ref)
         halves = []
         for i in range(2):
-            full = found(1 + i, cfold_ref)
-            part = jnp.broadcast_to(columns(outer[1 + i], first), (size, D))
+            full = both[i * size : (i + 1) * size]
+            part = jnp.broadcast_to(columns(outer[1 + i], first, WIDE_GROUP), (size, D))
             pair_of = part >> 1
             got = jnp.zeros((size, D), F32)
             for pair in range(FOLD // 2):
@@ -210,7 +213,7 @@
         for at in range(0, size, CAP):
             parts.append(rows[at : at + CAP])
             parts.append(cols[at : at + CAP])
-        out_ref[first * 2 * wide : (first + GROUP) * 2 * wide, :] = jnp.concatenate(
+        out_ref[first * 2 * wide : (first + WIDE_GROUP) * 2 * wide, :] = jnp.concatenate(
             parts, axis=0
         ).astype(BF16)
 

time: 269 us -> 269 us (level)
  no operation moved by 1% of the time
where the time goes in v6:
time: 269 us; the launch traced here: 268 us
  waiting for transfers between devices  121 us (45%)
  starting transfers between devices  93.1 us (35%)
  Pallas kernels  26.4 us (10%)
  blocking collectives  19.5 us (7%)
  local copies, waits for them, and re-layouts  7.51 us (3%)
    all_to_all x6, waiting for transfers between devices, exchange(): return lax.all_to_all(array, axes, split_axis=0, concat_axis=0, tiled=True)  106 us
    all_to_all x6, starting transfers between devices, exchange(): return lax.all_to_all(array, axes, split_axis=0, concat_axis=0, tiled=True)  61.2 us
    ppermute x10, starting transfers between devices, shifted(): lax.ppermute(array, axis, [(i, (i + step) % size) for i in range(size)])  31.9 us
    all_to_all x1, blocking collectives, exchange(): return lax.all_to_all(array, axes, split_axis=0, concat_axis=0, tiled=True)  19.5 us
    ppermute x10, waiting for transfers between devices, shifted(): lax.ppermute(array, axis, [(i, (i + step) % size) for i in range(size)])  14.7 us
    pallas_call x1, Pallas kernels, look_up(): call(lookup_kernel, jax.ShapeDtypeStruct((N_ROW * 2 * PEERS * CAP, D), BF...  8.72 us
    pallas_call x1, Pallas kernels, update(): call(update_kernel, (jax.ShapeDtypeStruct(table.shape, BF16), jax.ShapeDt...  5.45 us
  transfers between devices with their start and end apart: 16, of which 11 were waited for; matrix products, arithmetic and copies ran while one was open for 1% of the time, Pallas kernels for 3%

profile of v6, /device:TPU:1, one launch (start us, length us, event | category | flops | bytes accessed | tf_op | source)
XLA Modules:
  0.0 268.2 jit_solution(5970978121011430220)
XLA Ops:
  0.6 3.6 %shard_map.157 = (s32[128,128]{1,0:T(8,128)}, s32[48,128]{1,0:T(8,128)}) custom-call(s32[16,128]{1,0:T(8,128)} %bitcast.63, s32[16,128]{1,0:T(8,128)} %bitcast.64, s32[2,128]{1,0:T(2,128)} %bitcast.67, s32[8,128]{1,0:T(8,128)} %bitcast.65, s32[8,128]{1,0:T(8,128)} %bitcast.66, s32[1,128]{1,0:T(1,128)} %bitcast.68), custom_call_target="tpu_custom_call" | custom-call | flops 2000000000 | bytes 200000 | tf_op jit(solution)/shard_map/pallas_call | solution.py:417
  4.2 20.6 %all-to-all-start = ((s32[128,1,128]{2,1,0:T(1,128)}), s32[128,1,128]{2,1,0:T(1,128)S(1)}, u32[]{:S(2)}, u32[]{:S(2)}) async-start(s32[128,1,128]{2,1,0:T(1,128)} %bitcast.56), calls=%async_computation | async-start | bytes 131072 | tf_op jit(solution)/shard_map/all_to_all | solution.py:516
  27.1 12.7 %all-to-all-done = s32[128,1,128]{2,1,0:T(1,128)S(1)} async-done(((s32[128,1,128]{2,1,0:T(1,128)}), s32[128,1,128]{2,1,0:T(1,128)S(1)}, u32[]{:S(2)}, u32[]{:S(2)}) %all-to-all-start) | async-done | bytes 65568 | tf_op jit(solution)/shard_map/all_to_all | solution.py:516
  40.5 4.0 %all-to-all-start.1 = ((s32[4,32,128]{2,1,0:T(8,128)}), s32[4,32,128]{2,1,0:T(8,128)S(1)}, u32[]{:S(2)}, u32[]{:S(2)}) async-start(s32[4,32,128]{2,1,0:T(8,128)} %bitcast.16), calls=%async_computation.1 | async-start | bytes 131072 | tf_op jit(solution)/shard_map/all_to_all | solution.py:516
  44.9 4.1 %all-to-all-done.1.code_ref = s32[4,32,128]{2,1,0:T(8,128)S(1)} async-done(((s32[4,32,128]{2,1,0:T(8,128)}), s32[4,32,128]{2,1,0:T(8,128)S(1)}, u32[]{:S(2)}, u32[]{:S(2)}) %all-to-all-start.1) | async-done | bytes 65568 | tf_op jit(solution)/shard_map/all_to_all | solution.py:516
  49.0 8.7 %shard_map.161 = bf16[6144,128]{1,0:T(8,128)(2,1)} custom-call(s32[4,32,128]{2,1,0:T(8,128)S(1)} %all-to-all-done.1.code_ref, bf16[512,1024]{1,0:T(8,128)(2,1)S(1)} %shard_map.160.fold_ref, bf16[512,512]{1,0:T(8,128)(2,1)S(1)} %shard_map.159.cfold_ref), custom_call_target="tpu_custom_call" | custom-call | flops 7000000000 | bytes 3200000 | tf_op jit(solution)/shard_map/pallas_call | solution.py:448
  57.7 13.6 %all-to-all-start.2 = ((bf16[512,3,4,128]{3,2,1,0:T(4,128)(2,1)}), bf16[512,3,4,128]{3,2,1,0:T(4,128)(2,1)}, u32[]{:S(2)}, u32[]{:S(2)}) async-start(bf16[512,3,4,128]{3,2,1,0:T(4,128)(2,1)} %bitcast.18), calls=%async_computation.2 | async-start | bytes 3145728 | tf_op jit(solution)/shard_map/all_to_all | solution.py:516
  71.3 4.5 %collective-permute-start.2 = (bf16[320,1024]{1,0:T(8,128)(2,1)S(1)}, bf16[320,1024]{1,0:T(8,128)(2,1)S(1)}, u32[]{:S(2)}, u32[]{:S(2)}) collective-permute-start(bf16[320,1024]{1,0:T(8,128)(2,1)S(1)} %maximum_maximum_fusion.w0.j0), channel_id=1, source_target_pairs={{0,3},{1,0},{2,1},{3,2},{4,7},{5,4},{6,5},{7,6},{8,11},{9,8},{10,9... | collective-permute-start | bytes 1966088 | tf_op jit(solution)/shard_map/ppermute | solution.py:521
  75.9 2.5 collective-permute-start.1
  78.4 2.5 collective-permute-start
  80.9 69.7 %all-to-all-done.2 = bf16[512,3,4,128]{3,2,1,0:T(4,128)(2,1)} async-done(((bf16[512,3,4,128]{3,2,1,0:T(4,128)(2,1)}), bf16[512,3,4,128]{3,2,1,0:T(4,128)(2,1)}, u32[]{:S(2)}, u32[]{:S(2)}) %all-to-all-start.2) | async-done | bytes 1572896 | tf_op jit(solution)/shard_map/all_to_all | solution.py:516
  150.6 1.7 copy.25
  153.2 4.3 %shard_map.162 = (bf16[3072,128]{1,0:T(8,128)(2,1)}, bf16[128,640]{1,0:T(8,128)(2,1)S(1)}) custom-call(s32[3]{0:T(128)S(1)} %pad_add_fusion.place_ref, bf16[320,1024]{1,0:T(8,128)(2,1)S(1)} %maximum_maximum_fusion.w0.j0, bf16[320,1024]{1,0:T(8,128)(2,1)} %collective-permute-done.w1.j1, bf16[320,1024]{1,0:T(8,128)(2,1)S(1)} %collective-permute-done.1.w2.j2, ...), custom_call_target="tpu_custom_call" | custom-call | flops 2000000000 | bytes 5000000 | tf_op jit(solution)/shard_map/pallas_call | solution.py:458
  157.5 10.8 %all-to-all-start.3 = ((bf16[512,3,2,128]{3,2,1,0:T(2,128)(2,1)}), bf16[512,3,2,128]{3,2,1,0:T(2,128)(2,1)}, u32[]{:S(2)}, u32[]{:S(2)}) async-start(bf16[512,3,2,128]{3,2,1,0:T(2,128)(2,1)} %bitcast.29), calls=%async_computation.3 | async-start | bytes 1572864 | tf_op jit(solution)/shard_map/all_to_all | solution.py:516
  168.4 3.5 %collective-permute-start.5 = (bf16[128,640]{1,0:T(8,128)(2,1)S(1)}, bf16[128,640]{1,0:T(8,128)(2,1)S(1)}, u32[]{:S(2)}, u32[]{:S(2)}) collective-permute-start(bf16[128,640]{1,0:T(8,128)(2,1)S(1)} %get-tuple-element.27.s0), channel_id=1, source_target_pairs={{0,3},{1,0},{2,1},{3,2},{4,7},{5,4},{6,5},{7,6},{8,11},{9,8},{10,9... | collective-permute-start | bytes 491528 | tf_op jit(solution)/shard_map/ppermute | solution.py:521
  171.9 2.5 collective-permute-start.4
  174.4 2.5 collective-permute-start.3
  176.9 3.4 %collective-permute-done.4.s2 = bf16[128,640]{1,0:T(8,128)(2,1)S(1)} collective-permute-done((bf16[128,640]{1,0:T(8,128)(2,1)S(1)}, bf16[128,640]{1,0:T(8,128)(2,1)S(1)}, u32[]{:S(2)}, u32[]{:S(2)}) %collective-permute-start.4) | collective-permute-done | bytes 163872 | tf_op jit(solution)/shard_map/ppermute | solution.py:521
  180.3 5.3 %collective-permute-done.3.s1 = bf16[128,640]{1,0:T(8,128)(2,1)S(1)} collective-permute-done((bf16[128,640]{1,0:T(8,128)(2,1)S(1)}, bf16[128,640]{1,0:T(8,128)(2,1)S(1)}, u32[]{:S(2)}, u32[]{:S(2)}) %collective-permute-start.3) | collective-permute-done | bytes 163872 | tf_op jit(solution)/shard_map/ppermute | solution.py:521
  185.6 2.3 shard_map.163
  187.9 3.8 %collective-permute-start.6 = (f32[4,16,8,256]{3,2,1,0:T(8,128)S(1)}, f32[4,16,8,256]{3,2,1,0:T(8,128)S(1)}, u32[]{:S(2)}, u32[]{:S(2)}) collective-permute-start(f32[4,16,8,256]{3,2,1,0:T(8,128)S(1)} %get-tuple-element.29), channel_id=1, source_target_pairs={{0,4},{4,0},{1,5},{5,1},{2,6},{6,2},{3,7},{7,3},{8,12},{12,8},{9,1... | collective-permute-start | bytes 1572872 | tf_op jit(solution)/shard_map/ppermute | solution.py:521
  193.3 3.2 %collective-permute-start.7 = (f32[16,8,256]{2,1,0:T(8,128)S(1)}, f32[16,8,256]{2,1,0:T(8,128)S(1)}, u32[]{:S(2)}, u32[]{:S(2)}) collective-permute-start(f32[16,8,256]{2,1,0:T(8,128)S(1)} %get-tuple-element.35), channel_id=1, source_target_pairs={{0,128},{128,256},{256,384},{384,0},{1,129},{129,257},{257,385},{3... | collective-permute-start | bytes 393224 | tf_op jit(solution)/shard_map/ppermute | solution.py:521
  196.5 3.3 %collective-permute-start.9 = (f32[16,8,256]{2,1,0:T(8,128)S(1)}, f32[16,8,256]{2,1,0:T(8,128)S(1)}, u32[]{:S(2)}, u32[]{:S(2)}) collective-permute-start(f32[16,8,256]{2,1,0:T(8,128)S(1)} %get-tuple-element.36), channel_id=1, source_target_pairs={{0,384},{128,0},{256,128},{384,256},{1,385},{129,1},{257,129},{385... | collective-permute-start | bytes 393224 | tf_op jit(solution)/shard_map/ppermute | solution.py:521
  199.8 3.5 %collective-permute-start.8 = (f32[16,8,256]{2,1,0:T(8,128)S(1)}, f32[16,8,256]{2,1,0:T(8,128)S(1)}, u32[]{:S(2)}, u32[]{:S(2)}) collective-permute-start(f32[16,8,256]{2,1,0:T(8,128)S(1)} %get-tuple-element.37), channel_id=1, source_target_pairs={{0,256},{128,384},{256,0},{384,128},{1,257},{129,385},{257,1},{385... | collective-permute-start | bytes 393224 | tf_op jit(solution)/shard_map/ppermute | solution.py:521
  203.5 4.4 %collective-permute-done.8 = f32[16,8,256]{2,1,0:T(8,128)S(1)} collective-permute-done((f32[16,8,256]{2,1,0:T(8,128)S(1)}, f32[16,8,256]{2,1,0:T(8,128)S(1)}, u32[]{:S(2)}, u32[]{:S(2)}) %collective-permute-start.8) | collective-permute-done | bytes 131104 | tf_op jit(solution)/shard_map/ppermute | solution.py:521
  207.9 5.1 %all-to-all-done.3 = bf16[512,3,2,128]{3,2,1,0:T(2,128)(2,1)} async-done(((bf16[512,3,2,128]{3,2,1,0:T(2,128)(2,1)}), bf16[512,3,2,128]{3,2,1,0:T(2,128)(2,1)}, u32[]{:S(2)}, u32[]{:S(2)}) %all-to-all-start.3) | async-done | bytes 786464 | tf_op jit(solution)/shard_map/all_to_all | solution.py:516
  213.0 19.5 %all_to_all.42 = f32[16,8,256]{2,1,0:T(8,128)S(1)} all-to-all(f32[16,8,256]{2,1,0:T(8,128)S(1)} %fusion.2), channel_id=1, replica_groups=mesh['y'=4,'z'=16,'core'=2,'x'=4] {'z'}, dimensions={0} | all-to-all | bytes 262144 | tf_op jit(solution)/shard_map/all_to_all | solution.py:516
  233.1 4.0 %all-to-all-start.5 = ((bf16[16,8,256]{2,1,0:T(8,128)(2,1)}), bf16[16,8,256]{2,1,0:T(8,128)(2,1)S(1)}, u32[]{:S(2)}, u32[]{:S(2)}) async-start(bf16[16,8,256]{2,1,0:T(8,128)(2,1)} %broadcast_in_dim.28), calls=%async_computation.5 | async-start | bytes 131072 | tf_op jit(solution)/shard_map/all_to_all | solution.py:516
  238.5 10.1 %all-to-all-done.5 = bf16[16,8,256]{2,1,0:T(8,128)(2,1)S(1)} async-done(((bf16[16,8,256]{2,1,0:T(8,128)(2,1)}), bf16[16,8,256]{2,1,0:T(8,128)(2,1)S(1)}, u32[]{:S(2)}, u32[]{:S(2)}) %all-to-all-start.5) | async-done | bytes 65568 | tf_op jit(solution)/shard_map/all_to_all | solution.py:516
  249.5 8.1 %all-to-all-start.6 = ((bf16[8,16,8,256]{3,2,1,0:T(8,128)(2,1)}), bf16[8,16,8,256]{3,2,1,0:T(8,128)(2,1)S(1)}, u32[]{:S(2)}, u32[]{:S(2)}) async-start(bf16[8,16,8,256]{3,2,1,0:T(8,128)(2,1)} %broadcast_in_dim.29), calls=%async_computation.6 | async-start | bytes 1048576 | tf_op jit(solution)/shard_map/all_to_all | solution.py:516
  257.7 5.5 %shard_map.164 = (bf16[4096,128]{1,0:T(8,128)(2,1)}, f32[2,2048]{1,0:T(2,128)}) custom-call(s32[4,32,128]{2,1,0:T(8,128)S(1)} %all-to-all-done.1.code_ref, bf16[4,768,128]{2,1,0:T(8,128)(2,1)S(1)} %bitcast.52, bf16[4096,128]{1,0:T(8,128)(2,1)S(1)} %bitcast.51, f32[2,2048]{1,0:T(2,128)S(1)} %copy-done.5), custom_call_target="tpu_custom_call" | custom-call | flops 7000000000 | bytes 3000000 | tf_op jit(solution)/shard_map/pallas_call | solution.py:503
  263.1 4.0 %all-to-all-done.6.parts_ref = bf16[8,16,8,256]{3,2,1,0:T(8,128)(2,1)S(1)} async-done(((bf16[8,16,8,256]{3,2,1,0:T(8,128)(2,1)}), bf16[8,16,8,256]{3,2,1,0:T(8,128)(2,1)S(1)}, u32[]{:S(2)}, u32[]{:S(2)}) %all-to-all-start.6) | async-done | bytes 524320 | tf_op jit(solution)/shard_map/all_to_all | solution.py:516
  (48 shorter events, 9.8 us)
Async XLA Ops:
  4.2 35.6 %all-to-all-start = ((s32[128,1,128]{2,1,0:T(1,128)}), s32[128,1,128]{2,1,0:T(1,128)S(1)}, u32[]{:S(2)}, u32[]{:S(2)}) async-start(s32[128,1,128]{2,1,0:T(1,128)} %bitcast.56), calls=%async_computation | async-start | bytes 131072 | tf_op jit(solution)/shard_map/all_to_all | solution.py:516
  24.9 0.7 copy-start.10
  25.6 1.2 copy-start.1
  25.6 1.2 copy-start.2
  25.6 1.4 copy-start.3
  26.2 0.6 copy-start.8
  26.8 17.7 %copy-start.11 = (bf16[256,1024]{1,0:T(8,128)(2,1)S(1)}, bf16[256,1024]{1,0:T(8,128)(2,1)}, u32[]{:S(2)}) copy-start(bf16[256,1024]{1,0:T(8,128)(2,1)} %param.24) | copy-start | bytes 1572868
  26.8 17.7 %copy-start = (bf16[2,2048,128]{2,1,0:T(8,128)(2,1)S(1)}, bf16[2,2048,128]{2,1,0:T(8,128)(2,1)}, u32[]{:S(2)}) copy-start(bf16[2,2048,128]{2,1,0:T(8,128)(2,1)} %param.14) | copy-start | bytes 3145732
  40.5 8.5 %all-to-all-start.1 = ((s32[4,32,128]{2,1,0:T(8,128)}), s32[4,32,128]{2,1,0:T(8,128)S(1)}, u32[]{:S(2)}, u32[]{:S(2)}) async-start(s32[4,32,128]{2,1,0:T(8,128)} %bitcast.16), calls=%async_computation.1 | async-start | bytes 131072 | tf_op jit(solution)/shard_map/all_to_all | solution.py:516
  57.7 92.9 %all-to-all-start.2 = ((bf16[512,3,4,128]{3,2,1,0:T(4,128)(2,1)}), bf16[512,3,4,128]{3,2,1,0:T(4,128)(2,1)}, u32[]{:S(2)}, u32[]{:S(2)}) async-start(bf16[512,3,4,128]{3,2,1,0:T(4,128)(2,1)} %bitcast.18), calls=%async_computation.2 | async-start | bytes 3145728 | tf_op jit(solution)/shard_map/all_to_all | solution.py:516
  71.3 81.4 %collective-permute-start.2 = (bf16[320,1024]{1,0:T(8,128)(2,1)S(1)}, bf16[320,1024]{1,0:T(8,128)(2,1)S(1)}, u32[]{:S(2)}, u32[]{:S(2)}) collective-permute-start(bf16[320,1024]{1,0:T(8,128)(2,1)S(1)} %maximum_maximum_fusion.w0.j0), channel_id=1, source_target_pairs={{0,3},{1,0},{2,1},{3,2},{4,7},{5,4},{6,5},{7,6},{8,11},{9,8},{10,9... | collective-permute-start | bytes 1966088 | tf_op jit(solution)/shard_map/ppermute | solution.py:521
  75.9 76.8 %collective-permute-start.1 = (bf16[320,1024]{1,0:T(8,128)(2,1)S(1)}, bf16[320,1024]{1,0:T(8,128)(2,1)S(1)}, u32[]{:S(2)}, u32[]{:S(2)}) collective-permute-start(bf16[320,1024]{1,0:T(8,128)(2,1)S(1)} %maximum_maximum_fusion.w0.j0), channel_id=1, source_target_pairs={{0,2},{1,3},{2,0},{3,1},{4,6},{5,7},{6,4},{7,5},{8,10},{9,11},{10,... | collective-permute-start | bytes 1966088 | tf_op jit(solution)/shard_map/ppermute | solution.py:521
  78.4 74.4 %collective-permute-start = (bf16[320,1024]{1,0:T(8,128)(2,1)S(1)}, bf16[320,1024]{1,0:T(8,128)(2,1)}, u32[]{:S(2)}, u32[]{:S(2)}) collective-permute-start(bf16[320,1024]{1,0:T(8,128)(2,1)S(1)} %maximum_maximum_fusion.w0.j0), channel_id=1, source_target_pairs={{0,1},{1,2},{2,3},{3,0},{4,5},{5,6},{6,7},{7,4},{8,9},{9,10},{10,1... | collective-permute-start | bytes 1966088 | tf_op jit(solution)/shard_map/ppermute | solution.py:521
  152.3 0.7 copy-start.4
  152.3 0.7 copy-start.6
  152.3 0.7 copy-start.7
  152.3 0.9 copy-start.9
  157.5 55.5 %all-to-all-start.3 = ((bf16[512,3,2,128]{3,2,1,0:T(2,128)(2,1)}), bf16[512,3,2,128]{3,2,1,0:T(2,128)(2,1)}, u32[]{:S(2)}, u32[]{:S(2)}) async-start(bf16[512,3,2,128]{3,2,1,0:T(2,128)(2,1)} %bitcast.29), calls=%async_computation.3 | async-start | bytes 1572864 | tf_op jit(solution)/shard_map/all_to_all | solution.py:516
  168.4 8.5 %collective-permute-start.5 = (bf16[128,640]{1,0:T(8,128)(2,1)S(1)}, bf16[128,640]{1,0:T(8,128)(2,1)S(1)}, u32[]{:S(2)}, u32[]{:S(2)}) collective-permute-start(bf16[128,640]{1,0:T(8,128)(2,1)S(1)} %get-tuple-element.27.s0), channel_id=1, source_target_pairs={{0,3},{1,0},{2,1},{3,2},{4,7},{5,4},{6,5},{7,6},{8,11},{9,8},{10,9... | collective-permute-start | bytes 491528 | tf_op jit(solution)/shard_map/ppermute | solution.py:521
  171.9 8.4 %collective-permute-start.4 = (bf16[128,640]{1,0:T(8,128)(2,1)S(1)}, bf16[128,640]{1,0:T(8,128)(2,1)S(1)}, u32[]{:S(2)}, u32[]{:S(2)}) collective-permute-start(bf16[128,640]{1,0:T(8,128)(2,1)S(1)} %get-tuple-element.27.s0), channel_id=1, source_target_pairs={{0,2},{1,3},{2,0},{3,1},{4,6},{5,7},{6,4},{7,5},{8,10},{9,11},{10,... | collective-permute-start | bytes 491528 | tf_op jit(solution)/shard_map/ppermute | solution.py:521
  174.4 11.2 %collective-permute-start.3 = (bf16[128,640]{1,0:T(8,128)(2,1)S(1)}, bf16[128,640]{1,0:T(8,128)(2,1)S(1)}, u32[]{:S(2)}, u32[]{:S(2)}) collective-permute-start(bf16[128,640]{1,0:T(8,128)(2,1)S(1)} %get-tuple-element.27.s0), channel_id=1, source_target_pairs={{0,1},{1,2},{2,3},{3,0},{4,5},{5,6},{6,7},{7,4},{8,9},{9,10},{10,1... | collective-permute-start | bytes 491528 | tf_op jit(solution)/shard_map/ppermute | solution.py:521
  187.9 5.4 %collective-permute-start.6 = (f32[4,16,8,256]{3,2,1,0:T(8,128)S(1)}, f32[4,16,8,256]{3,2,1,0:T(8,128)S(1)}, u32[]{:S(2)}, u32[]{:S(2)}) collective-permute-start(f32[4,16,8,256]{3,2,1,0:T(8,128)S(1)} %get-tuple-element.29), channel_id=1, source_target_pairs={{0,4},{4,0},{1,5},{5,1},{2,6},{6,2},{3,7},{7,3},{8,12},{12,8},{9,1... | collective-permute-start | bytes 1572872 | tf_op jit(solution)/shard_map/ppermute | solution.py:521
  193.3 10.0 %collective-permute-start.7 = (f32[16,8,256]{2,1,0:T(8,128)S(1)}, f32[16,8,256]{2,1,0:T(8,128)S(1)}, u32[]{:S(2)}, u32[]{:S(2)}) collective-permute-start(f32[16,8,256]{2,1,0:T(8,128)S(1)} %get-tuple-element.35), channel_id=1, source_target_pairs={{0,128},{128,256},{256,384},{384,0},{1,129},{129,257},{257,385},{3... | collective-permute-start | bytes 393224 | tf_op jit(solution)/shard_map/ppermute | solution.py:521
  196.5 7.0 %collective-permute-start.9 = (f32[16,8,256]{2,1,0:T(8,128)S(1)}, f32[16,8,256]{2,1,0:T(8,128)S(1)}, u32[]{:S(2)}, u32[]{:S(2)}) collective-permute-start(f32[16,8,256]{2,1,0:T(8,128)S(1)} %get-tuple-element.36), channel_id=1, source_target_pairs={{0,384},{128,0},{256,128},{384,256},{1,385},{129,1},{257,129},{385... | collective-permute-start | bytes 393224 | tf_op jit(solution)/shard_map/ppermute | solution.py:521
  199.8 8.0 %collective-permute-start.8 = (f32[16,8,256]{2,1,0:T(8,128)S(1)}, f32[16,8,256]{2,1,0:T(8,128)S(1)}, u32[]{:S(2)}, u32[]{:S(2)}) collective-permute-start(f32[16,8,256]{2,1,0:T(8,128)S(1)} %get-tuple-element.37), channel_id=1, source_target_pairs={{0,256},{128,384},{256,0},{384,128},{1,257},{129,385},{257,1},{385... | collective-permute-start | bytes 393224 | tf_op jit(solution)/shard_map/ppermute | solution.py:521
  233.1 15.6 %all-to-all-start.5 = ((bf16[16,8,256]{2,1,0:T(8,128)(2,1)}), bf16[16,8,256]{2,1,0:T(8,128)(2,1)S(1)}, u32[]{:S(2)}, u32[]{:S(2)}) async-start(bf16[16,8,256]{2,1,0:T(8,128)(2,1)} %broadcast_in_dim.28), calls=%async_computation.5 | async-start | bytes 131072 | tf_op jit(solution)/shard_map/all_to_all | solution.py:516
  238.4 19.3 %copy-start.5 = (f32[2,2048]{1,0:T(2,128)S(1)}, f32[2,2048]{1,0:T(2,128)}, u32[]{:S(2)}) copy-start(f32[2,2048]{1,0:T(2,128)} %accum_ref.1) | copy-start | bytes 49156
  249.5 17.6 %all-to-all-start.6 = ((bf16[8,16,8,256]{3,2,1,0:T(8,128)(2,1)}), bf16[8,16,8,256]{3,2,1,0:T(8,128)(2,1)S(1)}, u32[]{:S(2)}, u32[]{:S(2)}) async-start(bf16[8,16,8,256]{3,2,1,0:T(8,128)(2,1)} %broadcast_in_dim.29), calls=%async_computation.6 | async-start | bytes 1048576 | tf_op jit(solution)/shard_map/all_to_all | solution.py:516

commit v7 on v6

--- a/solution.py
+++ b/solution.py
@@ -91,8 +91,6 @@
     copies = [pltpu.make_async_copy(a, b, sems.at[i]) for i, (a, b) in enumerate(moves)]
     for copy in copies:
         copy.start()
-    for copy in copies:
-        copy.wait()
     ahead = jnp.concatenate(
         [
             (iota((LANES, LANES), 0) < iota((LANES, LANES), 1)).astype(F32),
@@ -103,6 +101,9 @@
     rows128 = iota((LANES, LANES), 0)
     half128 = half_iota((LANES, LANES), 0)
     half32 = (rows128 & (BLOCK - 1)).astype(F32).astype(BF16)
+
+    for copy in copies:
+        copy.wait()
 
     def put(step, row, place, spot, code):
         place_ref[step : step + 1, :] = place
@@ -352,6 +353,20 @@
             parts = blocks_of(place_ref[1] ^ far_core, (place_ref[2] + far_y) & (Y - 1))
             for z, at in enumerate(parts):
                 (near_ref, far_ref)[far_core][far_y, z] = sum_s[at]
+
+
+def sum_kernel(parts_ref, out_ref):
+    total = parts_ref[0]
+    for z in range(1, Z):
+        total = total + parts_ref[z]
+    total = total.astype(BF16)
+    for z in range(Z):
+        out_ref[z] = total
+
+
+def spread_kernel(own_ref, out_ref):
+    for i in range(Y * CORES):
+        out_ref[i] = own_ref[...]
 
 
 def place_kernel(parts_ref, out_ref):
@@ -527,9 +542,10 @@
     for step in range(1, Y):
         own = own + shifted(total[step], "y", step)
     own, after = lax.optimization_barrier((own, after))
-    own = jnp.sum(exchange(own, "z"), axis=0).astype(BF16)
-    own = exchange(jnp.broadcast_to(own[None], (Z, *own.shape)), "z")
-    parts = exchange(jnp.broadcast_to(own[None], (Y * CORES, *own.shape)), ("y", "core"))
+    own = exchange(own, "z")
+    own = exchange(call(sum_kernel, jax.ShapeDtypeStruct(own.shape, BF16))(own), "z")
+    copies = jax.ShapeDtypeStruct((Y * CORES, *own.shape), BF16)
+    parts = exchange(call(spread_kernel, copies)(own), ("y", "core"))
     return put_in_place(parts), after
 
 

time: 269 us -> 269 us (level)
  no operation moved by 1% of the time
where the time goes in v7:
time: 269 us; the launch traced here: 268 us
  waiting for transfers between devices  121 us (45%)
  starting transfers between devices  92.8 us (34%)
  Pallas kernels  27.9 us (10%)
  blocking collectives  19.5 us (7%)
  local copies, waits for them, and re-layouts  6.05 us (2%)
    all_to_all x6, waiting for transfers between devices, exchange(): return lax.all_to_all(array, axes, split_axis=0, concat_axis=0, tiled=True)  106 us
    all_to_all x6, starting transfers between devices, exchange(): return lax.all_to_all(array, axes, split_axis=0, concat_axis=0, tiled=True)  61 us
    ppermute x10, starting transfers between devices, shifted(): lax.ppermute(array, axis, [(i, (i + step) % size) for i in range(size)])  31.8 us
    all_to_all x1, blocking collectives, exchange(): return lax.all_to_all(array, axes, split_axis=0, concat_axis=0, tiled=True)  19.5 us
    ppermute x10, waiting for transfers between devices, shifted(): lax.ppermute(array, axis, [(i, (i + step) % size) for i in range(size)])  14.7 us
    pallas_call x1, Pallas kernels, look_up(): call(lookup_kernel, jax.ShapeDtypeStruct((N_ROW * 2 * PEERS * CAP, D), BF...  8.72 us
    pallas_call x1, Pallas kernels, update(): call(update_kernel, (jax.ShapeDtypeStruct(table.shape, BF16), jax.ShapeDt...  5.45 us
  transfers between devices with their start and end apart: 16, of which 11 were waited for; matrix products, arithmetic and copies ran while one was open for 1% of the time, Pallas kernels for 3%

profile of v7, /device:TPU:1, one launch (start us, length us, event | category | flops | bytes accessed | tf_op | source)
XLA Modules:
  0.0 268.0 jit_solution(7506541209876108957)
XLA Ops:
  0.6 3.6 %shard_map.157 = (s32[128,128]{1,0:T(8,128)}, s32[48,128]{1,0:T(8,128)}) custom-call(s32[16,128]{1,0:T(8,128)} %bitcast.63, s32[16,128]{1,0:T(8,128)} %bitcast.64, s32[2,128]{1,0:T(2,128)} %bitcast.67, s32[8,128]{1,0:T(8,128)} %bitcast.65, s32[8,128]{1,0:T(8,128)} %bitcast.66, s32[1,128]{1,0:T(1,128)} %bitcast.68), custom_call_target="tpu_custom_call" | custom-call | flops 2000000000 | bytes 200000 | tf_op jit(solution)/shard_map/pallas_call | solution.py:432
  4.2 20.6 %all-to-all-start = ((s32[128,1,128]{2,1,0:T(1,128)}), s32[128,1,128]{2,1,0:T(1,128)S(1)}, u32[]{:S(2)}, u32[]{:S(2)}) async-start(s32[128,1,128]{2,1,0:T(1,128)} %bitcast.56), calls=%async_computation | async-start | bytes 131072 | tf_op jit(solution)/shard_map/all_to_all | solution.py:531
  27.1 12.7 %all-to-all-done = s32[128,1,128]{2,1,0:T(1,128)S(1)} async-done(((s32[128,1,128]{2,1,0:T(1,128)}), s32[128,1,128]{2,1,0:T(1,128)S(1)}, u32[]{:S(2)}, u32[]{:S(2)}) %all-to-all-start) | async-done | bytes 65568 | tf_op jit(solution)/shard_map/all_to_all | solution.py:531
  40.5 4.0 %all-to-all-start.1 = ((s32[4,32,128]{2,1,0:T(8,128)}), s32[4,32,128]{2,1,0:T(8,128)S(1)}, u32[]{:S(2)}, u32[]{:S(2)}) async-start(s32[4,32,128]{2,1,0:T(8,128)} %bitcast.16), calls=%async_computation.1 | async-start | bytes 131072 | tf_op jit(solution)/shard_map/all_to_all | solution.py:531
  44.9 4.1 %all-to-all-done.1.code_ref = s32[4,32,128]{2,1,0:T(8,128)S(1)} async-done(((s32[4,32,128]{2,1,0:T(8,128)}), s32[4,32,128]{2,1,0:T(8,128)S(1)}, u32[]{:S(2)}, u32[]{:S(2)}) %all-to-all-start.1) | async-done | bytes 65568 | tf_op jit(solution)/shard_map/all_to_all | solution.py:531
  49.0 8.7 %shard_map.161 = bf16[6144,128]{1,0:T(8,128)(2,1)} custom-call(s32[4,32,128]{2,1,0:T(8,128)S(1)} %all-to-all-done.1.code_ref, bf16[512,1024]{1,0:T(8,128)(2,1)S(1)} %shard_map.160.fold_ref, bf16[512,512]{1,0:T(8,128)(2,1)S(1)} %shard_map.159.cfold_ref), custom_call_target="tpu_custom_call" | custom-call | flops 7000000000 | bytes 3200000 | tf_op jit(solution)/shard_map/pallas_call | solution.py:463
  57.7 13.4 %all-to-all-start.2 = ((bf16[512,3,4,128]{3,2,1,0:T(4,128)(2,1)}), bf16[512,3,4,128]{3,2,1,0:T(4,128)(2,1)}, u32[]{:S(2)}, u32[]{:S(2)}) async-start(bf16[512,3,4,128]{3,2,1,0:T(4,128)(2,1)} %bitcast.18), calls=%async_computation.2 | async-start | bytes 3145728 | tf_op jit(solution)/shard_map/all_to_all | solution.py:531
  71.1 4.5 %collective-permute-start.2 = (bf16[320,1024]{1,0:T(8,128)(2,1)S(1)}, bf16[320,1024]{1,0:T(8,128)(2,1)S(1)}, u32[]{:S(2)}, u32[]{:S(2)}) collective-permute-start(bf16[320,1024]{1,0:T(8,128)(2,1)S(1)} %maximum_maximum_fusion.w0.j0), channel_id=1, source_target_pairs={{0,3},{1,0},{2,1},{3,2},{4,7},{5,4},{6,5},{7,6},{8,11},{9,8},{10,9... | collective-permute-start | bytes 1966088 | tf_op jit(solution)/shard_map/ppermute | solution.py:536
  75.7 2.5 collective-permute-start.1
  78.2 2.5 collective-permute-start
  80.7 69.7 %all-to-all-done.2 = bf16[512,3,4,128]{3,2,1,0:T(4,128)(2,1)} async-done(((bf16[512,3,4,128]{3,2,1,0:T(4,128)(2,1)}), bf16[512,3,4,128]{3,2,1,0:T(4,128)(2,1)}, u32[]{:S(2)}, u32[]{:S(2)}) %all-to-all-start.2) | async-done | bytes 1572896 | tf_op jit(solution)/shard_map/all_to_all | solution.py:531
  150.4 1.7 copy.25
  153.0 4.3 %shard_map.162 = (bf16[3072,128]{1,0:T(8,128)(2,1)}, bf16[128,640]{1,0:T(8,128)(2,1)S(1)}) custom-call(s32[3]{0:T(128)S(1)} %pad_add_fusion.place_ref, bf16[320,1024]{1,0:T(8,128)(2,1)S(1)} %maximum_maximum_fusion.w0.j0, bf16[320,1024]{1,0:T(8,128)(2,1)} %collective-permute-done.w1.j1, bf16[320,1024]{1,0:T(8,128)(2,1)S(1)} %collective-permute-done.1.w2.j2, ...), custom_call_target="tpu_custom_call" | custom-call | flops 2000000000 | bytes 5000000 | tf_op jit(solution)/shard_map/pallas_call | solution.py:473
  157.3 10.8 %all-to-all-start.3 = ((bf16[512,3,2,128]{3,2,1,0:T(2,128)(2,1)}), bf16[512,3,2,128]{3,2,1,0:T(2,128)(2,1)}, u32[]{:S(2)}, u32[]{:S(2)}) async-start(bf16[512,3,2,128]{3,2,1,0:T(2,128)(2,1)} %bitcast.29), calls=%async_computation.3 | async-start | bytes 1572864 | tf_op jit(solution)/shard_map/all_to_all | solution.py:531
  168.2 3.5 %collective-permute-start.5 = (bf16[128,640]{1,0:T(8,128)(2,1)S(1)}, bf16[128,640]{1,0:T(8,128)(2,1)S(1)}, u32[]{:S(2)}, u32[]{:S(2)}) collective-permute-start(bf16[128,640]{1,0:T(8,128)(2,1)S(1)} %get-tuple-element.27.s0), channel_id=1, source_target_pairs={{0,3},{1,0},{2,1},{3,2},{4,7},{5,4},{6,5},{7,6},{8,11},{9,8},{10,9... | collective-permute-start | bytes 491528 | tf_op jit(solution)/shard_map/ppermute | solution.py:536
  171.7 2.5 collective-permute-start.4
  174.2 2.5 collective-permute-start.3
  176.7 3.4 %collective-permute-done.4.s2 = bf16[128,640]{1,0:T(8,128)(2,1)S(1)} collective-permute-done((bf16[128,640]{1,0:T(8,128)(2,1)S(1)}, bf16[128,640]{1,0:T(8,128)(2,1)S(1)}, u32[]{:S(2)}, u32[]{:S(2)}) %collective-permute-start.4) | collective-permute-done | bytes 163872 | tf_op jit(solution)/shard_map/ppermute | solution.py:536
  180.1 5.3 %collective-permute-done.3.s1 = bf16[128,640]{1,0:T(8,128)(2,1)S(1)} collective-permute-done((bf16[128,640]{1,0:T(8,128)(2,1)S(1)}, bf16[128,640]{1,0:T(8,128)(2,1)S(1)}, u32[]{:S(2)}, u32[]{:S(2)}) %collective-permute-start.3) | collective-permute-done | bytes 163872 | tf_op jit(solution)/shard_map/ppermute | solution.py:536
  185.4 2.3 shard_map.163
  187.6 3.8 %collective-permute-start.6 = (f32[4,16,8,256]{3,2,1,0:T(8,128)S(1)}, f32[4,16,8,256]{3,2,1,0:T(8,128)S(1)}, u32[]{:S(2)}, u32[]{:S(2)}) collective-permute-start(f32[4,16,8,256]{3,2,1,0:T(8,128)S(1)} %get-tuple-element.29), channel_id=1, source_target_pairs={{0,4},{4,0},{1,5},{5,1},{2,6},{6,2},{3,7},{7,3},{8,12},{12,8},{9,1... | collective-permute-start | bytes 1572872 | tf_op jit(solution)/shard_map/ppermute | solution.py:536
  193.1 3.2 %collective-permute-start.7 = (f32[16,8,256]{2,1,0:T(8,128)S(1)}, f32[16,8,256]{2,1,0:T(8,128)S(1)}, u32[]{:S(2)}, u32[]{:S(2)}) collective-permute-start(f32[16,8,256]{2,1,0:T(8,128)S(1)} %get-tuple-element.35), channel_id=1, source_target_pairs={{0,128},{128,256},{256,384},{384,0},{1,129},{129,257},{257,385},{3... | collective-permute-start | bytes 393224 | tf_op jit(solution)/shard_map/ppermute | solution.py:536
  196.3 3.3 %collective-permute-start.9 = (f32[16,8,256]{2,1,0:T(8,128)S(1)}, f32[16,8,256]{2,1,0:T(8,128)S(1)}, u32[]{:S(2)}, u32[]{:S(2)}) collective-permute-start(f32[16,8,256]{2,1,0:T(8,128)S(1)} %get-tuple-element.36), channel_id=1, source_target_pairs={{0,384},{128,0},{256,128},{384,256},{1,385},{129,1},{257,129},{385... | collective-permute-start | bytes 393224 | tf_op jit(solution)/shard_map/ppermute | solution.py:536
  199.6 3.5 %collective-permute-start.8 = (f32[16,8,256]{2,1,0:T(8,128)S(1)}, f32[16,8,256]{2,1,0:T(8,128)S(1)}, u32[]{:S(2)}, u32[]{:S(2)}) collective-permute-start(f32[16,8,256]{2,1,0:T(8,128)S(1)} %get-tuple-element.37), channel_id=1, source_target_pairs={{0,256},{128,384},{256,0},{384,128},{1,257},{129,385},{257,1},{385... | collective-permute-start | bytes 393224 | tf_op jit(solution)/shard_map/ppermute | solution.py:536
  203.2 4.4 %collective-permute-done.8 = f32[16,8,256]{2,1,0:T(8,128)S(1)} collective-permute-done((f32[16,8,256]{2,1,0:T(8,128)S(1)}, f32[16,8,256]{2,1,0:T(8,128)S(1)}, u32[]{:S(2)}, u32[]{:S(2)}) %collective-permute-start.8) | collective-permute-done | bytes 131104 | tf_op jit(solution)/shard_map/ppermute | solution.py:536
  207.7 5.1 %all-to-all-done.3 = bf16[512,3,2,128]{3,2,1,0:T(2,128)(2,1)} async-done(((bf16[512,3,2,128]{3,2,1,0:T(2,128)(2,1)}), bf16[512,3,2,128]{3,2,1,0:T(2,128)(2,1)}, u32[]{:S(2)}, u32[]{:S(2)}) %all-to-all-start.3) | async-done | bytes 786464 | tf_op jit(solution)/shard_map/all_to_all | solution.py:531
  212.8 19.5 %all_to_all.42.parts_ref = f32[16,8,256]{2,1,0:T(8,128)S(1)} all-to-all(f32[16,8,256]{2,1,0:T(8,128)S(1)} %fusion.2), channel_id=1, replica_groups=mesh['y'=4,'z'=16,'core'=2,'x'=4] {'z'}, dimensions={0} | all-to-all | bytes 262144 | tf_op jit(solution)/shard_map/all_to_all | solution.py:531
  232.9 4.0 %all-to-all-start.5 = ((bf16[16,8,256]{2,1,0:T(8,128)(2,1)}), bf16[16,8,256]{2,1,0:T(8,128)(2,1)S(1)}, u32[]{:S(2)}, u32[]{:S(2)}) async-start(bf16[16,8,256]{2,1,0:T(8,128)(2,1)} %shard_map.165), calls=%async_computation.5 | async-start | bytes 131072 | tf_op jit(solution)/shard_map/all_to_all | solution.py:531
  238.3 10.1 %all-to-all-done.5.own_ref = bf16[16,8,256]{2,1,0:T(8,128)(2,1)S(1)} async-done(((bf16[16,8,256]{2,1,0:T(8,128)(2,1)}), bf16[16,8,256]{2,1,0:T(8,128)(2,1)S(1)}, u32[]{:S(2)}, u32[]{:S(2)}) %all-to-all-start.5) | async-done | bytes 65568 | tf_op jit(solution)/shard_map/all_to_all | solution.py:531
  249.3 8.1 %all-to-all-start.6 = ((bf16[8,16,8,256]{3,2,1,0:T(8,128)(2,1)}), bf16[8,16,8,256]{3,2,1,0:T(8,128)(2,1)S(1)}, u32[]{:S(2)}, u32[]{:S(2)}) async-start(bf16[8,16,8,256]{3,2,1,0:T(8,128)(2,1)} %shard_map.166), calls=%async_computation.6 | async-start | bytes 1048576 | tf_op jit(solution)/shard_map/all_to_all | solution.py:531
  257.4 5.5 %shard_map.164 = (bf16[4096,128]{1,0:T(8,128)(2,1)}, f32[2,2048]{1,0:T(2,128)}) custom-call(s32[4,32,128]{2,1,0:T(8,128)S(1)} %all-to-all-done.1.code_ref, bf16[4,768,128]{2,1,0:T(8,128)(2,1)S(1)} %bitcast.52, bf16[4096,128]{1,0:T(8,128)(2,1)S(1)} %bitcast.51, f32[2,2048]{1,0:T(2,128)S(1)} %copy-done.5), custom_call_target="tpu_custom_call" | custom-call | flops 7000000000 | bytes 3000000 | tf_op jit(solution)/shard_map/pallas_call | solution.py:518
  262.9 4.0 %all-to-all-done.6.parts_ref = bf16[8,16,8,256]{3,2,1,0:T(8,128)(2,1)S(1)} async-done(((bf16[8,16,8,256]{3,2,1,0:T(8,128)(2,1)}), bf16[8,16,8,256]{3,2,1,0:T(8,128)(2,1)S(1)}, u32[]{:S(2)}, u32[]{:S(2)}) %all-to-all-start.6) | async-done | bytes 524320 | tf_op jit(solution)/shard_map/all_to_all | solution.py:531
  (47 shorter events, 9.8 us)
Async XLA Ops:
  4.2 35.5 %all-to-all-start = ((s32[128,1,128]{2,1,0:T(1,128)}), s32[128,1,128]{2,1,0:T(1,128)S(1)}, u32[]{:S(2)}, u32[]{:S(2)}) async-start(s32[128,1,128]{2,1,0:T(1,128)} %bitcast.56), calls=%async_computation | async-start | bytes 131072 | tf_op jit(solution)/shard_map/all_to_all | solution.py:531
  24.9 0.7 copy-start.10
  25.6 1.2 copy-start.1
  25.6 1.2 copy-start.2
  25.6 1.4 copy-start.3
  26.2 0.6 copy-start.8
  26.8 17.7 %copy-start.11 = (bf16[256,1024]{1,0:T(8,128)(2,1)S(1)}, bf16[256,1024]{1,0:T(8,128)(2,1)}, u32[]{:S(2)}) copy-start(bf16[256,1024]{1,0:T(8,128)(2,1)} %param.24) | copy-start | bytes 1572868
  26.8 17.7 %copy-start = (bf16[2,2048,128]{2,1,0:T(8,128)(2,1)S(1)}, bf16[2,2048,128]{2,1,0:T(8,128)(2,1)}, u32[]{:S(2)}) copy-start(bf16[2,2048,128]{2,1,0:T(8,128)(2,1)} %param.14) | copy-start | bytes 3145732
  40.5 8.5 %all-to-all-start.1 = ((s32[4,32,128]{2,1,0:T(8,128)}), s32[4,32,128]{2,1,0:T(8,128)S(1)}, u32[]{:S(2)}, u32[]{:S(2)}) async-start(s32[4,32,128]{2,1,0:T(8,128)} %bitcast.16), calls=%async_computation.1 | async-start | bytes 131072 | tf_op jit(solution)/shard_map/all_to_all | solution.py:531
  57.7 92.7 %all-to-all-start.2 = ((bf16[512,3,4,128]{3,2,1,0:T(4,128)(2,1)}), bf16[512,3,4,128]{3,2,1,0:T(4,128)(2,1)}, u32[]{:S(2)}, u32[]{:S(2)}) async-start(bf16[512,3,4,128]{3,2,1,0:T(4,128)(2,1)} %bitcast.18), calls=%async_computation.2 | async-start | bytes 3145728 | tf_op jit(solution)/shard_map/all_to_all | solution.py:531
  71.1 81.4 %collective-permute-start.2 = (bf16[320,1024]{1,0:T(8,128)(2,1)S(1)}, bf16[320,1024]{1,0:T(8,128)(2,1)S(1)}, u32[]{:S(2)}, u32[]{:S(2)}) collective-permute-start(bf16[320,1024]{1,0:T(8,128)(2,1)S(1)} %maximum_maximum_fusion.w0.j0), channel_id=1, source_target_pairs={{0,3},{1,0},{2,1},{3,2},{4,7},{5,4},{6,5},{7,6},{8,11},{9,8},{10,9... | collective-permute-start | bytes 1966088 | tf_op jit(solution)/shard_map/ppermute | solution.py:536
  75.7 76.8 %collective-permute-start.1 = (bf16[320,1024]{1,0:T(8,128)(2,1)S(1)}, bf16[320,1024]{1,0:T(8,128)(2,1)S(1)}, u32[]{:S(2)}, u32[]{:S(2)}) collective-permute-start(bf16[320,1024]{1,0:T(8,128)(2,1)S(1)} %maximum_maximum_fusion.w0.j0), channel_id=1, source_target_pairs={{0,2},{1,3},{2,0},{3,1},{4,6},{5,7},{6,4},{7,5},{8,10},{9,11},{10,... | collective-permute-start | bytes 1966088 | tf_op jit(solution)/shard_map/ppermute | solution.py:536
  78.2 74.4 %collective-permute-start = (bf16[320,1024]{1,0:T(8,128)(2,1)S(1)}, bf16[320,1024]{1,0:T(8,128)(2,1)}, u32[]{:S(2)}, u32[]{:S(2)}) collective-permute-start(bf16[320,1024]{1,0:T(8,128)(2,1)S(1)} %maximum_maximum_fusion.w0.j0), channel_id=1, source_target_pairs={{0,1},{1,2},{2,3},{3,0},{4,5},{5,6},{6,7},{7,4},{8,9},{9,10},{10,1... | collective-permute-start | bytes 1966088 | tf_op jit(solution)/shard_map/ppermute | solution.py:536
  152.1 0.7 copy-start.4
  152.1 0.7 copy-start.6
  152.1 0.7 copy-start.7
  152.1 0.9 copy-start.9
  157.3 55.5 %all-to-all-start.3 = ((bf16[512,3,2,128]{3,2,1,0:T(2,128)(2,1)}), bf16[512,3,2,128]{3,2,1,0:T(2,128)(2,1)}, u32[]{:S(2)}, u32[]{:S(2)}) async-start(bf16[512,3,2,128]{3,2,1,0:T(2,128)(2,1)} %bitcast.29), calls=%async_computation.3 | async-start | bytes 1572864 | tf_op jit(solution)/shard_map/all_to_all | solution.py:531
  168.2 8.5 %collective-permute-start.5 = (bf16[128,640]{1,0:T(8,128)(2,1)S(1)}, bf16[128,640]{1,0:T(8,128)(2,1)S(1)}, u32[]{:S(2)}, u32[]{:S(2)}) collective-permute-start(bf16[128,640]{1,0:T(8,128)(2,1)S(1)} %get-tuple-element.27.s0), channel_id=1, source_target_pairs={{0,3},{1,0},{2,1},{3,2},{4,7},{5,4},{6,5},{7,6},{8,11},{9,8},{10,9... | collective-permute-start | bytes 491528 | tf_op jit(solution)/shard_map/ppermute | solution.py:536
  171.7 8.4 %collective-permute-start.4 = (bf16[128,640]{1,0:T(8,128)(2,1)S(1)}, bf16[128,640]{1,0:T(8,128)(2,1)S(1)}, u32[]{:S(2)}, u32[]{:S(2)}) collective-permute-start(bf16[128,640]{1,0:T(8,128)(2,1)S(1)} %get-tuple-element.27.s0), channel_id=1, source_target_pairs={{0,2},{1,3},{2,0},{3,1},{4,6},{5,7},{6,4},{7,5},{8,10},{9,11},{10,... | collective-permute-start | bytes 491528 | tf_op jit(solution)/shard_map/ppermute | solution.py:536
  174.2 11.2 %collective-permute-start.3 = (bf16[128,640]{1,0:T(8,128)(2,1)S(1)}, bf16[128,640]{1,0:T(8,128)(2,1)S(1)}, u32[]{:S(2)}, u32[]{:S(2)}) collective-permute-start(bf16[128,640]{1,0:T(8,128)(2,1)S(1)} %get-tuple-element.27.s0), channel_id=1, source_target_pairs={{0,1},{1,2},{2,3},{3,0},{4,5},{5,6},{6,7},{7,4},{8,9},{9,10},{10,1... | collective-permute-start | bytes 491528 | tf_op jit(solution)/shard_map/ppermute | solution.py:536
  187.6 5.4 %collective-permute-start.6 = (f32[4,16,8,256]{3,2,1,0:T(8,128)S(1)}, f32[4,16,8,256]{3,2,1,0:T(8,128)S(1)}, u32[]{:S(2)}, u32[]{:S(2)}) collective-permute-start(f32[4,16,8,256]{3,2,1,0:T(8,128)S(1)} %get-tuple-element.29), channel_id=1, source_target_pairs={{0,4},{4,0},{1,5},{5,1},{2,6},{6,2},{3,7},{7,3},{8,12},{12,8},{9,1... | collective-permute-start | bytes 1572872 | tf_op jit(solution)/shard_map/ppermute | solution.py:536
  193.1 10.0 %collective-permute-start.7 = (f32[16,8,256]{2,1,0:T(8,128)S(1)}, f32[16,8,256]{2,1,0:T(8,128)S(1)}, u32[]{:S(2)}, u32[]{:S(2)}) collective-permute-start(f32[16,8,256]{2,1,0:T(8,128)S(1)} %get-tuple-element.35), channel_id=1, source_target_pairs={{0,128},{128,256},{256,384},{384,0},{1,129},{129,257},{257,385},{3... | collective-permute-start | bytes 393224 | tf_op jit(solution)/shard_map/ppermute | solution.py:536
  196.3 7.0 %collective-permute-start.9 = (f32[16,8,256]{2,1,0:T(8,128)S(1)}, f32[16,8,256]{2,1,0:T(8,128)S(1)}, u32[]{:S(2)}, u32[]{:S(2)}) collective-permute-start(f32[16,8,256]{2,1,0:T(8,128)S(1)} %get-tuple-element.36), channel_id=1, source_target_pairs={{0,384},{128,0},{256,128},{384,256},{1,385},{129,1},{257,129},{385... | collective-permute-start | bytes 393224 | tf_op jit(solution)/shard_map/ppermute | solution.py:536
  199.6 8.0 %collective-permute-start.8 = (f32[16,8,256]{2,1,0:T(8,128)S(1)}, f32[16,8,256]{2,1,0:T(8,128)S(1)}, u32[]{:S(2)}, u32[]{:S(2)}) collective-permute-start(f32[16,8,256]{2,1,0:T(8,128)S(1)} %get-tuple-element.37), channel_id=1, source_target_pairs={{0,256},{128,384},{256,0},{384,128},{1,257},{129,385},{257,1},{385... | collective-permute-start | bytes 393224 | tf_op jit(solution)/shard_map/ppermute | solution.py:536
  232.9 15.6 %all-to-all-start.5 = ((bf16[16,8,256]{2,1,0:T(8,128)(2,1)}), bf16[16,8,256]{2,1,0:T(8,128)(2,1)S(1)}, u32[]{:S(2)}, u32[]{:S(2)}) async-start(bf16[16,8,256]{2,1,0:T(8,128)(2,1)} %shard_map.165), calls=%async_computation.5 | async-start | bytes 131072 | tf_op jit(solution)/shard_map/all_to_all | solution.py:531
  238.1 19.3 %copy-start.5 = (f32[2,2048]{1,0:T(2,128)S(1)}, f32[2,2048]{1,0:T(2,128)}, u32[]{:S(2)}) copy-start(f32[2,2048]{1,0:T(2,128)} %accum_ref.1) | copy-start | bytes 49156
  249.3 17.6 %all-to-all-start.6 = ((bf16[8,16,8,256]{3,2,1,0:T(8,128)(2,1)}), bf16[8,16,8,256]{3,2,1,0:T(8,128)(2,1)S(1)}, u32[]{:S(2)}, u32[]{:S(2)}) async-start(bf16[8,16,8,256]{3,2,1,0:T(8,128)(2,1)} %shard_map.166), calls=%async_computation.6 | async-start | bytes 1048576 | tf_op jit(solution)/shard_map/all_to_all | solution.py:531
